TPU v7x, 32 devices: a whole 2x2x4 slice. The times are simulated.
32 devices in a mesh: groups: 2 (over y), member: 2 (over x), fsdp: 8 (over z, core).
Axes of the slice: x: 2, y: 2, z: 4, core: 2. Of those that a mesh axis runs over, the one named last changes fastest.
Arguments:
- gate_pre: bfloat16 [12288, 2560], P(('groups', 'member', 'fsdp')), parts along dimension 0, may hold values from -6 to 6
- up_pre: bfloat16 [12288, 2560], P(('groups', 'member', 'fsdp')), parts along dimension 0, may hold values from -6 to 6
- out_grad: bfloat16 [12288, 2048], P(('groups', 'member', 'fsdp')), parts along dimension 0, may hold values from -6 to 6
- in_scale: float32 [4, 2560], P('member'), may hold values from 0.1 to 1.9
- out_scale: float32 [4, 2048], P('member'), may hold values from 0.1 to 1.9
- down_weight: bfloat16 [2560, 2048], P('fsdp'), may hold values from -0.125 to 0.125
- member_slot: int32 [12288], P(('groups', 'member', 'fsdp')), parts along dimension 0, may hold values from 0 to 1, as said below
Outputs:
- grad_gate: bfloat16 [12288, 2560], P(('groups', 'member', 'fsdp')), parts along dimension 0
- grad_up: bfloat16 [12288, 2560], P(('groups', 'member', 'fsdp')), parts along dimension 0
- grad_down: float32 [5120, 2048], P(('groups', 'fsdp'), 'member'), parts along dimension 0
- grad_in_scale: float32 [8, 2560], P(('groups', 'member')), parts along dimension 0
- grad_out_scale: float32 [8, 2048], P(('groups', 'member')), parts along dimension 0
There are 2 independent parts, one for each index of `groups`. A program takes and returns all parts, laid end to end along the dimension named above; an argument that names none is the same for every part. Nothing has to cross between parts.
Inputs may be any that keep to these rules, and one draw needn't show every extreme that they name: `member_slot`: constant over each sequence of 1024 tokens; the first sequence uses slot 1.
All inputs are finite; a program needn't handle non-finite values.
Results may differ from a plain program's by a relative error of at most 0.0051.
Values may be sent and summed in bfloat16 or wider, within the bound.
No kernel may reach another device: no remote copies, remote signals or barrier semaphores. Data moves between devices by JAX's collectives and lax.ppermute only.
A program may use at most 128 MiB of HBM per device.

v0:
```python
import jax
import jax.numpy as jnp
from jax import lax
from jax.sharding import PartitionSpec as P


def gelu_tanh(value):
    return jax.nn.gelu(value, approximate=True)


def on_device(gate_pre, up_pre, out_grad, in_scale, out_scale, down_weight, member_slot):
    mem_count = in_scale.shape[0]
    slot_ids = lax.broadcasted_iota(jnp.int32, (1, mem_count), 1)
    onehot = (member_slot[:, None] == slot_ids).astype(jnp.float32)
    row_in = jnp.dot(onehot, in_scale, precision=lax.Precision.HIGHEST)
    row_out = jnp.dot(onehot, out_scale, precision=lax.Precision.HIGHEST)
    gate32 = gate_pre.astype(jnp.float32)
    up32 = up_pre.astype(jnp.float32)
    gelu_val, gelu_back = jax.vjp(gelu_tanh, gate32)
    act = gelu_val * up32
    hidden = (act * row_in).astype(jnp.bfloat16)
    grad32 = out_grad.astype(jnp.float32)
    scaled = (grad32 * row_out).astype(jnp.bfloat16)
    whole_weight = lax.all_gather(down_weight, "fsdp", axis=0, tiled=True)
    forward = jnp.dot(hidden, whole_weight, preferred_element_type=jnp.float32)
    grad_hidden = lax.dot_general(
        scaled, whole_weight, (((1,), (1,)), ((), ())), preferred_element_type=jnp.float32
    )
    local_in = jnp.dot(onehot.T, grad_hidden * act, precision=lax.Precision.HIGHEST)
    local_out = jnp.dot(onehot.T, grad32 * forward, precision=lax.Precision.HIGHEST)
    grad_in_scale, grad_out_scale = lax.psum((local_in, local_out), "fsdp")
    grad_act = grad_hidden * row_in
    (grad_gelu,) = gelu_back(grad_act * up32)
    grad_gate = grad_gelu.astype(jnp.bfloat16)
    grad_up = (grad_act * gelu_val).astype(jnp.bfloat16)
    own_rows = lax.psum_scatter(
        lax.dot_general(
            hidden, scaled, (((0,), (0,)), ((), ())), preferred_element_type=jnp.float32
        ),
        "fsdp",
        scatter_dimension=0,
        tiled=True,
    )
    grad_down = lax.psum_scatter(own_rows, "member", scatter_dimension=1, tiled=True)
    return (grad_gate, grad_up, grad_down, grad_in_scale, grad_out_scale)


def solution(mesh):
    in_specs = (
        P(("groups", "member", "fsdp"), None),
        P(("groups", "member", "fsdp"), None),
        P(("groups", "member", "fsdp"), None),
        P("member", None),
        P("member", None),
        P("fsdp", None),
        P(("groups", "member", "fsdp")),
    )
    out_specs = (
        P(("groups", "member", "fsdp"), None),
        P(("groups", "member", "fsdp"), None),
        P(("groups", "fsdp"), "member"),
        P(("groups", "member"), None),
        P(("groups", "member"), None),
    )
    return jax.shard_map(
        on_device, mesh=mesh, in_specs=in_specs, out_specs=out_specs, check_vma=False
    )
```

profile of v0, /device:TPU:0, one launch (start us, length us, event | category | flops | bytes accessed | tf_op | source)
XLA Modules:
  0.0 393.0 jit_solution(11954649479777929656)
XLA Ops:
  7.2 0.0 copy-start
  7.2 0.0 copy-start.4
  7.2 0.0 all-gather.2.cloned.1.call-start
  7.2 0.7 all-gather.2.cloned.1.call-update
  7.9 0.0 reduce-scatter.3.cloned.1.call-start
  8.0 3.0 fusion.11
  11.0 0.0 copy-done
  11.0 0.0 copy-done.4
  11.0 3.6 fusion.13
  14.6 97.2 %all-gather.2.cloned.1.call-done = bf16[2560,2048]{1,0:T(8,128)(2,1)} async-done(((bf16[320,2048]{1,0:T(8,128)(2,1)}), bf16[2560,2048]{1,0:T(8,128)(2,1)}) %all-gather.2.cloned.1.call-update) | async-done | bytes 10485776 | tf_op jit(solution)/shard_map/all_gather | solution.py:24
  111.8 17.6 %multiply_convert_fusion.1 = (bf16[384,2560]{1,0:T(8,128)(2,1)}, bf16[384,2560]{1,0:T(8,128)(2,1)}, bf16[384,2560]{1,0:T(8,128)(2,1)S(1)}, f32[384,2560]{1,0:T(8,128)}) fusion(bf16[384,2560]{1,0:T(8,128)(2,1)} %param.7, f32[384,2560]{1,0:T(8,128)} %fusion.13, bf16[384,2560]{1,0:T(8,128)(2,1)} %param.8, bf16[384,2048]{1,0:T(8,128)(2,1)S(1)} %fusion.11, ...), kind=kOutput, calls=%fused_computation.19 | convolution fusion | flops 4056023040 | bytes 29753344 | tf_op jit(solution)/shard_map/dot_general | solution.py:26
  129.4 0.0 copy-start.2
  129.4 1.3 copy-done.2
  130.7 9.9 %fusion.22 = f32[2560,2048]{1,0:T(8,128)} fusion(bf16[384,2560]{1,0:T(8,128)(2,1)S(1)} %get-tuple-element.9, bf16[384,2048]{1,0:T(8,128)(2,1)S(1)} %fusion.11), kind=kOutput, calls=%fused_computation.34 | convolution fusion | flops 4026531840 | bytes 24510464 | tf_op jit(solution)/shard_map/dot_general | solution.py:37
  140.6 0.0 copy-start.3
  140.6 0.0 reduce-scatter.3.cloned.1.call-update
  140.6 0.2 reduce-scatter.5.cloned.1.call-start
  140.9 206.0 %reduce-scatter.3.cloned.1.call-done = f32[320,2048]{1,0:T(8,128)} async-done(((f32[2560,2048]{1,0:T(8,128)}), f32[320,2048]{1,0:T(8,128)}) %reduce-scatter.3.cloned.1.call-update) | async-done | bytes 2621456 | tf_op jit(solution)/shard_map/reduce_scatter | solution.py:36
  346.9 0.0 reduce-scatter.5.cloned.1.call-update
  346.9 0.0 copy-done.3
  346.9 0.0 copy-start.1
  346.9 0.0 copy-start.7
  346.9 7.1 %fusion.23 = f32[384,2048]{1,0:T(8,128)S(1)} fusion(bf16[384,2560]{1,0:T(8,128)(2,1)S(1)} %copy-done.3, bf16[2560,2048]{1,0:T(8,128)(2,1)} %all-gather.2.cloned.1.call-done), kind=kOutput, calls=%fused_computation.35 | convolution fusion | flops 4026531840 | bytes 15597568 | tf_op jit(solution)/shard_map/dot_general | solution.py:25
  354.0 0.0 copy-done.1
  354.0 0.0 copy-start.5
  354.0 0.0 copy-start.6
  354.0 1.3 fusion.12
  355.3 0.0 copy-done.7
  355.4 0.5 copy-done.5
  355.9 0.6 copy-done.6
  356.5 3.1 fusion.9
  359.5 26.9 %all-reduce = (f32[2,2560]{1,0:T(2,128)}, f32[2,2048]{1,0:T(2,128)}) all-reduce(f32[2,2560]{1,0:T(2,128)S(1)} %fusion.9, f32[2,2048]{1,0:T(2,128)S(1)} %fusion.12), channel_id=1, replica_groups=mesh['groups'=2,'member'=2,'fsdp'=8] {'fsdp'}, use_global_device_ids=true, to_apply=%region_2.0 | all-reduce | flops 9216 | bytes 73728 | tf_op jit(solution)/shard_map/psum | solution.py:31
  (1 shorter events, 0.0 us)
Async XLA Ops:
  7.2 3.8 copy-start
  7.2 3.8 copy-start.4
  7.2 104.6 %all-gather.2.cloned.1.call-start = ((), (), s32[]{:S(2)}) async-start(), calls=%async_computation.2 | async-start | bytes 11796480 | tf_op jit(solution)/shard_map/all_gather | solution.py:24
  7.9 338.9 %reduce-scatter.3.cloned.1.call-start = ((), (), s32[]{:S(2)}) async-start(), calls=%async_computation.3 | async-start | bytes 23592960 | tf_op jit(solution)/shard_map/reduce_scatter | solution.py:36
  129.4 1.3 copy-start.2
  140.6 206.3 %copy-start.3 = (bf16[384,2560]{1,0:T(8,128)(2,1)S(1)}, bf16[384,2560]{1,0:T(8,128)(2,1)}, u32[]{:S(2)}) copy-start(bf16[384,2560]{1,0:T(8,128)(2,1)} %copy-done.2) | copy-start | bytes 5898244
  140.6 245.8 %reduce-scatter.5.cloned.1.call-start = ((), (), s32[]{:S(2)}) async-start(), calls=%async_computation.4 | async-start | bytes 3932160 | tf_op jit(solution)/shard_map/reduce_scatter | solution.py:44
  346.9 7.1 %copy-start.1 = (bf16[384,2048]{1,0:T(8,128)(2,1)S(1)}, bf16[384,2048]{1,0:T(8,128)(2,1)}, u32[]{:S(2)}) copy-start(bf16[384,2048]{1,0:T(8,128)(2,1)} %param.9) | copy-start | bytes 4718596
  346.9 8.4 %copy-start.7 = (f32[384,2560]{1,0:T(8,128)S(1)}, f32[384,2560]{1,0:T(8,128)}, u32[]{:S(2)}) copy-start(f32[384,2560]{1,0:T(8,128)} %get-tuple-element.10) | copy-start | bytes 11796484
  354.0 1.9 copy-start.5
  354.0 2.5 copy-start.6
Sparse Core Ops, SparseCore 0:
  9.7 102.0 all-gather.1
  140.7 206.0 reduce-scatter.2
  349.7 35.9 reduce-scatter.4
where the time goes:
time: 393 us
  waiting for transfers between devices  304 us (77%)
  matrix products  45.6 us (12%)
  blocking collectives  26.9 us (7%)
  between operations  13.8 us (4%)
    reduce_scatter x1, waiting for transfers between devices, on_device(): lax.psum_scatter(lax.dot_general(hidden, scaled, (((0,), (0,)), ((), ()))...  206 us
    all_gather x1, waiting for transfers between devices, on_device(): whole_weight = lax.all_gather(down_weight, 'fsdp', axis=0, tiled=True)  97.2 us
    psum x1, blocking collectives, on_device(): grad_in_scale, grad_out_scale = lax.psum((local_in, local_out), 'fsdp')  26.9 us
    dot_general x1, matrix products, on_device(): lax.dot_general(scaled, whole_weight, (((1,), (1,)), ((), ())), preferred...  17.6 us
    dot_general x1, matrix products, on_device(): lax.dot_general(hidden, scaled, (((0,), (0,)), ((), ())), preferred_eleme...  9.91 us
  transfers between devices with their start and end apart: 3, of which 2 were waited for; matrix products, arithmetic and copies ran while one was open for 5% of the time, Pallas kernels for 0%

commit v1 on v0

v1 whole, which is shorter than its diff:
```python
import functools
import math

import jax
import jax.numpy as jnp
from jax import lax
from jax.experimental import pallas as pl
from jax.experimental.pallas import tpu as pltpu
from jax.sharding import PartitionSpec as P

F32 = jnp.float32
BF16 = jnp.bfloat16
VMEM_BYTES = 40 * 1024 * 1024
ROOT_2_PI = math.sqrt(2.0 / math.pi)
CUBIC = 0.044715


def tanh_of(x):
    return jnp.tanh(ROOT_2_PI * (x + CUBIC * (x * x * x)))


def pick_rows(slot, scale):
    rows = jnp.zeros((slot.shape[0], scale.shape[1]), F32)
    for k in range(scale.shape[0]):
        rows = jnp.where(slot == k, scale[k : k + 1, :], rows)
    return rows


def hidden_kernel(lo, core_ref, gate_ref, up_ref, in_scale_ref, slot_ref, *refs):
    outs, turned = refs[:lo], refs[lo]
    gate = gate_ref[...].astype(F32)
    gelu = gate * (0.5 * (1.0 + tanh_of(gate)))
    act = gelu * up_ref[...].astype(F32)
    hidden = act * pick_rows(slot_ref[...], in_scale_ref[...])
    turned[...] = hidden.T.astype(BF16)
    rows = turned.shape[0] // lo
    for j in range(lo):
        start = pl.multiple_of(lax.rem(core_ref[0] + j, lo) * rows, rows)
        outs[j][0] = turned[pl.ds(start, rows), :]


def hidden_turned(core, gate, up, in_scale, slot, blocks, lo):
    tokens, ff = gate.shape
    width = ff // blocks
    rows = width // lo
    column = pl.BlockSpec((tokens, width), lambda i, core: (0, i))
    return pl.pallas_call(
        functools.partial(hidden_kernel, lo),
        out_shape=[jax.ShapeDtypeStruct((blocks, rows, tokens), BF16)] * lo,
        grid_spec=pltpu.PrefetchScalarGridSpec(
            num_scalar_prefetch=1,
            grid=(blocks,),
            in_specs=[
                column,
                column,
                pl.BlockSpec((in_scale.shape[0], width), lambda i, core: (0, i)),
                pl.BlockSpec((tokens, 1), lambda i, core: (0, 0)),
            ],
            out_specs=[pl.BlockSpec((1, rows, tokens), lambda i, core: (i, 0, 0))] * lo,
            scratch_shapes=[pltpu.VMEM((width, tokens), BF16)],
        ),
        compiler_params=pltpu.CompilerParams(vmem_limit_bytes=VMEM_BYTES),
        cost_estimate=pl.CostEstimate(
            flops=20 * tokens * ff, bytes_accessed=6 * tokens * ff, transcendentals=tokens * ff
        ),
    )(core, gate, up, in_scale, slot)


def partial_kernel(lo, n_add, ids_ref, *refs):
    lefts, rights, adds, out_ref = refs[:lo], refs[lo : 2 * lo], refs[2 * lo : -1], refs[-1]
    total = adds[0][...].astype(F32) if n_add else None
    for i in range(1, n_add):
        total = total + adds[i][...].astype(F32)
    for left, right in zip(lefts, rights):
        term = jnp.dot(left[0], right[...], preferred_element_type=F32)
        total = term if total is None else total + term
    out_ref[...] = total.astype(out_ref.dtype)


def partial_block(block, column, lefts, rights, members, adds, dtype):
    lo = len(lefts)
    _, rows, tokens = lefts[0].shape
    width = rights[0].shape[1] // members
    ids = jnp.stack([block, column]).astype(jnp.int32)
    whole = pl.BlockSpec((rows, width), lambda i, ids: (0, 0))
    return pl.pallas_call(
        functools.partial(partial_kernel, lo, len(adds)),
        out_shape=jax.ShapeDtypeStruct((rows, width), dtype),
        grid_spec=pltpu.PrefetchScalarGridSpec(
            num_scalar_prefetch=1,
            grid=(1,),
            in_specs=[pl.BlockSpec((1, rows, tokens), lambda i, ids: (ids[0], 0, 0))] * lo
            + [pl.BlockSpec((tokens, width), lambda i, ids: (0, ids[1]))] * lo
            + [whole] * len(adds),
            out_specs=whole,
        ),
        compiler_params=pltpu.CompilerParams(vmem_limit_bytes=VMEM_BYTES),
        cost_estimate=pl.CostEstimate(
            flops=2 * lo * rows * tokens * width,
            bytes_accessed=2 * lo * tokens * (rows + width) + 4 * rows * width,
            transcendentals=0,
        ),
    )(ids, *lefts, *rights, *adds)


def slot_kernel(
    n_alias,
    ids_ref,
    weight_ref,
    scaled_ref,
    out_grad_ref,
    gate_ref,
    up_ref,
    in_scale_ref,
    slot_ref,
    *refs,
):
    grad_gate_ref, grad_up_ref, sum_in_ref, sum_out_ref = refs[n_alias:]
    weight = weight_ref[...]
    grad_hidden = lax.dot_general(
        scaled_ref[...], weight, (((1,), (1,)), ((), ())), preferred_element_type=F32
    )
    slot = slot_ref[...]
    gate = gate_ref[...].astype(F32)
    up = up_ref[...].astype(F32)
    tanh = tanh_of(gate)
    cdf = 0.5 * (1.0 + tanh)
    slope = cdf + gate * (0.5 * ROOT_2_PI) * (1.0 - tanh * tanh) * (
        1.0 + (3.0 * CUBIC) * (gate * gate)
    )
    gelu = gate * cdf
    act = gelu * up
    row_in = pick_rows(slot, in_scale_ref[...])
    hidden = (act * row_in).astype(BF16)
    grad_act = grad_hidden * row_in
    grad_gate_ref[...] = (grad_act * up * slope).astype(BF16)
    grad_up_ref[...] = (grad_act * gelu).astype(BF16)
    product = grad_hidden * act
    forward = jnp.dot(hidden, weight, preferred_element_type=F32)
    forward = forward * out_grad_ref[...].astype(F32)
    for k in range(in_scale_ref.shape[0]):
        mine = slot == k
        sum_in_ref[k : k + 1, :] = jnp.sum(jnp.where(mine, product, 0.0), axis=0, keepdims=True)
        sum_out_ref[k : k + 1, :] = jnp.sum(jnp.where(mine, forward, 0.0), axis=0, keepdims=True)


def weight_slot(block, weight, scaled, out_grad, gate, up, in_scale, slot, kept):
    tokens, ff = gate.shape
    width, d = weight.shape
    mem = in_scale.shape[0]
    ids = jnp.reshape(block, (1,)).astype(jnp.int32)
    column = pl.BlockSpec((tokens, width), lambda i, ids: (0, ids[0]))
    full = lambda shape: pl.BlockSpec(shape, lambda i, ids: (0, 0))
    ins = [weight, scaled, out_grad, gate, up, in_scale, slot]
    specs = [
        full((width, d)),
        full((tokens, d)),
        full((tokens, d)),
        column,
        column,
        pl.BlockSpec((mem, width), lambda i, ids: (0, ids[0])),
        full((tokens, 1)),
    ]
    aliases = {}
    if kept is not None:
        aliases = {1 + len(ins): 0, 2 + len(ins): 1}
        ins += list(kept)
        specs += [pl.BlockSpec(memory_space=pl.ANY)] * 2
    return pl.pallas_call(
        functools.partial(slot_kernel, len(aliases)),
        out_shape=[
            jax.ShapeDtypeStruct((tokens, ff), BF16),
            jax.ShapeDtypeStruct((tokens, ff), BF16),
            jax.ShapeDtypeStruct((mem, width), F32),
            jax.ShapeDtypeStruct((mem, d), F32),
        ],
        grid_spec=pltpu.PrefetchScalarGridSpec(
            num_scalar_prefetch=1,
            grid=(1,),
            in_specs=specs,
            out_specs=[column, column, full((mem, width)), full((mem, d))],
        ),
        input_output_aliases=aliases,
        compiler_params=pltpu.CompilerParams(vmem_limit_bytes=VMEM_BYTES),
        cost_estimate=pl.CostEstimate(
            flops=4 * tokens * width * d,
            bytes_accessed=2 * width * d + 4 * tokens * d + 8 * tokens * width,
            transcendentals=tokens * width,
        ),
    )(ids, *ins)


def place(pieces, me):
    n, rows = len(pieces), pieces[0].shape[0]
    if n == 1:
        return pieces[0]
    if n == 2:
        first = me == 0
        return jnp.concatenate(
            [jnp.where(first, pieces[0], pieces[1]), jnp.where(first, pieces[1], pieces[0])]
        )
    whole = jnp.zeros((n * rows,) + pieces[0].shape[1:], pieces[0].dtype)
    for j, piece in enumerate(pieces):
        whole = lax.dynamic_update_slice_in_dim(whole, piece, lax.rem(me + j, n) * rows, 0)
    return whole


def on_device(groups, members, fsdp):
    def run(gate, up, out_grad, in_scale, out_scale, weight, member_slot):
        tokens, ff = gate.shape
        shard = weight.shape[0]
        lo = 128 // math.gcd(shard, 128)
        line = fsdp // lo
        group = lax.axis_index("groups")
        member = lax.axis_index("member")
        place_id = lax.axis_index("fsdp")
        z, core = place_id // lo, lax.rem(place_id, lo)
        lower = z < line // 2
        slot = member_slot[:, None]

        def along_line(x, sources, step):
            pairs = [(s * lo + c, (s + step) * lo + c) for s in sources for c in range(lo)]
            return lax.ppermute(x, "fsdp", pairs)

        def within_chip(x, j):
            pairs = [
                (s * lo + (c + j) % lo, s * lo + c) for s in range(line) for c in range(lo)
            ]
            return lax.ppermute(x, "fsdp", pairs)

        def cyclic(x, axis, n, j):
            return lax.ppermute(x, axis, [((i + j) % n, i) for i in range(n)])

        part = shard // groups
        piece = lax.dynamic_slice_in_dim(weight, group * part, part, 0)
        ups, downs = [piece], [piece]
        for s in range(1, line):
            ups.append(along_line(ups[-1], range(s - 1, line - 1), 1))
            downs.append(along_line(downs[-1], range(1, line - s + 1), -1))

        scaled = (out_grad.astype(F32) * pick_rows(slot, out_scale)).astype(BF16)
        turned = hidden_turned(
            jnp.reshape(core, (1,)).astype(jnp.int32), gate, up, in_scale, slot, line, lo
        )
        lefts, rights = [turned[0]], [scaled]
        for j in range(1, lo):
            rights.append(within_chip(scaled, j))
            lefts.append(within_chip(turned[(lo - j) % lo], j))

        sums = [None] * line
        for k in list(range(1, line)) + [0]:
            block = lax.rem(jnp.where(lower, z - k, z + k) + line, line)
            got = []
            for j in range(1, members):
                to = lax.rem(member + members - j, members)
                send = partial_block(block, to, lefts, rights, members, [], BF16)
                got.append(cyclic(send, "member", members, j))
            sums[k] = partial_block(block, member, lefts, rights, members, got, F32)

        from_below = from_above = None
        for s in range(1, line):
            send_up = send_down = sums[s]
            if 2 * s > line:
                send_up = jnp.where(lower, sums[s], sums[line - s])
                send_down = jnp.where(lower, sums[line - s], sums[s])
            if from_below is not None:
                send_up = send_up + from_below.astype(F32)
                send_down = send_down + from_above.astype(F32)
            from_below = along_line(send_up.astype(BF16), range(s), 1)
            from_above = along_line(send_down.astype(BF16), range(line - s, line), -1)
        grad_down = sums[0] + from_below.astype(F32) + from_above.astype(F32)

        kept, sums_in, sum_out = None, jnp.zeros((in_scale.shape[0], ff), F32), None
        for j in range(line):
            block = lax.rem(jnp.where(lower, z + j, z - j) + line, line)
            if j == 0:
                rows = weight
            else:
                mine = jnp.where(lower, downs[j], ups[j])
                if 2 * j > line:
                    mine = jnp.where(
                        lower,
                        jnp.where(z + j < line, downs[j], ups[line - j]),
                        jnp.where(z >= j, ups[j], downs[line - j]),
                    )
                parts = [mine] + [cyclic(mine, "groups", groups, i) for i in range(1, groups)]
                rows = place(parts, group)
            rows = place([rows] + [within_chip(rows, i) for i in range(1, lo)], core)
            *kept, sum_in, more = weight_slot(
                block, rows, scaled, out_grad, gate, up, in_scale, slot, kept
            )
            sums_in = lax.dynamic_update_slice_in_dim(
                sums_in, sum_in, block * sum_in.shape[1], 1
            )
            sum_out = more if sum_out is None else sum_out + more
        both = jnp.concatenate([sums_in, sum_out], axis=1)
        if fsdp & (fsdp - 1):
            both = lax.psum(both, "fsdp")
        else:
            stage = 1
            while stage < fsdp:
                both = both + lax.ppermute(both, "fsdp", [(i, i ^ stage) for i in range(fsdp)])
                stage *= 2
        return kept[0], kept[1], grad_down, both[:, :ff], both[:, ff:]

    return run


def solution(mesh):
    rows = P(("groups", "member", "fsdp"), None)
    in_specs = (
        rows,
        rows,
        rows,
        P("member", None),
        P("member", None),
        P("fsdp", None),
        P(("groups", "member", "fsdp")),
    )
    out_specs = (
        rows,
        rows,
        P(("groups", "fsdp"), "member"),
        P(("groups", "member"), None),
        P(("groups", "member"), None),
    )
    run = on_device(mesh.shape["groups"], mesh.shape["member"], mesh.shape["fsdp"])
    return jax.shard_map(run, mesh=mesh, in_specs=in_specs, out_specs=out_specs, check_vma=False)
```

time: 393 us -> 178 us (0.45)
  waiting for transfers between devices: 304 us -> 64 us
  starting transfers between devices: 0.3 us -> 49.1 us
  matrix products: 45.6 us -> 0 us
  Pallas kernels: 0 us -> 36.5 us
  blocking collectives: 26.9 us -> 0 us
  other arithmetic: 0 us -> 17.6 us
  between operations: 13.8 us -> 1.14 us
  local copies, waits for them, and re-layouts: 2.43 us -> 8.38 us
    reduce_scatter x2 -> x0, waiting for transfers between devices: 206 us -> none  [the longest x1 206 us: on_device(): lax.psum_scatter(lax.dot_general(hidden, scaled, (((0,), (0,)), ((), ()))...]
    all_gather x1 -> x0, waiting for transfers between devices: 97.2 us -> none  [on_device(): whole_weight = lax.all_gather(down_weight, 'fsdp', axis=0, tiled=True)]
    ppermute x0 -> x28, waiting for transfers between devices: none -> 64 us  [the longest x7 24.3 us: cyclic(): return lax.ppermute(x, axis, [((i + j) % n, i) for i in range(n)])]
    ppermute x0 -> x28, starting transfers between devices: none -> 49.1 us  [the longest x12 35.9 us: along_line(): return lax.ppermute(x, 'fsdp', pairs)]
    dot_general x7 -> x0, matrix products: 45.6 us -> none  [the longest x1 17.6 us: on_device(): lax.dot_general(scaled, whole_weight, (((1,), (1,)), ((), ())), preferred...]
    pallas_call x0 -> x13, Pallas kernels: none -> 36.5 us  [the longest x8 18.5 us: partial_block(): pl.pallas_call(functools.partial(partial_kernel, lo, len(adds)), out_shap...]
    psum x1 -> x0, blocking collectives: 26.9 us -> none  [on_device(): grad_in_scale, grad_out_scale = lax.psum((local_in, local_out), 'fsdp')]
    select_n x0 -> x8, other arithmetic: none -> 8.52 us  [the longest x6 5.87 us: place(): jnp.where(first, pieces[0], pieces[1])]
  transfers between devices with their start and end apart: 3 -> 28, of which waited for: 2 -> 7; matrix products, arithmetic and copies ran while one was open for 5% -> 10% of each run, Pallas kernels for 0% -> 21%
where the time goes in v1:
time: 178 us; the launch traced here: 177 us
  waiting for transfers between devices  64 us (36%)
  starting transfers between devices  49.1 us (28%)
  Pallas kernels  36.5 us (21%)
  other arithmetic  17.6 us (10%)
  local copies, waits for them, and re-layouts  8.38 us (5%)
    ppermute x12, starting transfers between devices, along_line(): return lax.ppermute(x, 'fsdp', pairs)  35.9 us
    ppermute x7, waiting for transfers between devices, cyclic(): return lax.ppermute(x, axis, [((i + j) % n, i) for i in range(n)])  24.3 us
    ppermute x12, waiting for transfers between devices, along_line(): return lax.ppermute(x, 'fsdp', pairs)  22.9 us
    pallas_call x8, Pallas kernels, partial_block(): pl.pallas_call(functools.partial(partial_kernel, lo, len(adds)), out_shap...  18.5 us
    ppermute x3, waiting for transfers between devices, run(): lax.ppermute(both, 'fsdp', [(i, i ^ stage) for i in range(fsdp)])  16.7 us
    pallas_call x4, Pallas kernels, weight_slot(): pl.pallas_call(functools.partial(slot_kernel, len(aliases)), out_shape=[j...  13.7 us
    ppermute x7, starting transfers between devices, cyclic(): return lax.ppermute(x, axis, [((i + j) % n, i) for i in range(n)])  7.22 us
    select_n x6, other arithmetic, place(): jnp.where(first, pieces[0], pieces[1])  5.87 us
  transfers between devices with their start and end apart: 28, of which 7 were waited for; matrix products, arithmetic and copies ran while one was open for 10% of the time, Pallas kernels for 21%

profile of v1, /device:TPU:0, one launch (start us, length us, event | category | flops | bytes accessed | tf_op | source)
XLA Modules:
  0.0 176.7 jit_solution(17848757044044545101)
XLA Ops:
  0.7 2.0 %constant_dynamic-slice_fusion = bf16[160,2048]{1,0:T(8,128)(2,1)} fusion(bf16[320,2048]{1,0:T(8,128)(2,1)} %param.12, s32[]{:T(128)S(6)} %select_n.155), kind=kLoop, calls=%fused_computation.36 | loop fusion | bytes 1310724 | tf_op jit(solution)/shard_map/dynamic_slice | solution.py:235
  3.9 6.4 %collective-permute-start.3 = (bf16[160,2048]{1,0:T(8,128)(2,1)}, bf16[160,2048]{1,0:T(8,128)(2,1)}, u32[]{:S(2)}, u32[]{:S(2)}) collective-permute-start(bf16[160,2048]{1,0:T(8,128)(2,1)} %constant_dynamic-slice_fusion), channel_id=1, source_target_pairs={{0,2},{1,3},{2,4},{3,5},{4,6},{5,7},{8,10},{9,11},{10,12},{11,13},... | collective-permute-start | bytes 1966088 | tf_op jit(solution)/shard_map/ppermute | solution.py:223
  10.5 1.5 copy-done.2
  12.1 1.5 copy-done.4
  13.6 4.3 %shard_map.114 = (bf16[4,320,384]{2,1,0:T(8,128)(2,1)S(1)}, bf16[4,320,384]{2,1,0:T(8,128)(2,1)}) custom-call(s32[1]{0:T(128)} %bitcast.7.core_ref, bf16[384,2560]{1,0:T(8,128)(2,1)S(1)} %copy-done.2, bf16[384,2560]{1,0:T(8,128)(2,1)S(1)} %copy-done.4, f32[2,2560]{1,0:T(2,128)S(1)} %copy-done.8, s32[384,1]{1,0:T(8,128)S(1)} %broadcast_in_dim.48.slot_ref), custom_call_target="tpu_custom_call" | custom-call | flops 19660800 | bytes 5898240 | tf_op jit(solution)/shard_map/pallas_call | solution.py:47
  19.5 3.1 %collective-permute-done = bf16[160,2048]{1,0:T(8,128)(2,1)} collective-permute-done((bf16[160,2048]{1,0:T(8,128)(2,1)}, bf16[160,2048]{1,0:T(8,128)(2,1)}, u32[]{:S(2)}, u32[]{:S(2)}) %collective-permute-start) | collective-permute-done | bytes 655392 | tf_op jit(solution)/shard_map/ppermute | solution.py:223
  25.9 14.9 %collective-permute-done.1 = bf16[160,2048]{1,0:T(8,128)(2,1)} collective-permute-done((bf16[160,2048]{1,0:T(8,128)(2,1)}, bf16[160,2048]{1,0:T(8,128)(2,1)}, u32[]{:S(2)}, u32[]{:S(2)}) %collective-permute-start.1) | collective-permute-done | bytes 655392 | tf_op jit(solution)/shard_map/ppermute | solution.py:223
  45.3 2.0 %broadcast_select_fusion.1 = (bf16[320,2048]{1,0:T(8,128)(2,1)S(1)}, bf16[320,2048]{1,0:T(8,128)(2,1)S(1)}) fusion(bf16[320,2048]{1,0:T(8,128)(2,1)} %param.12, bf16[320,2048]{1,0:T(8,128)(2,1)} %collective-permute-done.12, pred[]{:T(512)S(6)} %eq.25), kind=kLoop, calls=%fused_computation.14 | loop fusion | flops 1310720 | bytes 5242881 | tf_op jit(solution)/shard_map/jit(_where)/select_n | solution.py:200
  49.5 3.4 %shard_map.110 = (bf16[384,2560]{1,0:T(8,128)(2,1)}, bf16[384,2560]{1,0:T(8,128)(2,1)}, f32[2,640]{1,0:T(2,128)S(1)}, f32[2,2048]{1,0:T(2,128)S(1)}) custom-call(s32[1]{0:T(128)} %bitcast.5.ids_ref, bf16[640,2048]{1,0:T(8,128)(2,1)S(1)} %pad_maximum_fusion.3.weight_ref, bf16[384,2048]{1,0:T(8,128)(2,1)S(1)} %multiply_convert_fusion.scaled_ref.refs_2_, ...), custom_call_target="tpu_custom_call" | custom-call | flops 2013265920 | bytes 7733248 | tf_op jit(solution)/shard_map/pallas_call | solution.py:169
  53.0 2.3 %shard_map.119 = bf16[320,1024]{1,0:T(8,128)(2,1)S(1)} custom-call(s32[2]{0:T(128)S(1)} %pad_add_fusion.4.ids_ref, bf16[4,320,384]{2,1,0:T(8,128)(2,1)S(1)} %copy-done.1, bf16[4,320,384]{2,1,0:T(8,128)(2,1)} %collective-permute-done.13.refs_1_, bf16[384,2048]{1,0:T(8,128)(2,1)S(1)} %multiply_convert_fusion.scaled_ref.refs_2_, ...), custom_call_target="tpu_custom_call" | custom-call | flops 503316480 | bytes 3375104 | tf_op jit(solution)/shard_map/pallas_call | solution.py:86
  55.3 1.5 collective-permute-start.17
  56.8 2.3 %shard_map.121 = bf16[320,1024]{1,0:T(8,128)(2,1)S(1)} custom-call(s32[2]{0:T(128)S(1)} %pad_add_fusion.6.ids_ref, bf16[4,320,384]{2,1,0:T(8,128)(2,1)S(1)} %copy-done.1, bf16[4,320,384]{2,1,0:T(8,128)(2,1)} %collective-permute-done.13.refs_1_, bf16[384,2048]{1,0:T(8,128)(2,1)S(1)} %multiply_convert_fusion.scaled_ref.refs_2_, ...), custom_call_target="tpu_custom_call" | custom-call | flops 503316480 | bytes 3375104 | tf_op jit(solution)/shard_map/pallas_call | solution.py:86
  59.8 2.3 %shard_map.117 = bf16[320,1024]{1,0:T(8,128)(2,1)S(1)} custom-call(s32[2]{0:T(128)S(1)} %pad_add_fusion.2.ids_ref, bf16[4,320,384]{2,1,0:T(8,128)(2,1)S(1)} %copy-done.1, bf16[4,320,384]{2,1,0:T(8,128)(2,1)} %collective-permute-done.13.refs_1_, bf16[384,2048]{1,0:T(8,128)(2,1)S(1)} %multiply_convert_fusion.scaled_ref.refs_2_, ...), custom_call_target="tpu_custom_call" | custom-call | flops 503316480 | bytes 3375104 | tf_op jit(solution)/shard_map/pallas_call | solution.py:86
  62.1 1.5 collective-permute-start.16
  66.1 14.0 %collective-permute-done.10 = bf16[160,2048]{1,0:T(8,128)(2,1)S(1)} collective-permute-done((bf16[160,2048]{1,0:T(8,128)(2,1)S(1)}, bf16[160,2048]{1,0:T(8,128)(2,1)S(1)}, u32[]{:S(2)}, u32[]{:S(2)}) %collective-permute-start.10) | collective-permute-done | bytes 655392 | tf_op jit(solution)/shard_map/ppermute | solution.py:232
  82.0 2.3 %shard_map.115 = bf16[320,1024]{1,0:T(8,128)(2,1)S(1)} custom-call(s32[2]{0:T(128)S(1)} %pad_add_fusion.ids_ref, bf16[4,320,384]{2,1,0:T(8,128)(2,1)S(1)} %copy-done.1, bf16[4,320,384]{2,1,0:T(8,128)(2,1)} %collective-permute-done.13.refs_1_, bf16[384,2048]{1,0:T(8,128)(2,1)S(1)} %multiply_convert_fusion.scaled_ref.refs_2_, ...), custom_call_target="tpu_custom_call" | custom-call | flops 503316480 | bytes 3375104 | tf_op jit(solution)/shard_map/pallas_call | solution.py:86
  84.3 2.3 %shard_map.120 = f32[320,1024]{1,0:T(8,128)S(1)} custom-call(s32[2]{0:T(128)S(1)} %pad_add_fusion.5.ids_ref, bf16[4,320,384]{2,1,0:T(8,128)(2,1)S(1)} %copy-done.1, bf16[4,320,384]{2,1,0:T(8,128)(2,1)} %collective-permute-done.13.refs_1_, bf16[384,2048]{1,0:T(8,128)(2,1)S(1)} %multiply_convert_fusion.scaled_ref.refs_2_, ...), custom_call_target="tpu_custom_call" | custom-call | flops 503316480 | bytes 3375104 | tf_op jit(solution)/shard_map/pallas_call | solution.py:86
  88.6 2.3 %shard_map.122 = f32[320,1024]{1,0:T(8,128)S(1)} custom-call(s32[2]{0:T(128)S(1)} %pad_add_fusion.7.ids_ref, bf16[4,320,384]{2,1,0:T(8,128)(2,1)S(1)} %copy-done.1, bf16[4,320,384]{2,1,0:T(8,128)(2,1)} %collective-permute-done.13.refs_1_, bf16[384,2048]{1,0:T(8,128)(2,1)S(1)} %multiply_convert_fusion.scaled_ref.refs_2_, ...), custom_call_target="tpu_custom_call" | custom-call | flops 503316480 | bytes 3375104 | tf_op jit(solution)/shard_map/pallas_call | solution.py:86
  90.9 10.2 %collective-permute-done.16.refs_4_ = bf16[320,1024]{1,0:T(8,128)(2,1)S(1)} collective-permute-done((bf16[320,1024]{1,0:T(8,128)(2,1)S(1)}, bf16[320,1024]{1,0:T(8,128)(2,1)S(1)}, u32[]{:S(2)}, u32[]{:S(2)}) %collective-permute-start.16) | collective-permute-done | bytes 655392 | tf_op jit(solution)/shard_map/ppermute | solution.py:232
  101.1 5.6 %collective-permute-start.19 = (bf16[320,1024]{1,0:T(8,128)(2,1)}, bf16[320,1024]{1,0:T(8,128)(2,1)S(1)}, u32[]{:S(2)}, u32[]{:S(2)}) collective-permute-start(bf16[320,1024]{1,0:T(8,128)(2,1)} %convert_element_type.42), channel_id=1, source_target_pairs={{0,2},{1,3},{8,10},{9,11},{16,18},{17,19},{24,26},{25,27}} | collective-permute-start | bytes 1966088 | tf_op jit(solution)/shard_map/ppermute | solution.py:223
  106.7 2.3 %shard_map.118 = f32[320,1024]{1,0:T(8,128)S(1)} custom-call(s32[2]{0:T(128)S(1)} %pad_add_fusion.3.ids_ref, bf16[4,320,384]{2,1,0:T(8,128)(2,1)S(1)} %copy-done.1, bf16[4,320,384]{2,1,0:T(8,128)(2,1)} %collective-permute-done.13.refs_1_, bf16[384,2048]{1,0:T(8,128)(2,1)S(1)} %multiply_convert_fusion.scaled_ref.refs_2_, ...), custom_call_target="tpu_custom_call" | custom-call | flops 503316480 | bytes 3375104 | tf_op jit(solution)/shard_map/pallas_call | solution.py:86
  110.2 4.9 %collective-permute-done.19 = bf16[320,1024]{1,0:T(8,128)(2,1)S(1)} collective-permute-done((bf16[320,1024]{1,0:T(8,128)(2,1)}, bf16[320,1024]{1,0:T(8,128)(2,1)S(1)}, u32[]{:S(2)}, u32[]{:S(2)}) %collective-permute-start.19) | collective-permute-done | bytes 655392 | tf_op jit(solution)/shard_map/ppermute | solution.py:223
  116.6 5.1 %collective-permute-start.20 = (bf16[320,1024]{1,0:T(8,128)(2,1)}, bf16[320,1024]{1,0:T(8,128)(2,1)}, u32[]{:S(2)}, u32[]{:S(2)}) collective-permute-start(bf16[320,1024]{1,0:T(8,128)(2,1)} %get-tuple-element.51), channel_id=1, source_target_pairs={{0,2},{1,3},{2,4},{3,5},{8,10},{9,11},{10,12},{11,13},{16,18},{17,... | collective-permute-start | bytes 1966088 | tf_op jit(solution)/shard_map/ppermute | solution.py:223
  123.2 2.8 %broadcast_select_fusion.3 = (bf16[320,2048]{1,0:T(8,128)(2,1)S(1)}, bf16[320,2048]{1,0:T(8,128)(2,1)S(1)}, bf16[320,2048]{1,0:T(8,128)(2,1)S(1)}, bf16[320,2048]{1,0:T(8,128)(2,1)S(1)}) fusion(bf16[320,2048]{1,0:T(8,128)(2,1)} %collective-permute-done.11, pred[]{:T(512)S(6)} %eq.25, bf16[160,2048]{1,0:T(8,128)(2,1)S(1)} %get-tuple-element.54, ...), kind=kLoop, calls=%fused_computation.16 | loop fusion | flops 7864320 | bytes 10485761 | tf_op jit(solution)/shard_map/jit(_where)/select_n | solution.py:200
  127.3 3.4 %shard_map.111 = (bf16[384,2560]{1,0:T(8,128)(2,1)}, bf16[384,2560]{1,0:T(8,128)(2,1)}, f32[2,640]{1,0:T(2,128)S(1)}, f32[2,2048]{1,0:T(2,128)S(1)}) custom-call(s32[1]{0:T(128)} %bitcast.4.ids_ref, bf16[640,2048]{1,0:T(8,128)(2,1)S(1)} %pad_maximum_fusion.2.weight_ref, ...), custom_call_target="tpu_custom_call", output_to_operand_aliasing={{0}: (8, {}), {1}: (9, {})} | custom-call | flops 2013265920 | bytes 7733248 | tf_op jit(solution)/shard_map/pallas_call | solution.py:169
  130.8 3.4 %shard_map.112 = (bf16[384,2560]{1,0:T(8,128)(2,1)}, bf16[384,2560]{1,0:T(8,128)(2,1)}, f32[2,640]{1,0:T(2,128)S(1)}, f32[2,2048]{1,0:T(2,128)S(1)}) custom-call(s32[1]{0:T(128)} %bitcast.3.ids_ref, bf16[640,2048]{1,0:T(8,128)(2,1)S(1)} %pad_maximum_fusion.1.weight_ref, ...), custom_call_target="tpu_custom_call", output_to_operand_aliasing={{0}: (8, {}), {1}: (9, {})} | custom-call | flops 2013265920 | bytes 7733248 | tf_op jit(solution)/shard_map/pallas_call | solution.py:169
  134.2 3.4 %shard_map.113 = (bf16[384,2560]{1,0:T(8,128)(2,1)}, bf16[384,2560]{1,0:T(8,128)(2,1)}, f32[2,640]{1,0:T(2,128)S(1)}, f32[2,2048]{1,0:T(2,128)S(1)}) custom-call(s32[1]{0:T(128)} %bitcast.ids_ref, bf16[640,2048]{1,0:T(8,128)(2,1)S(1)} %pad_maximum_fusion.weight_ref, ...), custom_call_target="tpu_custom_call", output_to_operand_aliasing={{0}: (8, {}), {1}: (9, {})} | custom-call | flops 2013265920 | bytes 7733248 | tf_op jit(solution)/shard_map/pallas_call | solution.py:169
  138.0 1.8 add_convert_fusion.2
  139.8 9.0 %collective-permute-start.21 = (bf16[320,1024]{1,0:T(8,128)(2,1)S(1)}, bf16[320,1024]{1,0:T(8,128)(2,1)S(1)}, u32[]{:S(2)}, u32[]{:S(2)}) collective-permute-start(bf16[320,1024]{1,0:T(8,128)(2,1)S(1)} %get-tuple-element.41), channel_id=1, source_target_pairs={{0,2},{1,3},{2,4},{3,5},{4,6},{5,7},{8,10},{9,11},{10,12},{11,13},... | collective-permute-start | bytes 1966088 | tf_op jit(solution)/shard_map/ppermute | solution.py:223
  150.2 3.3 %collective-permute-start.26 = (f32[2,4608]{1,0:T(2,128)S(1)}, f32[2,4608]{1,0:T(2,128)S(1)}, u32[]{:S(2)}, u32[]{:S(2)}) collective-permute-start(f32[2,4608]{1,0:T(2,128)S(1)} %fusion), channel_id=1, source_target_pairs={{0,2},{1,3},{2,0},{3,1},{4,6},{5,7},{6,4},{7,5},{8,10},{9,11},{10,... | collective-permute-start | bytes 110600 | tf_op jit(solution)/shard_map/ppermute | solution.py:302
  153.5 15.7 %collective-permute-done.26 = f32[2,4608]{1,0:T(2,128)S(1)} collective-permute-done((f32[2,4608]{1,0:T(2,128)S(1)}, f32[2,4608]{1,0:T(2,128)S(1)}, u32[]{:S(2)}, u32[]{:S(2)}) %collective-permute-start.26) | collective-permute-done | bytes 36896 | tf_op jit(solution)/shard_map/ppermute | solution.py:302
  170.7 2.3 %shard_map.116 = f32[320,1024]{1,0:T(8,128)S(1)} custom-call(s32[2]{0:T(128)S(1)} %pad_add_fusion.1.ids_ref, bf16[4,320,384]{2,1,0:T(8,128)(2,1)S(1)} %copy-done.1, bf16[4,320,384]{2,1,0:T(8,128)(2,1)} %collective-permute-done.13.refs_1_, bf16[384,2048]{1,0:T(8,128)(2,1)S(1)} %multiply_convert_fusion.scaled_ref.refs_2_, ...), custom_call_target="tpu_custom_call" | custom-call | flops 503316480 | bytes 3375104 | tf_op jit(solution)/shard_map/pallas_call | solution.py:86
  (103 shorter events, 32.1 us)
Async XLA Ops:
  0.6 9.7 %copy-start.10 = (s32[384]{0:T(512)S(1)}, s32[384]{0:T(512)}, u32[]{:S(2)}) copy-start(s32[384]{0:T(512)} %param.13) | copy-start | bytes 4612
  0.6 9.8 %copy-start.8 = (f32[2,2560]{1,0:T(2,128)S(1)}, f32[2,2560]{1,0:T(2,128)}, u32[]{:S(2)}) copy-start(f32[2,2560]{1,0:T(2,128)} %in_scale_ref.9) | copy-start | bytes 61444
  2.6 20.0 %collective-permute-start = (bf16[160,2048]{1,0:T(8,128)(2,1)}, bf16[160,2048]{1,0:T(8,128)(2,1)}, u32[]{:S(2)}, u32[]{:S(2)}) collective-permute-start(bf16[160,2048]{1,0:T(8,128)(2,1)} %constant_dynamic-slice_fusion), channel_id=1, source_target_pairs={{2,0},{3,1},{4,2},{5,3},{6,4},{7,5},{10,8},{11,9},{12,10},{13,11},... | collective-permute-start | bytes 1966088 | tf_op jit(solution)/shard_map/ppermute | solution.py:223
  3.9 20.0 %collective-permute-start.3 = (bf16[160,2048]{1,0:T(8,128)(2,1)}, bf16[160,2048]{1,0:T(8,128)(2,1)}, u32[]{:S(2)}, u32[]{:S(2)}) collective-permute-start(bf16[160,2048]{1,0:T(8,128)(2,1)} %constant_dynamic-slice_fusion), channel_id=1, source_target_pairs={{0,2},{1,3},{2,4},{3,5},{4,6},{5,7},{8,10},{9,11},{10,12},{11,13},... | collective-permute-start | bytes 1966088 | tf_op jit(solution)/shard_map/ppermute | solution.py:223
  10.4 34.2 %collective-permute-start.12 = (bf16[320,2048]{1,0:T(8,128)(2,1)}, bf16[320,2048]{1,0:T(8,128)(2,1)}, u32[]{:S(2)}, u32[]{:S(2)}) collective-permute-start(bf16[320,2048]{1,0:T(8,128)(2,1)} %param.12), channel_id=1, source_target_pairs={{1,0},{0,1},{3,2},{2,3},{5,4},{4,5},{7,6},{6,7},{9,8},{8,9},{11,10... | collective-permute-start | bytes 3932168 | tf_op jit(solution)/shard_map/ppermute | solution.py:229
  13.6 4.8 %copy-start.9 = (f32[2,2048]{1,0:T(2,128)S(1)}, f32[2,2048]{1,0:T(2,128)}, u32[]{:S(2)}) copy-start(f32[2,2048]{1,0:T(2,128)} %param.11) | copy-start | bytes 49156
  13.6 4.8 %copy-start.6 = (bf16[384,2048]{1,0:T(8,128)(2,1)S(1)}, bf16[384,2048]{1,0:T(8,128)(2,1)}, u32[]{:S(2)}) copy-start(bf16[384,2048]{1,0:T(8,128)(2,1)} %out_grad_ref.7) | copy-start | bytes 4718596
  17.9 35.0 %collective-permute-start.13 = (bf16[4,320,384]{2,1,0:T(8,128)(2,1)}, bf16[4,320,384]{2,1,0:T(8,128)(2,1)}, u32[]{:S(2)}, u32[]{:S(2)}) collective-permute-start(bf16[4,320,384]{2,1,0:T(8,128)(2,1)} %get-tuple-element.32), channel_id=1, source_target_pairs={{1,0},{0,1},{3,2},{2,3},{5,4},{4,5},{7,6},{6,7},{9,8},{8,9},{11,10... | collective-permute-start | bytes 2949128 | tf_op jit(solution)/shard_map/ppermute | solution.py:229
  19.1 33.9 %collective-permute-start.14 = (bf16[384,2048]{1,0:T(8,128)(2,1)S(1)}, bf16[384,2048]{1,0:T(8,128)(2,1)S(1)}, u32[]{:S(2)}, u32[]{:S(2)}) collective-permute-start(bf16[384,2048]{1,0:T(8,128)(2,1)S(1)} %multiply_convert_fusion.scaled_ref.refs_2_), channel_id=1, source_target_pairs={{1,0},{0,1},{3,2},{2,3},{5,4},{4,5},{7,6},{6,7},{9,8},{8,9},{11,10... | collective-permute-start | bytes 4718600 | tf_op jit(solution)/shard_map/ppermute | solution.py:229
  22.6 18.1 %collective-permute-start.1 = (bf16[160,2048]{1,0:T(8,128)(2,1)}, bf16[160,2048]{1,0:T(8,128)(2,1)}, u32[]{:S(2)}, u32[]{:S(2)}) collective-permute-start(bf16[160,2048]{1,0:T(8,128)(2,1)} %collective-permute-done), channel_id=1, source_target_pairs={{2,0},{3,1},{4,2},{5,3},{10,8},{11,9},{12,10},{13,11},{18,16},{19,... | collective-permute-start | bytes 1966088 | tf_op jit(solution)/shard_map/ppermute | solution.py:223
  23.9 16.8 %collective-permute-start.4 = (bf16[160,2048]{1,0:T(8,128)(2,1)}, bf16[160,2048]{1,0:T(8,128)(2,1)}, u32[]{:S(2)}, u32[]{:S(2)}) collective-permute-start(bf16[160,2048]{1,0:T(8,128)(2,1)} %collective-permute-done.3), channel_id=1, source_target_pairs={{2,4},{3,5},{4,6},{5,7},{10,12},{11,13},{12,14},{13,15},{18,20},{1... | collective-permute-start | bytes 1966088 | tf_op jit(solution)/shard_map/ppermute | solution.py:223
  41.9 23.8 %collective-permute-start.8 = (bf16[160,2048]{1,0:T(8,128)(2,1)S(1)}, bf16[160,2048]{1,0:T(8,128)(2,1)S(1)}, u32[]{:S(2)}, u32[]{:S(2)}) collective-permute-start(bf16[160,2048]{1,0:T(8,128)(2,1)S(1)} %broadcast_select_fusion.9), channel_id=1, source_target_pairs={{16,0},{0,16},{17,1},{1,17},{18,2},{2,18},{19,3},{3,19},{20,4},{4,... | collective-permute-start | bytes 1966088 | tf_op jit(solution)/shard_map/ppermute | solution.py:232
  43.3 18.8 %collective-permute-start.2 = (bf16[160,2048]{1,0:T(8,128)(2,1)}, bf16[160,2048]{1,0:T(8,128)(2,1)S(1)}, u32[]{:S(2)}, u32[]{:S(2)}) collective-permute-start(bf16[160,2048]{1,0:T(8,128)(2,1)} %collective-permute-done.1), channel_id=1, source_target_pairs={{2,0},{3,1},{10,8},{11,9},{18,16},{19,17},{26,24},{27,25}} | collective-permute-start | bytes 1966088 | tf_op jit(solution)/shard_map/ppermute | solution.py:223
  44.6 19.0 %collective-permute-start.5 = (bf16[160,2048]{1,0:T(8,128)(2,1)}, bf16[160,2048]{1,0:T(8,128)(2,1)S(1)}, u32[]{:S(2)}, u32[]{:S(2)}) collective-permute-start(bf16[160,2048]{1,0:T(8,128)(2,1)} %collective-permute-done.4), channel_id=1, source_target_pairs={{4,6},{5,7},{12,14},{13,15},{20,22},{21,23},{28,30},{29,31}} | collective-permute-start | bytes 1966088 | tf_op jit(solution)/shard_map/ppermute | solution.py:223
  55.3 26.6 %collective-permute-start.17 = (bf16[320,1024]{1,0:T(8,128)(2,1)S(1)}, bf16[320,1024]{1,0:T(8,128)(2,1)S(1)}, u32[]{:S(2)}, u32[]{:S(2)}) collective-permute-start(bf16[320,1024]{1,0:T(8,128)(2,1)S(1)} %shard_map.119), channel_id=1, source_target_pairs={{8,0},{0,8},{9,1},{1,9},{10,2},{2,10},{11,3},{3,11},{12,4},{4,12},... | collective-permute-start | bytes 1966088 | tf_op jit(solution)/shard_map/ppermute | solution.py:232
  59.2 28.4 %collective-permute-start.18 = (bf16[320,1024]{1,0:T(8,128)(2,1)S(1)}, bf16[320,1024]{1,0:T(8,128)(2,1)S(1)}, u32[]{:S(2)}, u32[]{:S(2)}) collective-permute-start(bf16[320,1024]{1,0:T(8,128)(2,1)S(1)} %shard_map.121), channel_id=1, source_target_pairs={{8,0},{0,8},{9,1},{1,9},{10,2},{2,10},{11,3},{3,11},{12,4},{4,12},... | collective-permute-start | bytes 1966088 | tf_op jit(solution)/shard_map/ppermute | solution.py:232
  62.1 39.0 %collective-permute-start.16 = (bf16[320,1024]{1,0:T(8,128)(2,1)S(1)}, bf16[320,1024]{1,0:T(8,128)(2,1)S(1)}, u32[]{:S(2)}, u32[]{:S(2)}) collective-permute-start(bf16[320,1024]{1,0:T(8,128)(2,1)S(1)} %shard_map.117), channel_id=1, source_target_pairs={{8,0},{0,8},{9,1},{1,9},{10,2},{2,10},{11,3},{3,11},{12,4},{4,12},... | collective-permute-start | bytes 1966088 | tf_op jit(solution)/shard_map/ppermute | solution.py:232
  65.1 15.0 %collective-permute-start.10 = (bf16[160,2048]{1,0:T(8,128)(2,1)S(1)}, bf16[160,2048]{1,0:T(8,128)(2,1)S(1)}, u32[]{:S(2)}, u32[]{:S(2)}) collective-permute-start(bf16[160,2048]{1,0:T(8,128)(2,1)S(1)} %get-tuple-element.55), channel_id=1, source_target_pairs={{16,0},{0,16},{17,1},{1,17},{18,2},{2,18},{19,3},{3,19},{20,4},{4,... | collective-permute-start | bytes 1966088 | tf_op jit(solution)/shard_map/ppermute | solution.py:232
  66.0 55.7 %collective-permute-start.9 = (bf16[320,2048]{1,0:T(8,128)(2,1)S(1)}, bf16[320,2048]{1,0:T(8,128)(2,1)}, u32[]{:S(2)}, u32[]{:S(2)}) collective-permute-start(bf16[320,2048]{1,0:T(8,128)(2,1)S(1)} %pad_maximum_fusion.5), channel_id=1, source_target_pairs={{1,0},{0,1},{3,2},{2,3},{5,4},{4,5},{7,6},{6,7},{9,8},{8,9},{11,10... | collective-permute-start | bytes 3932168 | tf_op jit(solution)/shard_map/ppermute | solution.py:229
  80.1 28.9 %collective-permute-start.6 = (bf16[160,2048]{1,0:T(8,128)(2,1)S(1)}, bf16[160,2048]{1,0:T(8,128)(2,1)S(1)}, u32[]{:S(2)}, u32[]{:S(2)}) collective-permute-start(bf16[160,2048]{1,0:T(8,128)(2,1)S(1)} %get-tuple-element.56), channel_id=1, source_target_pairs={{16,0},{0,16},{17,1},{1,17},{18,2},{2,18},{19,3},{3,19},{20,4},{4,... | collective-permute-start | bytes 1966088 | tf_op jit(solution)/shard_map/ppermute | solution.py:232
  81.9 41.3 %collective-permute-start.11 = (bf16[320,2048]{1,0:T(8,128)(2,1)}, bf16[320,2048]{1,0:T(8,128)(2,1)}, u32[]{:S(2)}, u32[]{:S(2)}) collective-permute-start(bf16[320,2048]{1,0:T(8,128)(2,1)} %pad_maximum_fusion.6), channel_id=1, source_target_pairs={{1,0},{0,1},{3,2},{2,3},{5,4},{4,5},{7,6},{6,7},{9,8},{8,9},{11,10... | collective-permute-start | bytes 3932168 | tf_op jit(solution)/shard_map/ppermute | solution.py:229
  87.6 83.2 %collective-permute-start.15 = (bf16[320,1024]{1,0:T(8,128)(2,1)S(1)}, bf16[320,1024]{1,0:T(8,128)(2,1)S(1)}, u32[]{:S(2)}, u32[]{:S(2)}) collective-permute-start(bf16[320,1024]{1,0:T(8,128)(2,1)S(1)} %shard_map.115), channel_id=1, source_target_pairs={{8,0},{0,8},{9,1},{1,9},{10,2},{2,10},{11,3},{3,11},{12,4},{4,12},... | collective-permute-start | bytes 1966088 | tf_op jit(solution)/shard_map/ppermute | solution.py:232
  101.1 13.9 %collective-permute-start.19 = (bf16[320,1024]{1,0:T(8,128)(2,1)}, bf16[320,1024]{1,0:T(8,128)(2,1)S(1)}, u32[]{:S(2)}, u32[]{:S(2)}) collective-permute-start(bf16[320,1024]{1,0:T(8,128)(2,1)} %convert_element_type.42), channel_id=1, source_target_pairs={{0,2},{1,3},{8,10},{9,11},{16,18},{17,19},{24,26},{25,27}} | collective-permute-start | bytes 1966088 | tf_op jit(solution)/shard_map/ppermute | solution.py:223
  109.0 6.0 %collective-permute-start.22 = (bf16[320,1024]{1,0:T(8,128)(2,1)}, bf16[320,1024]{1,0:T(8,128)(2,1)S(1)}, u32[]{:S(2)}, u32[]{:S(2)}) collective-permute-start(bf16[320,1024]{1,0:T(8,128)(2,1)} %convert_element_type.42), channel_id=1, source_target_pairs={{6,4},{7,5},{14,12},{15,13},{22,20},{23,21},{30,28},{31,29}} | collective-permute-start | bytes 1966088 | tf_op jit(solution)/shard_map/ppermute | solution.py:223
  115.1 11.3 %collective-permute-start.7 = (bf16[320,2048]{1,0:T(8,128)(2,1)S(1)}, bf16[320,2048]{1,0:T(8,128)(2,1)S(1)}, u32[]{:S(2)}, u32[]{:S(2)}) collective-permute-start(bf16[320,2048]{1,0:T(8,128)(2,1)S(1)} %pad_maximum_fusion.4), channel_id=1, source_target_pairs={{1,0},{0,1},{3,2},{2,3},{5,4},{4,5},{7,6},{6,7},{9,8},{8,9},{11,10... | collective-permute-start | bytes 3932168 | tf_op jit(solution)/shard_map/ppermute | solution.py:229
  116.6 21.4 %collective-permute-start.20 = (bf16[320,1024]{1,0:T(8,128)(2,1)}, bf16[320,1024]{1,0:T(8,128)(2,1)}, u32[]{:S(2)}, u32[]{:S(2)}) collective-permute-start(bf16[320,1024]{1,0:T(8,128)(2,1)} %get-tuple-element.51), channel_id=1, source_target_pairs={{0,2},{1,3},{2,4},{3,5},{8,10},{9,11},{10,12},{11,13},{16,18},{17,... | collective-permute-start | bytes 1966088 | tf_op jit(solution)/shard_map/ppermute | solution.py:223
  121.7 16.3 %collective-permute-start.23 = (bf16[320,1024]{1,0:T(8,128)(2,1)}, bf16[320,1024]{1,0:T(8,128)(2,1)}, u32[]{:S(2)}, u32[]{:S(2)}) collective-permute-start(bf16[320,1024]{1,0:T(8,128)(2,1)} %get-tuple-element.52), channel_id=1, source_target_pairs={{4,2},{5,3},{6,4},{7,5},{12,10},{13,11},{14,12},{15,13},{20,18},{2... | collective-permute-start | bytes 1966088 | tf_op jit(solution)/shard_map/ppermute | solution.py:223
  137.7 12.4 %collective-permute-start.25 = (f32[2,4608]{1,0:T(2,128)S(1)}, f32[2,4608]{1,0:T(2,128)S(1)}, u32[]{:S(2)}, u32[]{:S(2)}) collective-permute-start(f32[2,4608]{1,0:T(2,128)S(1)} %pad_maximum_fusion.7), channel_id=1, source_target_pairs={{0,1},{1,0},{2,3},{3,2},{4,5},{5,4},{6,7},{7,6},{8,9},{9,8},{10,11... | collective-permute-start | bytes 110600 | tf_op jit(solution)/shard_map/ppermute | solution.py:302
  139.8 35.6 %collective-permute-start.21 = (bf16[320,1024]{1,0:T(8,128)(2,1)S(1)}, bf16[320,1024]{1,0:T(8,128)(2,1)S(1)}, u32[]{:S(2)}, u32[]{:S(2)}) collective-permute-start(bf16[320,1024]{1,0:T(8,128)(2,1)S(1)} %get-tuple-element.41), channel_id=1, source_target_pairs={{0,2},{1,3},{2,4},{3,5},{4,6},{5,7},{8,10},{9,11},{10,12},{11,13},... | collective-permute-start | bytes 1966088 | tf_op jit(solution)/shard_map/ppermute | solution.py:223
  148.8 26.6 %collective-permute-start.24 = (bf16[320,1024]{1,0:T(8,128)(2,1)S(1)}, bf16[320,1024]{1,0:T(8,128)(2,1)S(1)}, u32[]{:S(2)}, u32[]{:S(2)}) collective-permute-start(bf16[320,1024]{1,0:T(8,128)(2,1)S(1)} %get-tuple-element.42), channel_id=1, source_target_pairs={{2,0},{3,1},{4,2},{5,3},{6,4},{7,5},{10,8},{11,9},{12,10},{13,11},... | collective-permute-start | bytes 1966088 | tf_op jit(solution)/shard_map/ppermute | solution.py:223
  150.2 19.0 %collective-permute-start.26 = (f32[2,4608]{1,0:T(2,128)S(1)}, f32[2,4608]{1,0:T(2,128)S(1)}, u32[]{:S(2)}, u32[]{:S(2)}) collective-permute-start(f32[2,4608]{1,0:T(2,128)S(1)} %fusion), channel_id=1, source_target_pairs={{0,2},{1,3},{2,0},{3,1},{4,6},{5,7},{6,4},{7,5},{8,10},{9,11},{10,... | collective-permute-start | bytes 110600 | tf_op jit(solution)/shard_map/ppermute | solution.py:302
  169.2 4.9 %collective-permute-start.27 = (f32[2,4608]{1,0:T(2,128)S(1)}, f32[2,4608]{1,0:T(2,128)S(1)}, u32[]{:S(2)}, u32[]{:S(2)}) collective-permute-start(f32[2,4608]{1,0:T(2,128)S(1)} %add.122), channel_id=1, source_target_pairs={{0,4},{1,5},{2,6},{3,7},{4,0},{5,1},{6,2},{7,3},{8,12},{9,13},{10,... | collective-permute-start | bytes 110600 | tf_op jit(solution)/shard_map/ppermute | solution.py:302
  (7 other events, 13.8 us)

commit v2 on v0

v2 whole, which is shorter than its diff:
```python
import functools
import math

import jax
import jax.numpy as jnp
from jax import lax
from jax.experimental import pallas as pl
from jax.experimental.pallas import tpu as pltpu
from jax.sharding import PartitionSpec as P

F32 = jnp.float32
BF16 = jnp.bfloat16
VMEM_BYTES = 60 * 1024 * 1024
ROOT_2_PI = math.sqrt(2.0 / math.pi)
CUBIC = 0.044715
SHORT = pl.CostEstimate(flops=1, bytes_accessed=1, transcendentals=0)


def tanh_of(x):
    return jnp.tanh(ROOT_2_PI * (x + CUBIC * (x * x * x)))


def pick_rows(slot, scale):
    rows = jnp.zeros((slot.shape[0], scale.shape[1]), F32)
    for k in range(scale.shape[0]):
        rows = jnp.where(slot == k, scale[k : k + 1, :], rows)
    return rows


def prepare_kernel(nh, gate_ref, up_ref, in_scale_ref, grad_ref, out_scale_ref, slot_ref, *outs):
    slot = slot_ref[...]
    gate = gate_ref[...].astype(F32)
    gelu = gate * (0.5 * (1.0 + tanh_of(gate)))
    act = gelu * up_ref[...].astype(F32)
    turned = (act * pick_rows(slot, in_scale_ref[...])).T.astype(BF16)
    shard = outs[0].shape[1] // nh
    for i in range(nh):
        for p in range(2):
            first = (2 * i + p) * shard
            outs[p][0, i * shard : (i + 1) * shard, :] = turned[first : first + shard]
    scaled = (grad_ref[...].astype(F32) * pick_rows(slot, out_scale_ref[...])).astype(BF16)
    half = scaled.shape[0] // 2
    outs[2][...] = scaled[:half]
    outs[3][...] = scaled[half:]


def prepare(gate, up, in_scale, out_grad, out_scale, slot, blocks, nh):
    tokens, ff = gate.shape
    d = out_grad.shape[1]
    width, columns = ff // blocks, d // blocks
    mem = in_scale.shape[0]
    spec = lambda shape: pl.BlockSpec(shape, lambda i: (0, i))
    turned = jax.ShapeDtypeStruct((blocks, width // 2, tokens), BF16)
    scaled = jax.ShapeDtypeStruct((tokens // 2, d), BF16)
    return pl.pallas_call(
        functools.partial(prepare_kernel, nh),
        out_shape=[turned, turned, scaled, scaled],
        grid=(blocks,),
        in_specs=[
            spec((tokens, width)),
            spec((tokens, width)),
            spec((mem, width)),
            spec((tokens, columns)),
            spec((mem, columns)),
            pl.BlockSpec((tokens, 1), lambda i: (0, 0)),
        ],
        out_specs=[pl.BlockSpec((1, width // 2, tokens), lambda i: (i, 0, 0))] * 2
        + [spec((tokens // 2, columns))] * 2,
        compiler_params=pltpu.CompilerParams(vmem_limit_bytes=VMEM_BYTES),
        cost_estimate=SHORT,
    )(gate, up, in_scale, out_grad, out_scale, slot)


def partials_kernel(lo, items, n_columns, own_at, ids_ref, *refs):
    lefts, refs = [refs[2 * i : 2 * i + 2] for i in range(lo)], refs[2 * lo :]
    if own_at is not None:
        owns, refs = [refs[2 * i : 2 * i + 2] for i in range(lo)], refs[2 * lo :]
    rights = []
    for _ in range(n_columns):
        rights.append(jnp.concatenate([r[...] for r in refs[: 2 * lo]], axis=0))
        refs = refs[2 * lo :]
    single = lefts[0][0].shape[0] == 1
    for (row, column, _), out in zip(items, refs):
        if row is None:
            odd = ids_ref[own_at] == 1
            left = jnp.concatenate([jnp.where(odd, b[0], a[0]) for a, b in owns], axis=1)
            total = jnp.dot(left, rights[column], preferred_element_type=F32)
            out[...] = total.astype(out.dtype)
            continue
        block = 0 if single else ids_ref[row]
        shard = lefts[0][0].shape[1]
        for p in range(2):
            left = jnp.concatenate([pair[p][block] for pair in lefts], axis=1)
            total = jnp.dot(left, rights[column], preferred_element_type=F32)
            out[p * shard : (p + 1) * shard, :] = total.astype(out.dtype)


def partials(ids, at, items, column_at, lefts, rights, members):
    lo = len(lefts)
    line, part, tokens = lefts[0][0].shape
    shard = part // (lo // 2)
    width = rights[0][0].shape[1] // members
    tile = max(width // 4, 128)
    tiles = width // tile
    single = len({row for row, _, _ in items}) == 1
    if single:
        row = items[0][0]
        left_spec = pl.BlockSpec((1, shard, tokens), lambda i, ids: (ids[row], ids[at["half"]], 0))
    else:
        left_spec = pl.BlockSpec((line, shard, tokens), lambda i, ids: (0, ids[at["half"]], 0))
    flat = [x for pair in lefts for x in pair]
    ins, specs = list(flat), [left_spec] * len(flat)
    own_at = None
    if any(row is None for row, _, _ in items):
        own_at = at["odd"]
        ins += flat
        specs += [
            pl.BlockSpec((1, shard, tokens), lambda i, ids: (ids[at["z"]], ids[at["own"]], 0))
        ] * len(flat)
    for where in column_at:
        ins += [x for pair in rights for x in pair]
        specs += [
            pl.BlockSpec((tokens // 2, tile), lambda i, ids, w=where: (0, ids[w] * tiles + i))
        ] * (2 * lo)
    shapes = [
        jax.ShapeDtypeStruct((shard if row is None else 2 * shard, width), dtype)
        for row, _, dtype in items
    ]
    return pl.pallas_call(
        functools.partial(partials_kernel, lo, items, len(column_at), own_at),
        out_shape=shapes,
        grid_spec=pltpu.PrefetchScalarGridSpec(
            num_scalar_prefetch=1,
            grid=(tiles,),
            in_specs=specs,
            out_specs=[pl.BlockSpec((s.shape[0], tile), lambda i, ids: (0, i)) for s in shapes],
        ),
        compiler_params=pltpu.CompilerParams(vmem_limit_bytes=VMEM_BYTES),
        cost_estimate=SHORT,
    )(ids, *ins)


def slot_kernel(n_pieces, kept, base, ids_ref, *refs):
    pieces, refs = refs[:n_pieces], refs[n_pieces:]
    scaled_refs, refs = refs[:2], refs[2:]
    out_grad_ref, gate_ref, up_ref, in_scale_ref, slot_ref = refs[:5]
    refs = refs[5:]
    if kept:
        before_ref, refs = refs[3], refs[4:]
    grad_gate_ref, grad_up_ref, sum_in_ref, sum_out_ref, weight_ref, sems = refs
    shard = pieces[0].shape[0]

    def copy_of(p):
        start = pl.multiple_of(jnp.maximum(ids_ref[base + 1 + p], 0) * shard, shard)
        return pltpu.make_async_copy(pieces[p], weight_ref.at[pl.ds(start, shard)], sems.at[p])

    for p in range(n_pieces):

        @pl.when(ids_ref[base + 1 + p] >= 0)
        def _():
            copy_of(p).start()

    slot = slot_ref[...]
    gate = gate_ref[...].astype(F32)
    up = up_ref[...].astype(F32)
    tanh = tanh_of(gate)
    cdf = 0.5 * (1.0 + tanh)
    slope = cdf + gate * (0.5 * ROOT_2_PI) * (1.0 - tanh * tanh) * (
        1.0 + (3.0 * CUBIC) * (gate * gate)
    )
    gelu = gate * cdf
    act = gelu * up
    row_in = pick_rows(slot, in_scale_ref[...])
    hidden = (act * row_in).astype(BF16)

    for p in range(n_pieces):

        @pl.when(ids_ref[base + 1 + p] >= 0)
        def _():
            copy_of(p).wait()

    weight = weight_ref[...]
    scaled = jnp.concatenate([r[...] for r in scaled_refs], axis=0)
    grad_hidden = lax.dot_general(
        scaled, weight, (((1,), (1,)), ((), ())), preferred_element_type=F32
    )
    grad_act = grad_hidden * row_in
    grad_gate_ref[...] = (grad_act * up * slope).astype(BF16)
    grad_up_ref[...] = (grad_act * gelu).astype(BF16)
    product = grad_hidden * act
    forward = jnp.dot(hidden, weight, preferred_element_type=F32)
    forward = forward * out_grad_ref[...].astype(F32)
    for k in range(in_scale_ref.shape[0]):
        mine = slot == k
        row = slice(k, k + 1)
        sum_in_ref[row, :] = jnp.sum(jnp.where(mine, product, 0.0), axis=0, keepdims=True)
        more = jnp.sum(jnp.where(mine, forward, 0.0), axis=0, keepdims=True)
        sum_out_ref[row, :] = before_ref[row, :] + more if kept else more


def weight_slot(ids, base, pieces, width, scaled, out_grad, gate, up, in_scale, slot, kept):
    tokens, ff = gate.shape
    d = out_grad.shape[1]
    mem = in_scale.shape[0]
    column = lambda rows: pl.BlockSpec((rows, width), lambda i, ids: (0, ids[base]))
    full = lambda shape: pl.BlockSpec(shape, lambda i, ids: (0, 0))
    anywhere = pl.BlockSpec(memory_space=pl.ANY)
    ins = list(pieces) + list(scaled) + [out_grad, gate, up, in_scale, slot]
    specs = [anywhere] * len(pieces) + [full((tokens // 2, d))] * 2
    specs += [full((tokens, d)), column(tokens), column(tokens), column(mem), full((tokens, 1))]
    aliases = {}
    if kept is not None:
        aliases = {1 + len(ins) + i: i for i in range(3)}
        ins += list(kept)
        specs += [anywhere] * 3 + [full((mem, d))]
    return pl.pallas_call(
        functools.partial(slot_kernel, len(pieces), kept is not None, base),
        out_shape=[
            jax.ShapeDtypeStruct((tokens, ff), BF16),
            jax.ShapeDtypeStruct((tokens, ff), BF16),
            jax.ShapeDtypeStruct((mem, ff), F32),
            jax.ShapeDtypeStruct((mem, d), F32),
        ],
        grid_spec=pltpu.PrefetchScalarGridSpec(
            num_scalar_prefetch=1,
            grid=(1,),
            in_specs=specs,
            out_specs=[column(tokens), column(tokens), column(mem), full((mem, d))],
            scratch_shapes=[
                pltpu.VMEM((width, d), BF16),
                pltpu.SemaphoreType.DMA((len(pieces),)),
            ],
        ),
        input_output_aliases=aliases,
        compiler_params=pltpu.CompilerParams(vmem_limit_bytes=VMEM_BYTES),
        cost_estimate=SHORT,
    )(ids, *ins)


def on_device(groups, members, fsdp):
    def run(gate, up, out_grad, in_scale, out_scale, weight, member_slot):
        tokens, ff = gate.shape
        shard = weight.shape[0]
        columns = out_grad.shape[1] // members
        lo = max(128 // math.gcd(shard, 128), 2)
        line, nh = fsdp // lo, lo // 2
        assert groups == 2 and line * lo == fsdp and line > 1
        width = lo * shard
        group = lax.axis_index("groups")
        member = lax.axis_index("member")
        place_id = lax.axis_index("fsdp")
        z, core = place_id // lo, lax.rem(place_id, lo)
        lower, rising = z < line // 2, core < nh
        slot = member_slot[:, None]
        last = [slot]
        chips = range(line)
        halves = range(nh)

        def after(x):
            return lax.optimization_barrier((x, last[-1]))[0]

        def mark(x):
            last.append(x[0] if isinstance(x, (list, tuple)) else x)
            return x

        def dev(zz, c, outer=0):
            return (outer * line + zz) * lo + c

        def line_step(x, rises, falls):
            pairs = [(dev(a, i), dev(a + 1, i)) for a in rises for i in halves]
            pairs += [(dev(a, nh + i), dev(a - 1, nh + i)) for a in falls for i in halves]
            return lax.ppermute(x, "fsdp", pairs)

        def to_chip(x, sources, o):
            return lax.ppermute(
                x, "fsdp", [(dev(a, c), dev(a, (c + o) % lo)) for a in chips for c in sources(a)]
            )

        every = lambda a: range(lo)

        arrived, mine, twin = [None] * line, [None] * line, [None] * line
        mine_in, twin_in = [None] * line, [None] * line

        def weight_first():
            pairs = []
            for g in range(2):
                for a in chips:
                    for i in halves:
                        if a + 1 < line:
                            pairs.append((dev(a, g * nh + i, g), dev(a + 1, i, g)))
                        if a > 0:
                            pairs.append((dev(a, (1 - g) * nh + i, g), dev(a - 1, nh + i, g)))
            arrived[1] = lax.ppermute(weight, ("groups", "fsdp"), pairs)

        def weight_next(s):
            arrived[s] = line_step(
                after(arrived[s - 1]), range(s - 1, line - 1), range(1, line - s + 1)
            )

        def falls(a, j):
            return a + j < line if a < line // 2 else a < j

        def fell(j):
            table = [int(falls(a, j)) for a in chips]
            flag = jnp.int32(table[-1])
            for a in range(line - 1):
                flag = jnp.where(z == a, table[a], flag)
            return flag

        def holders(j):
            return lambda a: [nh * falls(a, j) + i for i in halves]

        def weight_mine(j):
            block = after(arrived[j])
            if 2 * j > line:
                straight = jnp.where(lower, z + j < line, z >= j)
                block = mark(jnp.where(straight, block, arrived[line - j]))
            mine[j] = block
            pairs = [
                (dev(a, h, g), dev(a, h, 1 - g))
                for g in range(2)
                for a in chips
                for h in holders(j)(a)
            ]
            twin[j] = lax.ppermute(block, ("groups", "fsdp"), pairs)

        def spread_mine(j):
            mine_in[j] = [to_chip(after(mine[j]), holders(j), o) for o in range(1, lo)]

        def spread_twin(j):
            twin_in[j] = [to_chip(after(twin[j]), holders(j), o) for o in range(1, lo)]

        numbers, at = [], {}

        def number(name, value):
            at[name] = len(numbers)
            numbers.append(jnp.asarray(value, jnp.int32))

        number("z", z)
        number("half", lax.rem(core, nh) if nh > 1 else 0)
        number("own", core // 2)
        number("odd", lax.rem(core, 2))
        for j in range(members):
            number(("to", j), lax.rem(member + members - j, members))
        for k in range(1, line):
            number(("send", k), lax.rem(jnp.where(lower, z - k, z + k) + line, line))
            onward = jnp.where(rising, z + line - k, z - line + k)
            number(("keep", k), jnp.clip(onward, 0, line - 1))
        source = [lax.rem(core + lo - o, lo) for o in range(lo)]
        for j in range(line):
            number(("slot", j), lax.rem(jnp.where(lower, z + j, z - j) + line, line))
            if j == 0:
                places = source
            else:
                down = fell(j)
                held = [(h // nh) == down for h in source]
                first = jnp.where(down == 1, 1 - group, group)
                places = [jnp.where(ok, first * nh + h % nh, -1) for ok, h in zip(held, source)]
                places += [
                    jnp.where(ok, (1 - first) * nh + h % nh, -1) for ok, h in zip(held, source)
                ]
            for p, value in enumerate(places):
                number(("piece", j, p), value)
        ids = jnp.stack(numbers)

        kept = [None]

        def use_weight(j):
            if j == 0:
                pieces = [weight] + own_in
            else:
                pieces = [mine[j]] + mine_in[j] + [twin[j]] + twin_in[j]
            kept[0] = mark(
                weight_slot(
                    ids,
                    at[("slot", j)],
                    after(pieces),
                    width,
                    scaled,
                    out_grad,
                    gate,
                    up,
                    in_scale,
                    slot,
                    kept[0],
                )
            )

        weight_first()
        made = mark(prepare(gate, up, in_scale, out_grad, out_scale, slot, line, nh))
        turned, scaled = list(made[:2]), list(made[2:])
        lefts, rights = [turned], [scaled]
        for o in range(1, lo):
            rights.append([to_chip(x, every, o) for x in scaled])
            lefts.append([to_chip(x, every, o) for x in turned])

        got = [None] * line

        def works(a, c, k):
            if k == 0:
                return True
            if a < line // 2:
                return (c < nh) == (k > a)
            return (c >= nh) == (k > line - 1 - a)

        def exchange(k, blocks):
            got[k] = []
            for j in range(1, members):
                pairs = [
                    (dev(a, c, (m + j) % members), dev(a, c, m))
                    for m in range(members)
                    for a in chips
                    for c in range(lo)
                    if works(a, c, k)
                ]
                got[k].append(lax.ppermute(blocks[j - 1], ("member", "fsdp"), pairs))

        others = [at[("to", j)] for j in range(1, members)]
        items = [(at[("send", 1)], j, BF16) for j in range(members - 1)]
        mark(arrived[1])
        made = partials(after(ids), at, items, others, lefts, rights, members)
        mark(made)
        exchange(1, made)
        if line > 2:
            weight_next(2)
        weight_mine(1)
        spread_mine(1)
        own_in = [to_chip(after(weight), every, o) for o in range(1, lo)]
        order = list(range(2, line)) + [0]
        items = []
        for k in order:
            row = at[("send", k)] if k else None
            items += [(row, j, BF16) for j in range(1, members)]
        for k in order:
            row = at[("keep", k)] if k else None
            items.append((row, 0, BF16 if k else F32))
        items.append((at[("keep", 1)], 0, BF16))
        made = mark(
            partials(ids, at, items, [at[("to", 0)]] + others, after(lefts), rights, members)
        )
        to_send = {
            k: made[n * (members - 1) : (n + 1) * (members - 1)] for n, k in enumerate(order)
        }
        sums = dict(zip(order + [1], made[len(order) * (members - 1) :]))

        coming = []

        def line_both(s):
            total = sums[s].astype(F32)
            for one, two in zip(after(got[s]), got[line - s] or got[s]):
                if 2 * s > line:
                    one = jnp.where(rising != lower, two, one)
                total = total + one.astype(F32)
            for x in coming:
                total = total + jnp.concatenate([x[:, :columns], x[:, columns:]]).astype(F32)
            total = total.astype(BF16)
            total = jnp.concatenate([total[:shard], total[shard:]], axis=1)
            rises = [a for a in range(s)]
            falls = [a for a in range(line - s, line)]
            if s + 2 < line and total.shape == weight.shape:
                hop = jnp.where(rising, z > s, z < line - 1 - s)
                total = mark(jnp.where(hop, after(arrived[s + 1]), total))
                rises += range(s + 1, line - 1)
                falls += range(1, line - 1 - s)
                arrived[s + 2] = line_step(total, rises, falls)
                coming[:] = [arrived[s + 2]]
                return
            if s + 2 < line:
                weight_next(s + 2)
            coming[:] = [line_step(mark(total), rises, falls)]

        for s in range(1, line):
            mark(after(got[s]))
            k = s + 1 if s + 1 < line else 0
            exchange(k, after(to_send[k]))
            if s + 1 < line:
                weight_mine(s + 1)
            line_both(s)
            spread_twin(s)
            use_weight(s - 1)
            if s + 1 < line:
                spread_mine(s + 1)
        mark(after(got[0]))
        use_weight(line - 1)
        both = jnp.concatenate(kept[0][2:], axis=1)
        if fsdp & (fsdp - 1):
            both = lax.psum(both, "fsdp")
        else:
            stage = 1
            while stage < fsdp:
                both = both + lax.ppermute(both, "fsdp", [(i, i ^ stage) for i in range(fsdp)])
                stage *= 2
        top, bottom = coming[0][:, :columns], coming[0][:, columns:]
        landed = []
        for part in range(2):
            pairs = [(i, 2 * i + part) for i in halves]
            pairs += [(nh + i, 2 * i + 1 - part) for i in halves]
            x = jnp.where(rising, bottom, top) if part else jnp.where(rising, top, bottom)
            if any(c != d for c, d in pairs):
                x = lax.ppermute(
                    x, "fsdp", [(dev(a, c), dev(a, d)) for a in chips for c, d in pairs]
                )
            landed.append(x)
        grad_down = sums[0]
        for x in got[0] + landed:
            grad_down = grad_down + x.astype(F32)
        return kept[0][0], kept[0][1], grad_down, both[:, :ff], both[:, ff:]

    return run


def solution(mesh):
    rows = P(("groups", "member", "fsdp"), None)
    in_specs = (
        rows,
        rows,
        rows,
        P("member", None),
        P("member", None),
        P("fsdp", None),
        P(("groups", "member", "fsdp")),
    )
    out_specs = (
        rows,
        rows,
        P(("groups", "fsdp"), "member"),
        P(("groups", "member"), None),
        P(("groups", "member"), None),
    )
    run = on_device(mesh.shape["groups"], mesh.shape["member"], mesh.shape["fsdp"])
    return jax.shard_map(run, mesh=mesh, in_specs=in_specs, out_specs=out_specs, check_vma=False)
```

time: 393 us -> 162 us (0.41)
  waiting for transfers between devices: 304 us -> 21.1 us
  starting transfers between devices: 0.3 us -> 57.8 us
  Pallas kernels: 0 us -> 57.2 us
  matrix products: 45.6 us -> 0 us
  blocking collectives: 26.9 us -> 0 us
  other arithmetic: 0 us -> 13.6 us
  between operations: 13.8 us -> 0.99 us
  local copies, waits for them, and re-layouts: 2.43 us -> 9.93 us
    reduce_scatter x2 -> x0, waiting for transfers between devices: 206 us -> none  [the longest x1 206 us: on_device(): lax.psum_scatter(lax.dot_general(hidden, scaled, (((0,), (0,)), ((), ()))...]
    all_gather x1 -> x0, waiting for transfers between devices: 97.2 us -> none  [on_device(): whole_weight = lax.all_gather(down_weight, 'fsdp', axis=0, tiled=True)]
    ppermute x0 -> x27, starting transfers between devices: none -> 57.8 us  [the longest x4 22 us: line_step(): return lax.ppermute(x, 'fsdp', pairs)]
    pallas_call x0 -> x7, Pallas kernels: none -> 57.2 us  [the longest x4 32.8 us: weight_slot(): pl.pallas_call(functools.partial(slot_kernel, len(pieces), kept is not No...]
    dot_general x7 -> x0, matrix products: 45.6 us -> none  [the longest x1 17.6 us: on_device(): lax.dot_general(scaled, whole_weight, (((1,), (1,)), ((), ())), preferred...]
    psum x1 -> x0, blocking collectives: 26.9 us -> none  [on_device(): grad_in_scale, grad_out_scale = lax.psum((local_in, local_out), 'fsdp')]
    ppermute x0 -> x27, waiting for transfers between devices: none -> 21.1 us  [the longest x4 9.16 us: line_step(): return lax.ppermute(x, 'fsdp', pairs)]
    convert_element_type x0 -> x3, other arithmetic: none -> 6.54 us  [line_both(): total = total.astype(BF16)]
  transfers between devices with their start and end apart: 3 -> 27, of which waited for: 2 -> 9; matrix products, arithmetic and copies ran while one was open for 5% -> 11% of each run, Pallas kernels for 0% -> 32%
where the time goes in v2:
time: 162 us; the launch traced here: 161 us
  starting transfers between devices  57.8 us (36%)
  Pallas kernels  57.2 us (35%)
  waiting for transfers between devices  21.1 us (13%)
  other arithmetic  13.6 us (8%)
  local copies, waits for them, and re-layouts  9.93 us (6%)
    pallas_call x4, Pallas kernels, weight_slot(): pl.pallas_call(functools.partial(slot_kernel, len(pieces), kept is not No...  32.8 us
    ppermute x4, starting transfers between devices, line_step(): return lax.ppermute(x, 'fsdp', pairs)  22 us
    pallas_call x2, Pallas kernels, partials(): pl.pallas_call(functools.partial(partials_kernel, lo, items, len(column_a...  17.6 us
    ppermute x4, starting transfers between devices, exchange(): got[k].append(lax.ppermute(blocks[j - 1], ('member', 'fsdp'), pairs))  10.8 us
    ppermute x4, waiting for transfers between devices, line_step(): return lax.ppermute(x, 'fsdp', pairs)  9.16 us
    ppermute x11, starting transfers between devices, to_chip(): lax.ppermute(x, 'fsdp', [(dev(a, c), dev(a, (c + o) % lo)) for a in chips...  9.1 us
    pallas_call x1, Pallas kernels, prepare(): pl.pallas_call(functools.partial(prepare_kernel, nh), out_shape=[turned,...  6.81 us
    convert_element_type x3, other arithmetic, line_both(): total = total.astype(BF16)  6.54 us
  transfers between devices with their start and end apart: 27, of which 9 were waited for; matrix products, arithmetic and copies ran while one was open for 11% of the time, Pallas kernels for 32%

profile of v2, /device:TPU:0, one launch (start us, length us, event | category | flops | bytes accessed | tf_op | source)
XLA Modules:
  0.0 160.5 jit_solution(34537751254164053)
XLA Ops:
  0.6 6.0 %collective-permute-start = (bf16[320,2048]{1,0:T(8,128)(2,1)}, bf16[320,2048]{1,0:T(8,128)(2,1)}, u32[]{:S(2)}, u32[]{:S(2)}) collective-permute-start(bf16[320,2048]{1,0:T(8,128)(2,1)} %refs_0_), channel_id=1, source_target_pairs={{0,2},{2,4},{3,1},{4,6},{5,3},{7,5},{17,18},{19,20},{18,17},{21,22... | collective-permute-start | bytes 3932168 | tf_op jit(solution)/shard_map/ppermute | solution.py:293
  6.7 1.5 broadcast_in_dim.4.slot_ref.refs_8_.refs_10_
  8.1 6.8 %shard_map.110 = (bf16[4,320,384]{2,1,0:T(8,128)(2,1)}, bf16[4,320,384]{2,1,0:T(8,128)(2,1)}, bf16[192,2048]{1,0:T(8,128)(2,1)}, bf16[192,2048]{1,0:T(8,128)(2,1)}) custom-call(bf16[384,2560]{1,0:T(8,128)(2,1)} %refs_7_.7, bf16[384,2560]{1,0:T(8,128)(2,1)} %refs_8_.5, f32[2,2560]{1,0:T(2,128)} %refs_9_.5, bf16[384,2048]{1,0:T(8,128)(2,1)} %refs_6_.7, ...), custom_call_target="tpu_custom_call" | custom-call | flops 1 | bytes 1 | tf_op jit(solution)/shard_map/pallas_call | solution.py:55
  16.6 4.4 %collective-permute-done.refs_0_ = bf16[320,2048]{1,0:T(8,128)(2,1)} collective-permute-done((bf16[320,2048]{1,0:T(8,128)(2,1)}, bf16[320,2048]{1,0:T(8,128)(2,1)}, u32[]{:S(2)}, u32[]{:S(2)}) %collective-permute-start) | collective-permute-done | bytes 1310752 | tf_op jit(solution)/shard_map/ppermute | solution.py:293
  23.6 5.5 %shard_map.111 = bf16[640,1024]{1,0:T(8,128)(2,1)} custom-call(s32[30]{0:T(128)} %stack.107.ids_ref, bf16[4,320,384]{2,1,0:T(8,128)(2,1)} %get-tuple-element.76.refs_0_.refs_4_, bf16[4,320,384]{2,1,0:T(8,128)(2,1)} %get-tuple-element.77.refs_1_.refs_5_, bf16[4,320,384]{2,1,0:T(8,128)(2,1)} %copy-done, bf16[4,320,384]{2,1,0:T(8,128)(2,1)} %copy-done.1, ...), custom_call_target="tpu_custom_call" | custom-call | flops 1 | bytes 1 | tf_op jit(solution)/shard_map/pallas_call | solution.py:129
  29.1 3.4 %collective-permute-start.6 = (bf16[640,1024]{1,0:T(8,128)(2,1)}, bf16[640,1024]{1,0:T(8,128)(2,1)S(1)}, u32[]{:S(2)}, u32[]{:S(2)}) collective-permute-start(bf16[640,1024]{1,0:T(8,128)(2,1)} %shard_map.111), channel_id=1, source_target_pairs={{8,0},{11,3},{12,4},{15,7},{0,8},{3,11},{4,12},{7,15},{24,16},{27,... | collective-permute-start | bytes 3932168 | tf_op jit(solution)/shard_map/ppermute | solution.py:416
  32.5 1.7 %collective-permute-start.5 = (bf16[320,2048]{1,0:T(8,128)(2,1)}, bf16[320,2048]{1,0:T(8,128)(2,1)}, u32[]{:S(2)}, u32[]{:S(2)}) collective-permute-start(bf16[320,2048]{1,0:T(8,128)(2,1)} %collective-permute-done.refs_0_), channel_id=1, source_target_pairs={{2,4},{4,6},{3,1},{5,3},{10,12},{12,14},{11,9},{13,11},{18,20},{20... | collective-permute-start | bytes 3932168 | tf_op jit(solution)/shard_map/ppermute | solution.py:272
  34.3 1.8 %collective-permute-start.11 = (bf16[320,2048]{1,0:T(8,128)(2,1)}, bf16[320,2048]{1,0:T(8,128)(2,1)}, u32[]{:S(2)}, u32[]{:S(2)}) collective-permute-start(bf16[320,2048]{1,0:T(8,128)(2,1)} %collective-permute-done.refs_0_), channel_id=1, source_target_pairs={{1,17},{3,19},{4,20},{6,22},{17,1},{19,3},{20,4},{22,6},{9,25},{11... | collective-permute-start | bytes 3932168 | tf_op jit(solution)/shard_map/ppermute | solution.py:325
  36.0 12.1 %shard_map.112 = (bf16[640,1024]{1,0:T(8,128)(2,1)}, bf16[640,1024]{1,0:T(8,128)(2,1)}, bf16[320,1024]{1,0:T(8,128)(2,1)}, bf16[640,1024]{1,0:T(8,128)(2,1)}, bf...) custom-call(s32[30]{0:T(128)} %stack.107.ids_ref, ...), custom_call_target="tpu_custom_call" | custom-call | flops 1 | bytes 1 | tf_op jit(solution)/shard_map/pallas_call | solution.py:129
  48.8 1.8 %add_convert_fusion.2 = bf16[640,1024]{1,0:T(8,128)(2,1)S(1)} fusion(bf16[640,1024]{1,0:T(8,128)(2,1)S(1)} %collective-permute-done.6, bf16[640,1024]{1,0:T(8,128)(2,1)} %get-tuple-element.83), kind=kLoop, calls=%fused_computation.2 | loop fusion | flops 2621440 | bytes 3932160 | tf_op jit(solution)/shard_map/convert_element_type | solution.py:456
  50.8 3.4 %collective-permute-start.8 = (bf16[640,1024]{1,0:T(8,128)(2,1)}, bf16[640,1024]{1,0:T(8,128)(2,1)}, u32[]{:S(2)}, u32[]{:S(2)}) collective-permute-start(bf16[640,1024]{1,0:T(8,128)(2,1)} %get-tuple-element.85), channel_id=1, source_target_pairs={{8,0},{10,2},{13,5},{15,7},{0,8},{2,10},{5,13},{7,15},{24,16},{26,... | collective-permute-start | bytes 3932168 | tf_op jit(solution)/shard_map/ppermute | solution.py:416
  54.2 1.6 maximum_select_fusion
  55.8 5.4 %collective-permute-start.7 = (bf16[320,2048]{1,0:T(8,128)(2,1)}, bf16[320,2048]{1,0:T(8,128)(2,1)S(1)}, u32[]{:S(2)}, u32[]{:S(2)}) collective-permute-start(bf16[320,2048]{1,0:T(8,128)(2,1)} %maximum_select_fusion), channel_id=1, source_target_pairs={{0,2},{4,6},{7,5},{3,1},{8,10},{12,14},{15,13},{11,9},{16,18},{20,... | collective-permute-start | bytes 3932168 | tf_op jit(solution)/shard_map/ppermute | solution.py:272
  62.5 1.7 %collective-permute-start.19 = (bf16[320,2048]{1,0:T(8,128)(2,1)}, bf16[320,2048]{1,0:T(8,128)(2,1)}, u32[]{:S(2)}, u32[]{:S(2)}) collective-permute-start(bf16[320,2048]{1,0:T(8,128)(2,1)} %collective-permute-done.5.refs_0_), channel_id=1, source_target_pairs={{1,17},{3,19},{4,20},{6,22},{17,1},{19,3},{20,4},{22,6},{9,25},{11... | collective-permute-start | bytes 3932168 | tf_op jit(solution)/shard_map/ppermute | solution.py:325
  65.5 8.1 %shard_map.113 = (bf16[384,2560]{1,0:T(8,128)(2,1)}, bf16[384,2560]{1,0:T(8,128)(2,1)}, f32[2,2560]{1,0:T(2,128)}, f32[2,2048]{1,0:T(2,128)}) custom-call(s32[30]{0:T(128)} %stack.107.ids_ref, bf16[320,2048]{1,0:T(8,128)(2,1)} %refs_0_, bf16[320,2048]{1,0:T(8,128)(2,1)} %collective-permute-done.9.refs_1_, ...), custom_call_target="tpu_custom_call" | custom-call | flops 1 | bytes 1 | tf_op jit(solution)/shard_map/pallas_call | solution.py:216
  73.7 2.8 %collective-permute-done.7 = bf16[320,2048]{1,0:T(8,128)(2,1)S(1)} collective-permute-done((bf16[320,2048]{1,0:T(8,128)(2,1)}, bf16[320,2048]{1,0:T(8,128)(2,1)S(1)}, u32[]{:S(2)}, u32[]{:S(2)}) %collective-permute-start.7) | collective-permute-done | bytes 1310752 | tf_op jit(solution)/shard_map/ppermute | solution.py:272
  79.0 2.2 %add_convert_fusion.1 = bf16[640,1024]{1,0:T(8,128)(2,1)S(1)} fusion(bf16[640,1024]{1,0:T(8,128)(2,1)} %collective-permute-done.8, bf16[640,1024]{1,0:T(8,128)(2,1)S(1)} %copy-done.4, bf16[320,1024]{1,0:T(8,128)(2,1)S(1)} %get-tuple-element.142, bf16[320,1024]{1,0:T(8,128)(2,1)S(1)} %get-tuple-element.141), kind=kLoop, calls=%fused_computation.1 | loop fusion | flops 5898240 | bytes 5242880 | tf_op jit(solution)/shard_map/convert_element_type | solution.py:456
  81.3 3.4 %collective-permute-start.15 = (bf16[640,1024]{1,0:T(8,128)(2,1)}, bf16[640,1024]{1,0:T(8,128)(2,1)}, u32[]{:S(2)}, u32[]{:S(2)}) collective-permute-start(bf16[640,1024]{1,0:T(8,128)(2,1)} %get-tuple-element.107), channel_id=1, source_target_pairs={{8,0},{10,2},{13,5},{15,7},{0,8},{2,10},{5,13},{7,15},{24,16},{26,... | collective-permute-start | bytes 3932168 | tf_op jit(solution)/shard_map/ppermute | solution.py:416
  85.9 6.7 %collective-permute-start.16 = (bf16[320,2048]{1,0:T(8,128)(2,1)}, bf16[320,2048]{1,0:T(8,128)(2,1)}, u32[]{:S(2)}, u32[]{:S(2)}) collective-permute-start(bf16[320,2048]{1,0:T(8,128)(2,1)} %pad_maximum_fusion), channel_id=1, source_target_pairs={{0,2},{2,4},{5,3},{7,5},{8,10},{10,12},{13,11},{15,13},{16,18},{18... | collective-permute-start | bytes 3932168 | tf_op jit(solution)/shard_map/ppermute | solution.py:272
  92.6 1.8 %collective-permute-start.14 = (bf16[320,2048]{1,0:T(8,128)(2,1)}, bf16[320,2048]{1,0:T(8,128)(2,1)}, u32[]{:S(2)}, u32[]{:S(2)}) collective-permute-start(bf16[320,2048]{1,0:T(8,128)(2,1)} %broadcast_select_fusion.refs_0_), channel_id=1, source_target_pairs={{1,17},{2,18},{5,21},{6,22},{17,1},{18,2},{21,5},{22,6},{9,25},{10... | collective-permute-start | bytes 3932168 | tf_op jit(solution)/shard_map/ppermute | solution.py:325
  94.4 1.5 collective-permute-start.18
  95.9 8.2 %shard_map.114 = (bf16[384,2560]{1,0:T(8,128)(2,1)}, bf16[384,2560]{1,0:T(8,128)(2,1)}, f32[2,2560]{1,0:T(2,128)}, f32[2,2048]{1,0:T(2,128)}) custom-call(s32[30]{0:T(128)} %stack.107.ids_ref, bf16[320,2048]{1,0:T(8,128)(2,1)} %collective-permute-done.refs_0_, ...), custom_call_target="tpu_custom_call", output_to_operand_aliasing={{0}: (12, {}), {1}: (13, {}), {2}: (14, {})} | custom-call | flops 1 | bytes 1 | tf_op jit(solution)/shard_map/pallas_call | solution.py:216
  108.3 2.5 %add_convert_fusion = bf16[640,1024]{1,0:T(8,128)(2,1)S(1)} fusion(bf16[640,1024]{1,0:T(8,128)(2,1)S(1)} %copy-done.6, bf16[320,1024]{1,0:T(8,128)(2,1)S(1)} %get-tuple-element.138, bf16[320,1024]{1,0:T(8,128)(2,1)S(1)} %get-tuple-element.137, bf16[640,1024]{1,0:T(8,128)(2,1)S(1)} %collective-permute-done.6, bf16[640,1024]{1,0:T(8,128)(2,1)} %collective-permute-done.15, ...), kind=kLoop, calls=%fused_computation | loop fusion | flops 6553600 | bytes 6553601 | tf_op jit(solution)/shard_map/convert_element_type | solution.py:456
  112.4 8.2 %collective-permute-start.22 = (bf16[320,2048]{1,0:T(8,128)(2,1)S(1)}, bf16[320,2048]{1,0:T(8,128)(2,1)S(1)}, u32[]{:S(2)}, u32[]{:S(2)}) collective-permute-start(bf16[320,2048]{1,0:T(8,128)(2,1)S(1)} %pad_maximum_fusion.1), channel_id=1, source_target_pairs={{0,2},{2,4},{4,6},{3,1},{5,3},{7,5},{8,10},{10,12},{12,14},{11,9},... | collective-permute-start | bytes 3932168 | tf_op jit(solution)/shard_map/ppermute | solution.py:272
  121.2 8.2 %shard_map.115 = (bf16[384,2560]{1,0:T(8,128)(2,1)}, bf16[384,2560]{1,0:T(8,128)(2,1)}, f32[2,2560]{1,0:T(2,128)}, f32[2,2048]{1,0:T(2,128)}) custom-call(s32[30]{0:T(128)} %stack.107.ids_ref, bf16[320,2048]{1,0:T(8,128)(2,1)} %collective-permute-done.5.refs_0_, ...), custom_call_target="tpu_custom_call", output_to_operand_aliasing={{0}: (12, {}), {1}: (13, {}), {2}: (14, {})} | custom-call | flops 1 | bytes 1 | tf_op jit(solution)/shard_map/pallas_call | solution.py:216
  129.4 6.2 %collective-permute-done.22 = bf16[320,2048]{1,0:T(8,128)(2,1)S(1)} collective-permute-done((bf16[320,2048]{1,0:T(8,128)(2,1)S(1)}, bf16[320,2048]{1,0:T(8,128)(2,1)S(1)}, u32[]{:S(2)}, u32[]{:S(2)}) %collective-permute-start.22) | collective-permute-done | bytes 1310752 | tf_op jit(solution)/shard_map/ppermute | solution.py:272
  135.7 8.3 %shard_map.116 = (bf16[384,2560]{1,0:T(8,128)(2,1)}, bf16[384,2560]{1,0:T(8,128)(2,1)}, f32[2,2560]{1,0:T(2,128)}, f32[2,2048]{1,0:T(2,128)}) custom-call(s32[30]{0:T(128)} %stack.107.ids_ref, bf16[320,2048]{1,0:T(8,128)(2,1)} %broadcast_select_fusion.refs_0_, ...), custom_call_target="tpu_custom_call", output_to_operand_aliasing={{0}: (12, {}), {1}: (13, {}), {2}: (14, {})} | custom-call | flops 1 | bytes 1 | tf_op jit(solution)/shard_map/pallas_call | solution.py:216
  146.9 2.5 %collective-permute-start.25 = (f32[2,4608]{1,0:T(2,128)S(1)}, f32[2,4608]{1,0:T(2,128)S(1)}, u32[]{:S(2)}, u32[]{:S(2)}) collective-permute-start(f32[2,4608]{1,0:T(2,128)S(1)} %add.155), channel_id=1, source_target_pairs={{0,2},{1,3},{2,0},{3,1},{4,6},{5,7},{6,4},{7,5},{8,10},{9,11},{10,... | collective-permute-start | bytes 110600 | tf_op jit(solution)/shard_map/ppermute | solution.py:491
  149.4 2.0 %collective-permute-done.25 = f32[2,4608]{1,0:T(2,128)S(1)} collective-permute-done((f32[2,4608]{1,0:T(2,128)S(1)}, f32[2,4608]{1,0:T(2,128)S(1)}, u32[]{:S(2)}, u32[]{:S(2)}) %collective-permute-start.25) | collective-permute-done | bytes 36896 | tf_op jit(solution)/shard_map/ppermute | solution.py:491
  151.4 1.5 collective-permute-start.26
  152.9 3.5 %collective-permute-done.26 = f32[2,4608]{1,0:T(2,128)S(1)} collective-permute-done((f32[2,4608]{1,0:T(2,128)S(1)}, f32[2,4608]{1,0:T(2,128)S(1)}, u32[]{:S(2)}, u32[]{:S(2)}) %collective-permute-start.26) | collective-permute-done | bytes 36896 | tf_op jit(solution)/shard_map/ppermute | solution.py:491
  157.6 2.9 %convert_add_fusion = f32[320,1024]{1,0:T(8,128)} fusion(bf16[320,1024]{1,0:T(8,128)(2,1)} %collective-permute-done.23, f32[320,1024]{1,0:T(8,128)S(1)} %copy-done.5, bf16[320,1024]{1,0:T(8,128)(2,1)} %collective-permute-done.21, pred[]{:T(512)S(6)} %lt.37, bf16[320,2048]{1,0:T(8,128)(2,1)S(1)} %collective-permute-done.22), kind=kLoop, calls=%fused_computation.6 | loop fusion | flops 2293760 | bytes 5242881 | tf_op jit(solution)/shard_map/add | solution.py:506
  (66 shorter events, 22.0 us)
Async XLA Ops:
  0.6 20.4 %collective-permute-start = (bf16[320,2048]{1,0:T(8,128)(2,1)}, bf16[320,2048]{1,0:T(8,128)(2,1)}, u32[]{:S(2)}, u32[]{:S(2)}) collective-permute-start(bf16[320,2048]{1,0:T(8,128)(2,1)} %refs_0_), channel_id=1, source_target_pairs={{0,2},{2,4},{3,1},{4,6},{5,3},{7,5},{17,18},{19,20},{18,17},{21,22... | collective-permute-start | bytes 3932168 | tf_op jit(solution)/shard_map/ppermute | solution.py:293
  14.9 6.5 %collective-permute-start.1 = (bf16[4,320,384]{2,1,0:T(8,128)(2,1)}, bf16[4,320,384]{2,1,0:T(8,128)(2,1)S(1)}, u32[]{:S(2)}, u32[]{:S(2)}) collective-permute-start(bf16[4,320,384]{2,1,0:T(8,128)(2,1)} %get-tuple-element.76.refs_0_.refs_4_), channel_id=1, source_target_pairs={{0,1},{1,0},{2,3},{3,2},{4,5},{5,4},{6,7},{7,6},{8,9},{9,8},{10,11... | collective-permute-start | bytes 2949128 | tf_op jit(solution)/shard_map/ppermute | solution.py:275
  15.0 6.4 %collective-permute-start.2 = (bf16[4,320,384]{2,1,0:T(8,128)(2,1)}, bf16[4,320,384]{2,1,0:T(8,128)(2,1)S(1)}, u32[]{:S(2)}, u32[]{:S(2)}) collective-permute-start(bf16[4,320,384]{2,1,0:T(8,128)(2,1)} %get-tuple-element.77.refs_1_.refs_5_), channel_id=1, source_target_pairs={{0,1},{1,0},{2,3},{3,2},{4,5},{5,4},{6,7},{7,6},{8,9},{9,8},{10,11... | collective-permute-start | bytes 2949128 | tf_op jit(solution)/shard_map/ppermute | solution.py:275
  15.5 5.5 %collective-permute-start.3 = (bf16[192,2048]{1,0:T(8,128)(2,1)}, bf16[192,2048]{1,0:T(8,128)(2,1)S(1)}, u32[]{:S(2)}, u32[]{:S(2)}) collective-permute-start(bf16[192,2048]{1,0:T(8,128)(2,1)} %get-tuple-element.73.refs_4_.refs_8_.refs_12_.refs_2_), channel_id=1, source_target_pairs={{0,1},{1,0},{2,3},{3,2},{4,5},{5,4},{6,7},{7,6},{8,9},{9,8},{10,11... | collective-permute-start | bytes 2359304 | tf_op jit(solution)/shard_map/ppermute | solution.py:275
  15.6 5.8 %collective-permute-start.4 = (bf16[192,2048]{1,0:T(8,128)(2,1)}, bf16[192,2048]{1,0:T(8,128)(2,1)S(1)}, u32[]{:S(2)}, u32[]{:S(2)}) collective-permute-start(bf16[192,2048]{1,0:T(8,128)(2,1)} %get-tuple-element.74.refs_5_.refs_9_.refs_13_.refs_3_), channel_id=1, source_target_pairs={{0,1},{1,0},{2,3},{3,2},{4,5},{5,4},{6,7},{7,6},{8,9},{9,8},{10,11... | collective-permute-start | bytes 2359304 | tf_op jit(solution)/shard_map/ppermute | solution.py:275
  21.4 1.2 copy-start
  22.6 1.0 copy-start.1
  29.1 19.7 %collective-permute-start.6 = (bf16[640,1024]{1,0:T(8,128)(2,1)}, bf16[640,1024]{1,0:T(8,128)(2,1)S(1)}, u32[]{:S(2)}, u32[]{:S(2)}) collective-permute-start(bf16[640,1024]{1,0:T(8,128)(2,1)} %shard_map.111), channel_id=1, source_target_pairs={{8,0},{11,3},{12,4},{15,7},{0,8},{3,11},{4,12},{7,15},{24,16},{27,... | collective-permute-start | bytes 3932168 | tf_op jit(solution)/shard_map/ppermute | solution.py:416
  32.5 18.3 %collective-permute-start.5 = (bf16[320,2048]{1,0:T(8,128)(2,1)}, bf16[320,2048]{1,0:T(8,128)(2,1)}, u32[]{:S(2)}, u32[]{:S(2)}) collective-permute-start(bf16[320,2048]{1,0:T(8,128)(2,1)} %collective-permute-done.refs_0_), channel_id=1, source_target_pairs={{2,4},{4,6},{3,1},{5,3},{10,12},{12,14},{11,9},{13,11},{18,20},{20... | collective-permute-start | bytes 3932168 | tf_op jit(solution)/shard_map/ppermute | solution.py:272
  34.3 28.2 %collective-permute-start.11 = (bf16[320,2048]{1,0:T(8,128)(2,1)}, bf16[320,2048]{1,0:T(8,128)(2,1)}, u32[]{:S(2)}, u32[]{:S(2)}) collective-permute-start(bf16[320,2048]{1,0:T(8,128)(2,1)} %collective-permute-done.refs_0_), channel_id=1, source_target_pairs={{1,17},{3,19},{4,20},{6,22},{17,1},{19,3},{20,4},{22,6},{9,25},{11... | collective-permute-start | bytes 3932168 | tf_op jit(solution)/shard_map/ppermute | solution.py:325
  36.0 28.2 %collective-permute-start.9 = (bf16[320,2048]{1,0:T(8,128)(2,1)}, bf16[320,2048]{1,0:T(8,128)(2,1)}, u32[]{:S(2)}, u32[]{:S(2)}) collective-permute-start(bf16[320,2048]{1,0:T(8,128)(2,1)} %refs_0_), channel_id=1, source_target_pairs={{0,1},{1,0},{2,3},{3,2},{4,5},{5,4},{6,7},{7,6},{8,9},{9,8},{10,11... | collective-permute-start | bytes 3932168 | tf_op jit(solution)/shard_map/ppermute | solution.py:275
  50.8 22.9 %collective-permute-start.8 = (bf16[640,1024]{1,0:T(8,128)(2,1)}, bf16[640,1024]{1,0:T(8,128)(2,1)}, u32[]{:S(2)}, u32[]{:S(2)}) collective-permute-start(bf16[640,1024]{1,0:T(8,128)(2,1)} %get-tuple-element.85), channel_id=1, source_target_pairs={{8,0},{10,2},{13,5},{15,7},{0,8},{2,10},{5,13},{7,15},{24,16},{26,... | collective-permute-start | bytes 3932168 | tf_op jit(solution)/shard_map/ppermute | solution.py:416
  55.8 20.8 %collective-permute-start.7 = (bf16[320,2048]{1,0:T(8,128)(2,1)}, bf16[320,2048]{1,0:T(8,128)(2,1)S(1)}, u32[]{:S(2)}, u32[]{:S(2)}) collective-permute-start(bf16[320,2048]{1,0:T(8,128)(2,1)} %maximum_select_fusion), channel_id=1, source_target_pairs={{0,2},{4,6},{7,5},{3,1},{8,10},{12,14},{15,13},{11,9},{16,18},{20,... | collective-permute-start | bytes 3932168 | tf_op jit(solution)/shard_map/ppermute | solution.py:272
  61.2 31.4 %collective-permute-start.10 = (bf16[320,2048]{1,0:T(8,128)(2,1)}, bf16[320,2048]{1,0:T(8,128)(2,1)}, u32[]{:S(2)}, u32[]{:S(2)}) collective-permute-start(bf16[320,2048]{1,0:T(8,128)(2,1)} %collective-permute-done.refs_0_), channel_id=1, source_target_pairs={{1,0},{3,2},{4,5},{6,7},{9,8},{11,10},{12,13},{14,15},{17,16},{19,... | collective-permute-start | bytes 3932168 | tf_op jit(solution)/shard_map/ppermute | solution.py:275
  62.5 41.6 %collective-permute-start.19 = (bf16[320,2048]{1,0:T(8,128)(2,1)}, bf16[320,2048]{1,0:T(8,128)(2,1)}, u32[]{:S(2)}, u32[]{:S(2)}) collective-permute-start(bf16[320,2048]{1,0:T(8,128)(2,1)} %collective-permute-done.5.refs_0_), channel_id=1, source_target_pairs={{1,17},{3,19},{4,20},{6,22},{17,1},{19,3},{20,4},{22,6},{9,25},{11... | collective-permute-start | bytes 3932168 | tf_op jit(solution)/shard_map/ppermute | solution.py:325
  64.2 30.2 %collective-permute-start.12 = (bf16[320,2048]{1,0:T(8,128)(2,1)}, bf16[320,2048]{1,0:T(8,128)(2,1)}, u32[]{:S(2)}, u32[]{:S(2)}) collective-permute-start(bf16[320,2048]{1,0:T(8,128)(2,1)} %collective-permute-done.11.refs_2_), channel_id=1, source_target_pairs={{1,0},{3,2},{4,5},{6,7},{9,8},{11,10},{12,13},{14,15},{17,16},{19,... | collective-permute-start | bytes 3932168 | tf_op jit(solution)/shard_map/ppermute | solution.py:275
  77.7 1.3 copy-start.4
  81.3 24.2 %collective-permute-start.15 = (bf16[640,1024]{1,0:T(8,128)(2,1)}, bf16[640,1024]{1,0:T(8,128)(2,1)}, u32[]{:S(2)}, u32[]{:S(2)}) collective-permute-start(bf16[640,1024]{1,0:T(8,128)(2,1)} %get-tuple-element.107), channel_id=1, source_target_pairs={{8,0},{10,2},{13,5},{15,7},{0,8},{2,10},{5,13},{7,15},{24,16},{26,... | collective-permute-start | bytes 3932168 | tf_op jit(solution)/shard_map/ppermute | solution.py:416
  85.9 21.0 %collective-permute-start.16 = (bf16[320,2048]{1,0:T(8,128)(2,1)}, bf16[320,2048]{1,0:T(8,128)(2,1)}, u32[]{:S(2)}, u32[]{:S(2)}) collective-permute-start(bf16[320,2048]{1,0:T(8,128)(2,1)} %pad_maximum_fusion), channel_id=1, source_target_pairs={{0,2},{2,4},{5,3},{7,5},{8,10},{10,12},{13,11},{15,13},{16,18},{18... | collective-permute-start | bytes 3932168 | tf_op jit(solution)/shard_map/ppermute | solution.py:272
  92.6 18.5 %collective-permute-start.14 = (bf16[320,2048]{1,0:T(8,128)(2,1)}, bf16[320,2048]{1,0:T(8,128)(2,1)}, u32[]{:S(2)}, u32[]{:S(2)}) collective-permute-start(bf16[320,2048]{1,0:T(8,128)(2,1)} %broadcast_select_fusion.refs_0_), channel_id=1, source_target_pairs={{1,17},{2,18},{5,21},{6,22},{17,1},{18,2},{21,5},{22,6},{9,25},{10... | collective-permute-start | bytes 3932168 | tf_op jit(solution)/shard_map/ppermute | solution.py:325
  94.4 26.1 %collective-permute-start.18 = (bf16[320,2048]{1,0:T(8,128)(2,1)}, bf16[320,2048]{1,0:T(8,128)(2,1)}, u32[]{:S(2)}, u32[]{:S(2)}) collective-permute-start(bf16[320,2048]{1,0:T(8,128)(2,1)} %collective-permute-done.5.refs_0_), channel_id=1, source_target_pairs={{1,0},{3,2},{4,5},{6,7},{9,8},{11,10},{12,13},{14,15},{17,16},{19,... | collective-permute-start | bytes 3932168 | tf_op jit(solution)/shard_map/ppermute | solution.py:275
  104.1 4.2 %copy-start.6 = (bf16[640,1024]{1,0:T(8,128)(2,1)S(1)}, bf16[640,1024]{1,0:T(8,128)(2,1)}, u32[]{:S(2)}) copy-start(bf16[640,1024]{1,0:T(8,128)(2,1)} %get-tuple-element.105) | copy-start | bytes 3932164
  104.1 25.3 %collective-permute-start.13 = (bf16[320,2048]{1,0:T(8,128)(2,1)}, bf16[320,2048]{1,0:T(8,128)(2,1)}, u32[]{:S(2)}, u32[]{:S(2)}) collective-permute-start(bf16[320,2048]{1,0:T(8,128)(2,1)} %broadcast_select_fusion.refs_0_), channel_id=1, source_target_pairs={{1,0},{2,3},{5,4},{6,7},{9,8},{10,11},{13,12},{14,15},{17,16},{18,... | collective-permute-start | bytes 3932168 | tf_op jit(solution)/shard_map/ppermute | solution.py:275
  105.5 15.6 %collective-permute-start.20 = (bf16[320,2048]{1,0:T(8,128)(2,1)}, bf16[320,2048]{1,0:T(8,128)(2,1)}, u32[]{:S(2)}, u32[]{:S(2)}) collective-permute-start(bf16[320,2048]{1,0:T(8,128)(2,1)} %collective-permute-done.19.refs_2_), channel_id=1, source_target_pairs={{1,0},{3,2},{4,5},{6,7},{9,8},{11,10},{12,13},{14,15},{17,16},{19,... | collective-permute-start | bytes 3932168 | tf_op jit(solution)/shard_map/ppermute | solution.py:275
  111.1 18.3 %collective-permute-start.17 = (bf16[320,2048]{1,0:T(8,128)(2,1)}, bf16[320,2048]{1,0:T(8,128)(2,1)}, u32[]{:S(2)}, u32[]{:S(2)}) collective-permute-start(bf16[320,2048]{1,0:T(8,128)(2,1)} %collective-permute-done.14.refs_2_), channel_id=1, source_target_pairs={{1,0},{2,3},{5,4},{6,7},{9,8},{10,11},{13,12},{14,15},{17,16},{18,... | collective-permute-start | bytes 3932168 | tf_op jit(solution)/shard_map/ppermute | solution.py:275
  112.4 23.2 %collective-permute-start.22 = (bf16[320,2048]{1,0:T(8,128)(2,1)S(1)}, bf16[320,2048]{1,0:T(8,128)(2,1)S(1)}, u32[]{:S(2)}, u32[]{:S(2)}) collective-permute-start(bf16[320,2048]{1,0:T(8,128)(2,1)S(1)} %pad_maximum_fusion.1), channel_id=1, source_target_pairs={{0,2},{2,4},{4,6},{3,1},{5,3},{7,5},{8,10},{10,12},{12,14},{11,9},... | collective-permute-start | bytes 3932168 | tf_op jit(solution)/shard_map/ppermute | solution.py:272
  120.6 37.1 %collective-permute-start.21 = (bf16[320,1024]{1,0:T(8,128)(2,1)}, bf16[320,1024]{1,0:T(8,128)(2,1)}, u32[]{:S(2)}, u32[]{:S(2)}) collective-permute-start(bf16[320,1024]{1,0:T(8,128)(2,1)} %get-tuple-element.132), channel_id=1, source_target_pairs={{8,0},{9,1},{10,2},{11,3},{12,4},{13,5},{14,6},{15,7},{0,8},{1,9},... | collective-permute-start | bytes 1966088 | tf_op jit(solution)/shard_map/ppermute | solution.py:416
  135.6 22.0 %collective-permute-start.23 = (bf16[320,1024]{1,0:T(8,128)(2,1)S(1)}, bf16[320,1024]{1,0:T(8,128)(2,1)}, u32[]{:S(2)}, u32[]{:S(2)}) collective-permute-start(bf16[320,1024]{1,0:T(8,128)(2,1)S(1)} %broadcast_select_fusion.1), channel_id=1, source_target_pairs={{0,1},{1,0},{2,3},{3,2},{4,5},{5,4},{6,7},{7,6},{8,9},{9,8},{10,11... | collective-permute-start | bytes 1966088 | tf_op jit(solution)/shard_map/ppermute | solution.py:500
  135.7 21.9 %copy-start.5 = (f32[320,1024]{1,0:T(8,128)S(1)}, f32[320,1024]{1,0:T(8,128)}, u32[]{:S(2)}) copy-start(f32[320,1024]{1,0:T(8,128)} %get-tuple-element.130) | copy-start | bytes 3932164
  145.5 1.3 collective-permute-start.24
  146.9 4.5 %collective-permute-start.25 = (f32[2,4608]{1,0:T(2,128)S(1)}, f32[2,4608]{1,0:T(2,128)S(1)}, u32[]{:S(2)}, u32[]{:S(2)}) collective-permute-start(f32[2,4608]{1,0:T(2,128)S(1)} %add.155), channel_id=1, source_target_pairs={{0,2},{1,3},{2,0},{3,1},{4,6},{5,7},{6,4},{7,5},{8,10},{9,11},{10,... | collective-permute-start | bytes 110600 | tf_op jit(solution)/shard_map/ppermute | solution.py:491
  151.4 4.9 %collective-permute-start.26 = (f32[2,4608]{1,0:T(2,128)S(1)}, f32[2,4608]{1,0:T(2,128)S(1)}, u32[]{:S(2)}, u32[]{:S(2)}) collective-permute-start(f32[2,4608]{1,0:T(2,128)S(1)} %add.156), channel_id=1, source_target_pairs={{0,4},{1,5},{2,6},{3,7},{4,0},{5,1},{6,2},{7,3},{8,12},{9,13},{10,... | collective-permute-start | bytes 110600 | tf_op jit(solution)/shard_map/ppermute | solution.py:491
  (2 other events, 1.8 us)

commit v3 on v2

--- a/solution.py
+++ b/solution.py
@@ -140,8 +140,44 @@
     )(ids, *ins)
 
 
-def slot_kernel(n_pieces, kept, base, ids_ref, *refs):
-    pieces, refs = refs[:n_pieces], refs[n_pieces:]
+def hop_kernel(n_got, either, n_coming, flags, ids_ref, sum_ref, *refs):
+    gots, refs = refs[: n_got * (1 + either)], refs[n_got * (1 + either) :]
+    out_ref = refs[-1]
+    total = sum_ref[...].astype(F32)
+    for i in range(n_got):
+        one = gots[i][...].astype(F32)
+        if either:
+            one = jnp.where(ids_ref[flags[0]] == 1, gots[n_got + i][...].astype(F32), one)
+        total = total + one
+    for i in range(n_coming):
+        total = total + refs[i][...].astype(F32)
+    if len(refs) > n_coming + 1:
+        total = jnp.where(ids_ref[flags[1]] == 1, refs[n_coming][...].astype(F32), total)
+    out_ref[...] = total.astype(BF16)
+
+
+def hop(ids, flags, own, got, other, coming, weight):
+    rows, columns = own.shape
+    stacked = pl.BlockSpec((rows // 2, columns), lambda i, ids: (i, 0))
+    beside = pl.BlockSpec((rows // 2, columns), lambda i, ids: (0, i))
+    ins = [own] + got + other + coming + weight
+    return pl.pallas_call(
+        functools.partial(hop_kernel, len(got), bool(other), len(coming), flags),
+        out_shape=jax.ShapeDtypeStruct((rows // 2, 2 * columns), BF16),
+        grid_spec=pltpu.PrefetchScalarGridSpec(
+            num_scalar_prefetch=1,
+            grid=(2,),
+            in_specs=[stacked] * (1 + len(got) + len(other))
+            + [beside] * (len(coming) + len(weight)),
+            out_specs=beside,
+        ),
+        compiler_params=pltpu.CompilerParams(vmem_limit_bytes=VMEM_BYTES),
+        cost_estimate=SHORT,
+    )(ids, *ins)
+
+
+def slot_kernel(n, lo, kept, base, ids_ref, *refs):
+    pieces, refs = refs[: n * lo], refs[n * lo :]
     scaled_refs, refs = refs[:2], refs[2:]
     out_grad_ref, gate_ref, up_ref, in_scale_ref, slot_ref = refs[:5]
     refs = refs[5:]
@@ -150,15 +186,19 @@
     grad_gate_ref, grad_up_ref, sum_in_ref, sum_out_ref, weight_ref, sems = refs
     shard = pieces[0].shape[0]
 
-    def copy_of(p):
-        start = pl.multiple_of(jnp.maximum(ids_ref[base + 1 + p], 0) * shard, shard)
-        return pltpu.make_async_copy(pieces[p], weight_ref.at[pl.ds(start, shard)], sems.at[p])
-
-    for p in range(n_pieces):
-
-        @pl.when(ids_ref[base + 1 + p] >= 0)
-        def _():
-            copy_of(p).start()
+    step = pl.program_id(0)
+
+    def copy_of(i, p):
+        start = pl.multiple_of(ids_ref[base + i * (lo + 1) + 1 + p] * shard, shard)
+        return pltpu.make_async_copy(
+            pieces[i * lo + p], weight_ref.at[i, pl.ds(start, shard)], sems.at[i, p]
+        )
+
+    @pl.when(step == 0)
+    def _():
+        for i in range(n):
+            for p in range(lo):
+                copy_of(i, p).start()
 
     slot = slot_ref[...]
     gate = gate_ref[...].astype(F32)
@@ -173,13 +213,14 @@
     row_in = pick_rows(slot, in_scale_ref[...])
     hidden = (act * row_in).astype(BF16)
 
-    for p in range(n_pieces):
-
-        @pl.when(ids_ref[base + 1 + p] >= 0)
+    for i in range(n):
+
+        @pl.when(step == i)
         def _():
-            copy_of(p).wait()
-
-    weight = weight_ref[...]
+            for p in range(lo):
+                copy_of(i, p).wait()
+
+    weight = weight_ref[step]
     scaled = jnp.concatenate([r[...] for r in scaled_refs], axis=0)
     grad_hidden = lax.dot_general(
         scaled, weight, (((1,), (1,)), ((), ())), preferred_element_type=F32
@@ -190,19 +231,35 @@
     product = grad_hidden * act
     forward = jnp.dot(hidden, weight, preferred_element_type=F32)
     forward = forward * out_grad_ref[...].astype(F32)
+    mores = []
     for k in range(in_scale_ref.shape[0]):
         mine = slot == k
         row = slice(k, k + 1)
         sum_in_ref[row, :] = jnp.sum(jnp.where(mine, product, 0.0), axis=0, keepdims=True)
         more = jnp.sum(jnp.where(mine, forward, 0.0), axis=0, keepdims=True)
-        sum_out_ref[row, :] = before_ref[row, :] + more if kept else more
-
-
-def weight_slot(ids, base, pieces, width, scaled, out_grad, gate, up, in_scale, slot, kept):
+        mores.append(more)
+
+    @pl.when(step == 0)
+    def _():
+        for k, more in enumerate(mores):
+            row = slice(k, k + 1)
+            sum_out_ref[row, :] = before_ref[row, :] + more if kept else more
+
+    @pl.when(step > 0)
+    def _():
+        for k, more in enumerate(mores):
+            row = slice(k, k + 1)
+            sum_out_ref[row, :] = sum_out_ref[row, :] + more
+
+
+def weight_slots(ids, base, lo, pieces, width, scaled, out_grad, gate, up, in_scale, slot, kept):
     tokens, ff = gate.shape
     d = out_grad.shape[1]
     mem = in_scale.shape[0]
-    column = lambda rows: pl.BlockSpec((rows, width), lambda i, ids: (0, ids[base]))
+    n = len(pieces) // lo
+    column = lambda rows: pl.BlockSpec(
+        (rows, width), lambda i, ids: (0, ids[base + i * (lo + 1)])
+    )
     full = lambda shape: pl.BlockSpec(shape, lambda i, ids: (0, 0))
     anywhere = pl.BlockSpec(memory_space=pl.ANY)
     ins = list(pieces) + list(scaled) + [out_grad, gate, up, in_scale, slot]
@@ -214,7 +271,7 @@
         ins += list(kept)
         specs += [anywhere] * 3 + [full((mem, d))]
     return pl.pallas_call(
-        functools.partial(slot_kernel, len(pieces), kept is not None, base),
+        functools.partial(slot_kernel, n, lo, kept is not None, base),
         out_shape=[
             jax.ShapeDtypeStruct((tokens, ff), BF16),
             jax.ShapeDtypeStruct((tokens, ff), BF16),
@@ -223,12 +280,12 @@
         ],
         grid_spec=pltpu.PrefetchScalarGridSpec(
             num_scalar_prefetch=1,
-            grid=(1,),
+            grid=(n,),
             in_specs=specs,
             out_specs=[column(tokens), column(tokens), column(mem), full((mem, d))],
             scratch_shapes=[
-                pltpu.VMEM((width, d), BF16),
-                pltpu.SemaphoreType.DMA((len(pieces),)),
+                pltpu.VMEM((n, width, d), BF16),
+                pltpu.SemaphoreType.DMA((n, lo)),
             ],
         ),
         input_output_aliases=aliases,
@@ -252,16 +309,11 @@
         z, core = place_id // lo, lax.rem(place_id, lo)
         lower, rising = z < line // 2, core < nh
         slot = member_slot[:, None]
-        last = [slot]
         chips = range(line)
         halves = range(nh)
 
-        def after(x):
-            return lax.optimization_barrier((x, last[-1]))[0]
-
-        def mark(x):
-            last.append(x[0] if isinstance(x, (list, tuple)) else x)
-            return x
+        def tie(x, y):
+            return lax.optimization_barrier((x, y))
 
         def dev(zz, c, outer=0):
             return (outer * line + zz) * lo + c
@@ -279,7 +331,7 @@
         every = lambda a: range(lo)
 
         arrived, mine, twin = [None] * line, [None] * line, [None] * line
-        mine_in, twin_in = [None] * line, [None] * line
+        whole = [None] * line
 
         def weight_first():
             pairs = []
@@ -294,7 +346,7 @@
 
         def weight_next(s):
             arrived[s] = line_step(
-                after(arrived[s - 1]), range(s - 1, line - 1), range(1, line - s + 1)
+                arrived[s - 1], range(s - 1, line - 1), range(1, line - s + 1)
             )
 
         def falls(a, j):
@@ -311,24 +363,22 @@
             return lambda a: [nh * falls(a, j) + i for i in halves]
 
         def weight_mine(j):
-            block = after(arrived[j])
+            block = arrived[j]
             if 2 * j > line:
                 straight = jnp.where(lower, z + j < line, z >= j)
-                block = mark(jnp.where(straight, block, arrived[line - j]))
+                block = jnp.where(straight, block, arrived[line - j])
             mine[j] = block
             pairs = [
-                (dev(a, h, g), dev(a, h, 1 - g))
+                (dev(a, h, g), dev(a, (h + nh) % lo, 1 - g))
                 for g in range(2)
                 for a in chips
                 for h in holders(j)(a)
             ]
             twin[j] = lax.ppermute(block, ("groups", "fsdp"), pairs)
 
-        def spread_mine(j):
-            mine_in[j] = [to_chip(after(mine[j]), holders(j), o) for o in range(1, lo)]
-
-        def spread_twin(j):
-            twin_in[j] = [to_chip(after(twin[j]), holders(j), o) for o in range(1, lo)]
+        def spread(j, core):
+            held = jnp.where((core >= nh) == (fell(j) == 1), mine[j], twin[j])
+            whole[j] = [held] + [to_chip(held, every, o) for o in range(1, lo)]
 
         numbers, at = [], {}
 
@@ -340,6 +390,9 @@
         number("half", lax.rem(core, nh) if nh > 1 else 0)
         number("own", core // 2)
         number("odd", lax.rem(core, 2))
+        number("other", rising != lower)
+        for s in range(1, line):
+            number(("hop", s), jnp.where(rising, z > s, z < line - 1 - s))
         for j in range(members):
             number(("to", j), lax.rem(member + members - j, members))
         for k in range(1, line):
@@ -353,11 +406,9 @@
                 places = source
             else:
                 down = fell(j)
-                held = [(h // nh) == down for h in source]
                 first = jnp.where(down == 1, 1 - group, group)
-                places = [jnp.where(ok, first * nh + h % nh, -1) for ok, h in zip(held, source)]
-                places += [
-                    jnp.where(ok, (1 - first) * nh + h % nh, -1) for ok, h in zip(held, source)
+                places = [
+                    jnp.where((h // nh) == down, first, 1 - first) * nh + h % nh for h in source
                 ]
             for p, value in enumerate(places):
                 number(("piece", j, p), value)
@@ -365,29 +416,24 @@
 
         kept = [None]
 
-        def use_weight(j):
-            if j == 0:
-                pieces = [weight] + own_in
-            else:
-                pieces = [mine[j]] + mine_in[j] + [twin[j]] + twin_in[j]
-            kept[0] = mark(
-                weight_slot(
-                    ids,
-                    at[("slot", j)],
-                    after(pieces),
-                    width,
-                    scaled,
-                    out_grad,
-                    gate,
-                    up,
-                    in_scale,
-                    slot,
-                    kept[0],
-                )
+        def use_weight(first, n, ids):
+            kept[0] = weight_slots(
+                ids,
+                at[("slot", first)],
+                lo,
+                [x for j in range(first, first + n) for x in whole[j]],
+                width,
+                scaled,
+                out_grad,
+                gate,
+                up,
+                in_scale,
+                slot,
+                kept[0],
             )
 
         weight_first()
-        made = mark(prepare(gate, up, in_scale, out_grad, out_scale, slot, line, nh))
+        made = prepare(gate, up, in_scale, out_grad, out_scale, slot, line, nh)
         turned, scaled = list(made[:2]), list(made[2:])
         lefts, rights = [turned], [scaled]
         for o in range(1, lo):
@@ -417,15 +463,15 @@
 
         others = [at[("to", j)] for j in range(1, members)]
         items = [(at[("send", 1)], j, BF16) for j in range(members - 1)]
-        mark(arrived[1])
-        made = partials(after(ids), at, items, others, lefts, rights, members)
-        mark(made)
+        ids, arrived[1] = tie(ids, arrived[1])
+        made = partials(ids, at, items, others, lefts, rights, members)
+        behind = weight
         exchange(1, made)
         if line > 2:
             weight_next(2)
         weight_mine(1)
-        spread_mine(1)
-        own_in = [to_chip(after(weight), every, o) for o in range(1, lo)]
+        whole[0] = [weight] + [to_chip(behind, every, o) for o in range(1, lo)]
+        ids, whole[0] = tie(ids, whole[0])
         order = list(range(2, line)) + [0]
         items = []
         for k in order:
@@ -435,59 +481,69 @@
             row = at[("keep", k)] if k else None
             items.append((row, 0, BF16 if k else F32))
         items.append((at[("keep", 1)], 0, BF16))
-        made = mark(
-            partials(ids, at, items, [at[("to", 0)]] + others, after(lefts), rights, members)
-        )
+        made = partials(ids, at, items, [at[("to", 0)]] + others, lefts, rights, members)
+        twin[1], made = tie(twin[1], made)
         to_send = {
             k: made[n * (members - 1) : (n + 1) * (members - 1)] for n, k in enumerate(order)
         }
         sums = dict(zip(order + [1], made[len(order) * (members - 1) :]))
 
         coming = []
-
-        def line_both(s):
-            total = sums[s].astype(F32)
-            for one, two in zip(after(got[s]), got[line - s] or got[s]):
-                if 2 * s > line:
-                    one = jnp.where(rising != lower, two, one)
-                total = total + one.astype(F32)
-            for x in coming:
-                total = total + jnp.concatenate([x[:, :columns], x[:, columns:]]).astype(F32)
-            total = total.astype(BF16)
-            total = jnp.concatenate([total[:shard], total[shard:]], axis=1)
-            rises = [a for a in range(s)]
-            falls = [a for a in range(line - s, line)]
-            if s + 2 < line and total.shape == weight.shape:
-                hop = jnp.where(rising, z > s, z < line - 1 - s)
-                total = mark(jnp.where(hop, after(arrived[s + 1]), total))
+        joint = shard == weight.shape[0] and columns * 2 == weight.shape[1]
+
+        def line_sum(s):
+            return hop(
+                ids,
+                (at["other"], at[("hop", s)]),
+                sums[s],
+                list(got[s]),
+                list(got[line - s]) if 2 * s > line else [],
+                list(coming),
+                [arrived[s + 1]] if s + 2 < line and joint else [],
+            )
+
+        def line_send(s, total):
+            rises, falls = list(range(s)), list(range(line - s, line))
+            if s + 2 < line and joint:
                 rises += range(s + 1, line - 1)
                 falls += range(1, line - 1 - s)
                 arrived[s + 2] = line_step(total, rises, falls)
                 coming[:] = [arrived[s + 2]]
                 return
+            coming[:] = [line_step(total, rises, falls)]
             if s + 2 < line:
                 weight_next(s + 2)
-            coming[:] = [line_step(mark(total), rises, falls)]
-
+
+        spread(1, core)
+        whole[1][0], got[1] = tie(whole[1][0], got[1])
         for s in range(1, line):
-            mark(after(got[s]))
             k = s + 1 if s + 1 < line else 0
-            exchange(k, after(to_send[k]))
+            to_send[k], got[s] = tie(to_send[k], got[s])
+            total = line_sum(s)
+            ids, total = tie(ids, total)
+            here, total = tie(core, total)
+            line_send(s, total)
+            exchange(k, to_send[k])
             if s + 1 < line:
                 weight_mine(s + 1)
-            line_both(s)
-            spread_twin(s)
-            use_weight(s - 1)
+            if s > 1:
+                spread(s, here)
+            first = s if s > 1 else 0
+            use_weight(first, s + 1 - first, ids)
             if s + 1 < line:
-                spread_mine(s + 1)
-        mark(after(got[0]))
-        use_weight(line - 1)
+                (got[k], coming[0]), kept[0] = tie((got[k], coming[0]), kept[0])
+                twin[s + 1], kept[0] = tie(twin[s + 1], kept[0])
+                if s + 2 < line and joint:
+                    arrived[s + 2] = coming[0]
         both = jnp.concatenate(kept[0][2:], axis=1)
         if fsdp & (fsdp - 1):
             both = lax.psum(both, "fsdp")
         else:
             stage = 1
             while stage < fsdp:
+                if 2 * stage == fsdp:
+                    got[0], both = tie(got[0], both)
+                    coming[0], both = tie(coming[0], both)
                 both = both + lax.ppermute(both, "fsdp", [(i, i ^ stage) for i in range(fsdp)])
                 stage *= 2
         top, bottom = coming[0][:, :columns], coming[0][:, columns:]

time: 162 us -> 149 us (0.920)
  starting transfers between devices: 57.8 us -> 43.2 us
  Pallas kernels: 57.2 us -> 65.6 us
  other arithmetic: 13.6 us -> 6.4 us
  local copies, waits for them, and re-layouts: 9.93 us -> 12 us
    pallas_call x4 -> x6, Pallas kernels: 32.8 us -> 41.2 us  [the longest x3 29 us: weight_slots(): pl.pallas_call(functools.partial(slot_kernel, n, lo, kept is not None, ba...]
    ppermute x4, waiting for transfers between devices: 9.16 us -> 1.69 us  [line_step(): return lax.ppermute(x, 'fsdp', pairs)]
    convert_element_type x3 -> x0, other arithmetic: 6.54 us -> none  [line_both(): total = total.astype(BF16)]
    ppermute x4, starting transfers between devices: 22 us -> 16.3 us  [line_step(): return lax.ppermute(x, 'fsdp', pairs)]
    ppermute x11 -> x8, starting transfers between devices: 9.1 us -> 3.71 us  [to_chip(): lax.ppermute(x, 'fsdp', [(dev(a, c), dev(a, (c + o) % lo)) for a in chips...]
    unnamed x15 -> x31, local copies, waits for them, and re-layouts: 4.14 us -> 7.88 us
    ppermute x3, waiting for transfers between devices: 6.33 us -> 9.78 us  [run(): lax.ppermute(both, 'fsdp', [(i, i ^ stage) for i in range(fsdp)])]
    ppermute x3, starting transfers between devices: 4.5 us -> 1.17 us  [run(): lax.ppermute(both, 'fsdp', [(i, i ^ stage) for i in range(fsdp)])]
  transfers between devices with their start and end apart: 27 -> 24, of which waited for: 9 -> 10; matrix products, arithmetic and copies ran while one was open for 11% -> 6% of each run, Pallas kernels for 32% -> 44%
where the time goes in v3:
time: 149 us; the launch traced here: 148 us
  Pallas kernels  65.6 us (44%)
  starting transfers between devices  43.2 us (29%)
  waiting for transfers between devices  20.2 us (14%)
  local copies, waits for them, and re-layouts  12 us (8%)
  other arithmetic  6.4 us (4%)
    pallas_call x3, Pallas kernels, weight_slots(): pl.pallas_call(functools.partial(slot_kernel, n, lo, kept is not None, ba...  29 us
    pallas_call x2, Pallas kernels, partials(): pl.pallas_call(functools.partial(partials_kernel, lo, items, len(column_a...  17.6 us
    ppermute x4, starting transfers between devices, line_step(): return lax.ppermute(x, 'fsdp', pairs)  16.3 us
    pallas_call x3, Pallas kernels, hop(): pl.pallas_call(functools.partial(hop_kernel, len(got), bool(other), len(c...  12.2 us
    ppermute x4, starting transfers between devices, exchange(): got[k].append(lax.ppermute(blocks[j - 1], ('member', 'fsdp'), pairs))  10.8 us
    ppermute x3, waiting for transfers between devices, run(): lax.ppermute(both, 'fsdp', [(i, i ^ stage) for i in range(fsdp)])  9.78 us
    unnamed x31, local copies, waits for them, and re-layouts  7.88 us
    pallas_call x1, Pallas kernels, prepare(): pl.pallas_call(functools.partial(prepare_kernel, nh), out_shape=[turned,...  6.84 us
  transfers between devices with their start and end apart: 24, of which 10 were waited for; matrix products, arithmetic and copies ran while one was open for 6% of the time, Pallas kernels for 44%

profile of v3, /device:TPU:0, one launch (start us, length us, event | category | flops | bytes accessed | tf_op | source)
XLA Modules:
  0.0 148.4 jit_solution(12289615250475597823)
XLA Ops:
  0.6 6.0 %collective-permute-start = (bf16[320,2048]{1,0:T(8,128)(2,1)}, bf16[320,2048]{1,0:T(8,128)(2,1)}, u32[]{:S(2)}, u32[]{:S(2)}) collective-permute-start(bf16[320,2048]{1,0:T(8,128)(2,1)} %refs_0_), channel_id=1, source_target_pairs={{0,2},{2,4},{3,1},{4,6},{5,3},{7,5},{17,18},{19,20},{18,17},{21,22... | collective-permute-start | bytes 3932168 | tf_op jit(solution)/shard_map/ppermute | solution.py:345
  6.7 1.5 broadcast_in_dim.4.slot_ref.refs_10_.refs_8_
  8.1 6.8 %shard_map.110 = (bf16[4,320,384]{2,1,0:T(8,128)(2,1)}, bf16[4,320,384]{2,1,0:T(8,128)(2,1)}, bf16[192,2048]{1,0:T(8,128)(2,1)}, bf16[192,2048]{1,0:T(8,128)(2,1)}) custom-call(bf16[384,2560]{1,0:T(8,128)(2,1)} %refs_5_.3, bf16[384,2560]{1,0:T(8,128)(2,1)} %refs_6_.5, f32[2,2560]{1,0:T(2,128)} %refs_7_.5, bf16[384,2048]{1,0:T(8,128)(2,1)} %refs_4_.3, ...), custom_call_target="tpu_custom_call" | custom-call | flops 1 | bytes 1 | tf_op jit(solution)/shard_map/pallas_call | solution.py:55
  16.8 4.2 %collective-permute-done = bf16[320,2048]{1,0:T(8,128)(2,1)} collective-permute-done((bf16[320,2048]{1,0:T(8,128)(2,1)}, bf16[320,2048]{1,0:T(8,128)(2,1)}, u32[]{:S(2)}, u32[]{:S(2)}) %collective-permute-start) | collective-permute-done | bytes 1310752 | tf_op jit(solution)/shard_map/ppermute | solution.py:345
  21.0 1.3 collective-permute-start.2
  24.5 5.5 %shard_map.112 = bf16[640,1024]{1,0:T(8,128)(2,1)} custom-call(s32[28]{0:T(128)} %stack.121.ids_ref, bf16[4,320,384]{2,1,0:T(8,128)(2,1)} %get-tuple-element.89.refs_0_.refs_4_, bf16[4,320,384]{2,1,0:T(8,128)(2,1)} %get-tuple-element.90.refs_1_.refs_5_, bf16[4,320,384]{2,1,0:T(8,128)(2,1)} %copy-done, bf16[4,320,384]{2,1,0:T(8,128)(2,1)} %copy-done.1, ...), custom_call_target="tpu_custom_call" | custom-call | flops 1 | bytes 1 | tf_op jit(solution)/shard_map/pallas_call | solution.py:129
  30.0 3.4 %collective-permute-start.7 = (bf16[640,1024]{1,0:T(8,128)(2,1)}, bf16[640,1024]{1,0:T(8,128)(2,1)}, u32[]{:S(2)}, u32[]{:S(2)}) collective-permute-start(bf16[640,1024]{1,0:T(8,128)(2,1)} %shard_map.112), channel_id=1, source_target_pairs={{8,0},{11,3},{12,4},{15,7},{0,8},{3,11},{4,12},{7,15},{24,16},{27,... | collective-permute-start | bytes 3932168 | tf_op jit(solution)/shard_map/ppermute | solution.py:462
  34.2 12.1 %shard_map.111 = (bf16[640,1024]{1,0:T(8,128)(2,1)}, bf16[640,1024]{1,0:T(8,128)(2,1)}, bf16[320,1024]{1,0:T(8,128)(2,1)}, bf16[640,1024]{1,0:T(8,128)(2,1)}, bf...) custom-call(s32[28]{0:T(128)} %stack.121.ids_ref, ...), custom_call_target="tpu_custom_call" | custom-call | flops 1 | bytes 1 | tf_op jit(solution)/shard_map/pallas_call | solution.py:129
  46.3 1.5 broadcast_select_fusion.3.refs_2_
  47.8 2.5 %collective-permute-start.11 = (bf16[320,2048]{1,0:T(8,128)(2,1)S(1)}, bf16[320,2048]{1,0:T(8,128)(2,1)}, u32[]{:S(2)}, u32[]{:S(2)}) collective-permute-start(bf16[320,2048]{1,0:T(8,128)(2,1)S(1)} %broadcast_select_fusion.3.refs_2_), channel_id=1, source_target_pairs={{0,1},{1,0},{2,3},{3,2},{4,5},{5,4},{6,7},{7,6},{8,9},{9,8},{10,11... | collective-permute-start | bytes 3932168 | tf_op jit(solution)/shard_map/ppermute | solution.py:327
  51.4 3.9 %shard_map.113 = bf16[320,2048]{1,0:T(8,128)(2,1)} custom-call(s32[28]{0:T(128)} %stack.121.ids_ref, bf16[640,1024]{1,0:T(8,128)(2,1)} %get-tuple-element.100.sum_ref, bf16[640,1024]{1,0:T(8,128)(2,1)} %collective-permute-done.7.refs_0_.refs_1_, bf16[320,2048]{1,0:T(8,128)(2,1)} %copy-done.7), custom_call_target="tpu_custom_call" | custom-call | flops 1 | bytes 1 | tf_op jit(solution)/shard_map/pallas_call | solution.py:164
  55.2 3.4 %collective-permute-start.9 = (bf16[640,1024]{1,0:T(8,128)(2,1)}, bf16[640,1024]{1,0:T(8,128)(2,1)}, u32[]{:S(2)}, u32[]{:S(2)}) collective-permute-start(bf16[640,1024]{1,0:T(8,128)(2,1)} %get-tuple-element.108), channel_id=1, source_target_pairs={{8,0},{10,2},{13,5},{15,7},{0,8},{2,10},{5,13},{7,15},{24,16},{26,... | collective-permute-start | bytes 3932168 | tf_op jit(solution)/shard_map/ppermute | solution.py:462
  58.6 8.3 %collective-permute-start.10 = (bf16[320,2048]{1,0:T(8,128)(2,1)}, bf16[320,2048]{1,0:T(8,128)(2,1)S(1)}, u32[]{:S(2)}, u32[]{:S(2)}) collective-permute-start(bf16[320,2048]{1,0:T(8,128)(2,1)} %shard_map.113), channel_id=1, source_target_pairs={{0,2},{4,6},{7,5},{3,1},{8,10},{12,14},{15,13},{11,9},{16,18},{20,... | collective-permute-start | bytes 3932168 | tf_op jit(solution)/shard_map/ppermute | solution.py:324
  66.9 1.3 collective-permute-start.14
  68.2 12.7 %shard_map.114 = (bf16[384,2560]{1,0:T(8,128)(2,1)}, bf16[384,2560]{1,0:T(8,128)(2,1)}, f32[2,2560]{1,0:T(2,128)}, f32[2,2048]{1,0:T(2,128)}) custom-call(s32[28]{0:T(128)} %stack.121.ids_ref, bf16[320,2048]{1,0:T(8,128)(2,1)} %refs_0_, bf16[320,2048]{1,0:T(8,128)(2,1)} %collective-permute-done.1.refs_1_, bf16[320,2048]{1,0:T(8,128)(2,1)} %copy-done.4, ...), custom_call_target="tpu_custom_call" | custom-call | flops 1 | bytes 1 | tf_op jit(solution)/shard_map/pallas_call | solution.py:273
  80.9 1.3 collective-permute-done.10.refs_1_
  83.3 4.0 %shard_map.115 = bf16[320,2048]{1,0:T(8,128)(2,1)} custom-call(s32[28]{0:T(128)} %stack.121.ids_ref, bf16[640,1024]{1,0:T(8,128)(2,1)} %get-tuple-element.106.sum_ref, bf16[640,1024]{1,0:T(8,128)(2,1)} %collective-permute-done.9.refs_0_, bf16[320,2048]{1,0:T(8,128)(2,1)} %copy-done.9), custom_call_target="tpu_custom_call" | custom-call | flops 1 | bytes 1 | tf_op jit(solution)/shard_map/pallas_call | solution.py:164
  87.3 3.4 %collective-permute-start.12 = (bf16[640,1024]{1,0:T(8,128)(2,1)}, bf16[640,1024]{1,0:T(8,128)(2,1)}, u32[]{:S(2)}, u32[]{:S(2)}) collective-permute-start(bf16[640,1024]{1,0:T(8,128)(2,1)} %get-tuple-element.124), channel_id=1, source_target_pairs={{8,0},{10,2},{13,5},{15,7},{0,8},{2,10},{5,13},{7,15},{24,16},{26,... | collective-permute-start | bytes 3932168 | tf_op jit(solution)/shard_map/ppermute | solution.py:462
  90.7 5.4 %collective-permute-start.13 = (bf16[320,2048]{1,0:T(8,128)(2,1)}, bf16[320,2048]{1,0:T(8,128)(2,1)}, u32[]{:S(2)}, u32[]{:S(2)}) collective-permute-start(bf16[320,2048]{1,0:T(8,128)(2,1)} %shard_map.115), channel_id=1, source_target_pairs={{0,2},{2,4},{5,3},{7,5},{8,10},{10,12},{13,11},{15,13},{16,18},{18... | collective-permute-start | bytes 3932168 | tf_op jit(solution)/shard_map/ppermute | solution.py:324
  96.1 1.6 %broadcast_select_fusion.2.refs_0_ = bf16[320,2048]{1,0:T(8,128)(2,1)S(1)} fusion(bf16[320,2048]{1,0:T(8,128)(2,1)S(1)} %copy-done.8, bf16[320,2048]{1,0:T(8,128)(2,1)} %collective-permute-done.14, pred[]{:T(512)S(6)} %eq.74), kind=kLoop, calls=%fused_computation.3 | loop fusion | flops 655360 | bytes 3932161 | tf_op jit(solution)/shard_map/jit(_where)/select_n | solution.py:380
  98.8 1.5 collective-permute-start.16
  101.9 8.1 %shard_map.116 = (bf16[384,2560]{1,0:T(8,128)(2,1)}, bf16[384,2560]{1,0:T(8,128)(2,1)}, f32[2,2560]{1,0:T(2,128)}, f32[2,2048]{1,0:T(2,128)}) custom-call(s32[28]{0:T(128)} %stack.121.ids_ref, bf16[320,2048]{1,0:T(8,128)(2,1)} %copy-done.6, bf16[320,2048]{1,0:T(8,128)(2,1)} %copy-done.11, ...), custom_call_target="tpu_custom_call", output_to_operand_aliasing={{0}: (10, {}), {1}: (11, {}), {2}: (12, {})} | custom-call | flops 1 | bytes 1 | tf_op jit(solution)/shard_map/pallas_call | solution.py:273
  110.4 4.4 %shard_map.117 = bf16[320,2048]{1,0:T(8,128)(2,1)} custom-call(s32[28]{0:T(128)} %stack.121.ids_ref, bf16[640,1024]{1,0:T(8,128)(2,1)} %get-tuple-element.122.sum_ref, bf16[640,1024]{1,0:T(8,128)(2,1)} %collective-permute-done.12.refs_0_, bf16[640,1024]{1,0:T(8,128)(2,1)} %collective-permute-done.7.refs_0_.refs_1_, ...), custom_call_target="tpu_custom_call" | custom-call | flops 1 | bytes 1 | tf_op jit(solution)/shard_map/pallas_call | solution.py:164
  114.7 3.1 %collective-permute-done.16 = bf16[320,2048]{1,0:T(8,128)(2,1)} collective-permute-done((bf16[320,2048]{1,0:T(8,128)(2,1)S(1)}, bf16[320,2048]{1,0:T(8,128)(2,1)}, u32[]{:S(2)}, u32[]{:S(2)}) %collective-permute-start.16) | collective-permute-done | bytes 1310752 | tf_op jit(solution)/shard_map/ppermute | solution.py:377
  117.9 1.5 broadcast_select_fusion.1.refs_0_
  119.4 1.8 %collective-permute-start.21 = (bf16[320,2048]{1,0:T(8,128)(2,1)}, bf16[320,2048]{1,0:T(8,128)(2,1)S(1)}, u32[]{:S(2)}, u32[]{:S(2)}) collective-permute-start(bf16[320,2048]{1,0:T(8,128)(2,1)} %shard_map.117), channel_id=1, source_target_pairs={{0,2},{2,4},{4,6},{3,1},{5,3},{7,5},{8,10},{10,12},{12,14},{11,9},... | collective-permute-start | bytes 3932168 | tf_op jit(solution)/shard_map/ppermute | solution.py:324
  122.6 8.1 %shard_map.118 = (bf16[384,2560]{1,0:T(8,128)(2,1)}, bf16[384,2560]{1,0:T(8,128)(2,1)}, f32[2,2560]{1,0:T(2,128)}, f32[2,2048]{1,0:T(2,128)}) custom-call(s32[28]{0:T(128)} %stack.121.ids_ref, bf16[320,2048]{1,0:T(8,128)(2,1)} %copy-done.5, ...), custom_call_target="tpu_custom_call", output_to_operand_aliasing={{0}: (10, {}), {1}: (11, {}), {2}: (12, {})} | custom-call | flops 1 | bytes 1 | tf_op jit(solution)/shard_map/pallas_call | solution.py:273
  132.4 1.1 collective-permute-done.19
  134.5 3.5 %collective-permute-done.20 = f32[2,4608]{1,0:T(2,128)S(1)} collective-permute-done((f32[2,4608]{1,0:T(2,128)S(1)}, f32[2,4608]{1,0:T(2,128)S(1)}, u32[]{:S(2)}, u32[]{:S(2)}) %collective-permute-start.20) | collective-permute-done | bytes 36896 | tf_op jit(solution)/shard_map/ppermute | solution.py:547
  139.0 1.2 collective-permute-start.22
  140.3 5.2 %collective-permute-done.23 = f32[2,4608]{1,0:T(2,128)S(1)} collective-permute-done((f32[2,4608]{1,0:T(2,128)S(1)}, f32[2,4608]{1,0:T(2,128)S(1)}, u32[]{:S(2)}, u32[]{:S(2)}) %collective-permute-start.23) | collective-permute-done | bytes 36896 | tf_op jit(solution)/shard_map/ppermute | solution.py:547
  146.8 1.6 %convert_add_fusion = f32[320,1024]{1,0:T(8,128)} fusion(bf16[320,1024]{1,0:T(8,128)(2,1)S(1)} %collective-permute-done.22, f32[320,1024]{1,0:T(8,128)S(1)} %copy-done.12, bf16[320,1024]{1,0:T(8,128)(2,1)S(1)} %copy-done.14, pred[]{:T(512)S(6)} %lt.30, bf16[320,2048]{1,0:T(8,128)(2,1)S(1)} %collective-permute-done.21), kind=kLoop, calls=%fused_computation | loop fusion | flops 2293760 | bytes 5242881 | tf_op jit(solution)/shard_map/add | solution.py:562
  (70 shorter events, 16.3 us)
Async XLA Ops:
  0.6 20.4 %collective-permute-start = (bf16[320,2048]{1,0:T(8,128)(2,1)}, bf16[320,2048]{1,0:T(8,128)(2,1)}, u32[]{:S(2)}, u32[]{:S(2)}) collective-permute-start(bf16[320,2048]{1,0:T(8,128)(2,1)} %refs_0_), channel_id=1, source_target_pairs={{0,2},{2,4},{3,1},{4,6},{5,3},{7,5},{17,18},{19,20},{18,17},{21,22... | collective-permute-start | bytes 3932168 | tf_op jit(solution)/shard_map/ppermute | solution.py:345
  15.0 6.0 %collective-permute-start.5 = (bf16[192,2048]{1,0:T(8,128)(2,1)}, bf16[192,2048]{1,0:T(8,128)(2,1)S(1)}, u32[]{:S(2)}, u32[]{:S(2)}) collective-permute-start(bf16[192,2048]{1,0:T(8,128)(2,1)} %get-tuple-element.91.refs_8_.refs_12_.refs_4_.refs_2_), channel_id=1, source_target_pairs={{0,1},{1,0},{2,3},{3,2},{4,5},{5,4},{6,7},{7,6},{8,9},{9,8},{10,11... | collective-permute-start | bytes 2359304 | tf_op jit(solution)/shard_map/ppermute | solution.py:327
  15.0 7.3 %collective-permute-start.3 = (bf16[4,320,384]{2,1,0:T(8,128)(2,1)}, bf16[4,320,384]{2,1,0:T(8,128)(2,1)S(1)}, u32[]{:S(2)}, u32[]{:S(2)}) collective-permute-start(bf16[4,320,384]{2,1,0:T(8,128)(2,1)} %get-tuple-element.89.refs_0_.refs_4_), channel_id=1, source_target_pairs={{0,1},{1,0},{2,3},{3,2},{4,5},{5,4},{6,7},{7,6},{8,9},{9,8},{10,11... | collective-permute-start | bytes 2949128 | tf_op jit(solution)/shard_map/ppermute | solution.py:327
  15.5 6.8 %collective-permute-start.4 = (bf16[4,320,384]{2,1,0:T(8,128)(2,1)}, bf16[4,320,384]{2,1,0:T(8,128)(2,1)S(1)}, u32[]{:S(2)}, u32[]{:S(2)}) collective-permute-start(bf16[4,320,384]{2,1,0:T(8,128)(2,1)} %get-tuple-element.90.refs_1_.refs_5_), channel_id=1, source_target_pairs={{0,1},{1,0},{2,3},{3,2},{4,5},{5,4},{6,7},{7,6},{8,9},{9,8},{10,11... | collective-permute-start | bytes 2949128 | tf_op jit(solution)/shard_map/ppermute | solution.py:327
  15.6 6.7 %collective-permute-start.6 = (bf16[192,2048]{1,0:T(8,128)(2,1)}, bf16[192,2048]{1,0:T(8,128)(2,1)S(1)}, u32[]{:S(2)}, u32[]{:S(2)}) collective-permute-start(bf16[192,2048]{1,0:T(8,128)(2,1)} %get-tuple-element.92.refs_9_.refs_13_.refs_5_.refs_3_), channel_id=1, source_target_pairs={{0,1},{1,0},{2,3},{3,2},{4,5},{5,4},{6,7},{7,6},{8,9},{9,8},{10,11... | collective-permute-start | bytes 2359304 | tf_op jit(solution)/shard_map/ppermute | solution.py:327
  21.0 13.2 %collective-permute-start.1 = (bf16[320,2048]{1,0:T(8,128)(2,1)}, bf16[320,2048]{1,0:T(8,128)(2,1)}, u32[]{:S(2)}, u32[]{:S(2)}) collective-permute-start(bf16[320,2048]{1,0:T(8,128)(2,1)} %refs_0_), channel_id=1, source_target_pairs={{0,1},{1,0},{2,3},{3,2},{4,5},{5,4},{6,7},{7,6},{8,9},{9,8},{10,11... | collective-permute-start | bytes 3932168 | tf_op jit(solution)/shard_map/ppermute | solution.py:327
  21.0 1.4 copy-start.2
  21.0 25.3 %collective-permute-start.2 = (bf16[320,2048]{1,0:T(8,128)(2,1)}, bf16[320,2048]{1,0:T(8,128)(2,1)}, u32[]{:S(2)}, u32[]{:S(2)}) collective-permute-start(bf16[320,2048]{1,0:T(8,128)(2,1)} %collective-permute-done), channel_id=1, source_target_pairs={{1,16},{3,18},{4,21},{6,23},{17,0},{19,2},{20,5},{22,7},{9,24},{11... | collective-permute-start | bytes 3932168 | tf_op jit(solution)/shard_map/ppermute | solution.py:377
  22.3 1.2 copy-start
  30.0 20.3 %collective-permute-start.7 = (bf16[640,1024]{1,0:T(8,128)(2,1)}, bf16[640,1024]{1,0:T(8,128)(2,1)}, u32[]{:S(2)}, u32[]{:S(2)}) collective-permute-start(bf16[640,1024]{1,0:T(8,128)(2,1)} %shard_map.112), channel_id=1, source_target_pairs={{8,0},{11,3},{12,4},{15,7},{0,8},{3,11},{4,12},{7,15},{24,16},{27,... | collective-permute-start | bytes 3932168 | tf_op jit(solution)/shard_map/ppermute | solution.py:462
  33.4 16.9 %collective-permute-start.8 = (bf16[320,2048]{1,0:T(8,128)(2,1)}, bf16[320,2048]{1,0:T(8,128)(2,1)S(1)}, u32[]{:S(2)}, u32[]{:S(2)}) collective-permute-start(bf16[320,2048]{1,0:T(8,128)(2,1)} %collective-permute-done), channel_id=1, source_target_pairs={{2,4},{4,6},{3,1},{5,3},{10,12},{12,14},{11,9},{13,11},{18,20},{20... | collective-permute-start | bytes 3932168 | tf_op jit(solution)/shard_map/ppermute | solution.py:324
  47.8 7.5 %copy-start.4 = (bf16[320,2048]{1,0:T(8,128)(2,1)}, bf16[320,2048]{1,0:T(8,128)(2,1)S(1)}, u32[]{:S(2)}) copy-start(bf16[320,2048]{1,0:T(8,128)(2,1)S(1)} %broadcast_select_fusion.3.refs_2_) | copy-start | bytes 3932164
  47.8 20.4 %collective-permute-start.11 = (bf16[320,2048]{1,0:T(8,128)(2,1)S(1)}, bf16[320,2048]{1,0:T(8,128)(2,1)}, u32[]{:S(2)}, u32[]{:S(2)}) collective-permute-start(bf16[320,2048]{1,0:T(8,128)(2,1)S(1)} %broadcast_select_fusion.3.refs_2_), channel_id=1, source_target_pairs={{0,1},{1,0},{2,3},{3,2},{4,5},{5,4},{6,7},{7,6},{8,9},{9,8},{10,11... | collective-permute-start | bytes 3932168 | tf_op jit(solution)/shard_map/ppermute | solution.py:327
  55.2 25.7 %collective-permute-start.9 = (bf16[640,1024]{1,0:T(8,128)(2,1)}, bf16[640,1024]{1,0:T(8,128)(2,1)}, u32[]{:S(2)}, u32[]{:S(2)}) collective-permute-start(bf16[640,1024]{1,0:T(8,128)(2,1)} %get-tuple-element.108), channel_id=1, source_target_pairs={{8,0},{10,2},{13,5},{15,7},{0,8},{2,10},{5,13},{7,15},{24,16},{26,... | collective-permute-start | bytes 3932168 | tf_op jit(solution)/shard_map/ppermute | solution.py:462
  58.6 23.6 %collective-permute-start.10 = (bf16[320,2048]{1,0:T(8,128)(2,1)}, bf16[320,2048]{1,0:T(8,128)(2,1)S(1)}, u32[]{:S(2)}, u32[]{:S(2)}) collective-permute-start(bf16[320,2048]{1,0:T(8,128)(2,1)} %shard_map.113), channel_id=1, source_target_pairs={{0,2},{4,6},{7,5},{3,1},{8,10},{12,14},{15,13},{11,9},{16,18},{20,... | collective-permute-start | bytes 3932168 | tf_op jit(solution)/shard_map/ppermute | solution.py:324
  66.9 29.2 %collective-permute-start.14 = (bf16[320,2048]{1,0:T(8,128)(2,1)}, bf16[320,2048]{1,0:T(8,128)(2,1)}, u32[]{:S(2)}, u32[]{:S(2)}) collective-permute-start(bf16[320,2048]{1,0:T(8,128)(2,1)} %copy-done.7), channel_id=1, source_target_pairs={{1,16},{3,18},{4,21},{6,23},{17,0},{19,2},{20,5},{22,7},{9,24},{11... | collective-permute-start | bytes 3932168 | tf_op jit(solution)/shard_map/ppermute | solution.py:377
  83.3 12.8 %copy-start.8 = (bf16[320,2048]{1,0:T(8,128)(2,1)S(1)}, bf16[320,2048]{1,0:T(8,128)(2,1)}, u32[]{:S(2)}) copy-start(bf16[320,2048]{1,0:T(8,128)(2,1)} %copy-done.7) | copy-start | bytes 3932164
  87.3 22.7 %collective-permute-start.12 = (bf16[640,1024]{1,0:T(8,128)(2,1)}, bf16[640,1024]{1,0:T(8,128)(2,1)}, u32[]{:S(2)}, u32[]{:S(2)}) collective-permute-start(bf16[640,1024]{1,0:T(8,128)(2,1)} %get-tuple-element.124), channel_id=1, source_target_pairs={{8,0},{10,2},{13,5},{15,7},{0,8},{2,10},{5,13},{7,15},{24,16},{26,... | collective-permute-start | bytes 3932168 | tf_op jit(solution)/shard_map/ppermute | solution.py:462
  90.7 19.7 %collective-permute-start.13 = (bf16[320,2048]{1,0:T(8,128)(2,1)}, bf16[320,2048]{1,0:T(8,128)(2,1)}, u32[]{:S(2)}, u32[]{:S(2)}) collective-permute-start(bf16[320,2048]{1,0:T(8,128)(2,1)} %shard_map.115), channel_id=1, source_target_pairs={{0,2},{2,4},{5,3},{7,5},{8,10},{10,12},{13,11},{15,13},{16,18},{18... | collective-permute-start | bytes 3932168 | tf_op jit(solution)/shard_map/ppermute | solution.py:324
  96.1 1.7 %copy-start.10 = (bf16[320,2048]{1,0:T(8,128)(2,1)S(1)}, bf16[320,2048]{1,0:T(8,128)(2,1)}, u32[]{:S(2)}) copy-start(bf16[320,2048]{1,0:T(8,128)(2,1)} %copy-done.9) | copy-start | bytes 3932164
  97.7 3.1 %collective-permute-start.15 = (bf16[320,2048]{1,0:T(8,128)(2,1)S(1)}, bf16[320,2048]{1,0:T(8,128)(2,1)S(1)}, u32[]{:S(2)}, u32[]{:S(2)}) collective-permute-start(bf16[320,2048]{1,0:T(8,128)(2,1)S(1)} %broadcast_select_fusion.2.refs_0_), channel_id=1, source_target_pairs={{0,1},{1,0},{2,3},{3,2},{4,5},{5,4},{6,7},{7,6},{8,9},{9,8},{10,11... | collective-permute-start | bytes 3932168 | tf_op jit(solution)/shard_map/ppermute | solution.py:327
  98.8 19.0 %collective-permute-start.16 = (bf16[320,2048]{1,0:T(8,128)(2,1)S(1)}, bf16[320,2048]{1,0:T(8,128)(2,1)}, u32[]{:S(2)}, u32[]{:S(2)}) collective-permute-start(bf16[320,2048]{1,0:T(8,128)(2,1)S(1)} %broadcast_select_fusion), channel_id=1, source_target_pairs={{1,16},{2,19},{5,20},{6,23},{17,0},{18,3},{21,4},{22,7},{9,24},{10... | collective-permute-start | bytes 3932168 | tf_op jit(solution)/shard_map/ppermute | solution.py:377
  119.3 3.2 %copy-start.5 = (bf16[320,2048]{1,0:T(8,128)(2,1)}, bf16[320,2048]{1,0:T(8,128)(2,1)S(1)}, u32[]{:S(2)}) copy-start(bf16[320,2048]{1,0:T(8,128)(2,1)S(1)} %broadcast_select_fusion.1.refs_0_) | copy-start | bytes 3932164
  119.3 3.2 %collective-permute-start.17 = (bf16[320,2048]{1,0:T(8,128)(2,1)S(1)}, bf16[320,2048]{1,0:T(8,128)(2,1)}, u32[]{:S(2)}, u32[]{:S(2)}) collective-permute-start(bf16[320,2048]{1,0:T(8,128)(2,1)S(1)} %broadcast_select_fusion.1.refs_0_), channel_id=1, source_target_pairs={{0,1},{1,0},{2,3},{3,2},{4,5},{5,4},{6,7},{7,6},{8,9},{9,8},{10,11... | collective-permute-start | bytes 3932168 | tf_op jit(solution)/shard_map/ppermute | solution.py:327
  119.4 19.5 %collective-permute-start.21 = (bf16[320,2048]{1,0:T(8,128)(2,1)}, bf16[320,2048]{1,0:T(8,128)(2,1)S(1)}, u32[]{:S(2)}, u32[]{:S(2)}) collective-permute-start(bf16[320,2048]{1,0:T(8,128)(2,1)} %shard_map.117), channel_id=1, source_target_pairs={{0,2},{2,4},{4,6},{3,1},{5,3},{7,5},{8,10},{10,12},{12,14},{11,9},... | collective-permute-start | bytes 3932168 | tf_op jit(solution)/shard_map/ppermute | solution.py:324
  121.2 16.9 %collective-permute-start.18 = (bf16[320,1024]{1,0:T(8,128)(2,1)}, bf16[320,1024]{1,0:T(8,128)(2,1)S(1)}, u32[]{:S(2)}, u32[]{:S(2)}) collective-permute-start(bf16[320,1024]{1,0:T(8,128)(2,1)} %get-tuple-element.159), channel_id=1, source_target_pairs={{8,0},{9,1},{10,2},{11,3},{12,4},{13,5},{14,6},{15,7},{0,8},{1,9},... | collective-permute-start | bytes 1966088 | tf_op jit(solution)/shard_map/ppermute | solution.py:462
  130.7 16.1 %copy-start.12 = (f32[320,1024]{1,0:T(8,128)S(1)}, f32[320,1024]{1,0:T(8,128)}, u32[]{:S(2)}) copy-start(f32[320,1024]{1,0:T(8,128)} %get-tuple-element.158) | copy-start | bytes 3932164
  132.3 1.2 collective-permute-start.19
  133.5 4.5 %collective-permute-start.20 = (f32[2,4608]{1,0:T(2,128)S(1)}, f32[2,4608]{1,0:T(2,128)S(1)}, u32[]{:S(2)}, u32[]{:S(2)}) collective-permute-start(f32[2,4608]{1,0:T(2,128)S(1)} %add.120), channel_id=1, source_target_pairs={{0,2},{1,3},{2,0},{3,1},{4,6},{5,7},{6,4},{7,5},{8,10},{9,11},{10,... | collective-permute-start | bytes 110600 | tf_op jit(solution)/shard_map/ppermute | solution.py:547
  138.9 7.8 %copy-start.14 = (bf16[320,1024]{1,0:T(8,128)(2,1)S(1)}, bf16[320,1024]{1,0:T(8,128)(2,1)}, u32[]{:S(2)}) copy-start(bf16[320,1024]{1,0:T(8,128)(2,1)} %copy-done.13) | copy-start | bytes 1966084
  139.0 7.7 %collective-permute-start.22 = (bf16[320,1024]{1,0:T(8,128)(2,1)S(1)}, bf16[320,1024]{1,0:T(8,128)(2,1)S(1)}, u32[]{:S(2)}, u32[]{:S(2)}) collective-permute-start(bf16[320,1024]{1,0:T(8,128)(2,1)S(1)} %broadcast_select_fusion.4), channel_id=1, source_target_pairs={{0,1},{1,0},{2,3},{3,2},{4,5},{5,4},{6,7},{7,6},{8,9},{9,8},{10,11... | collective-permute-start | bytes 1966088 | tf_op jit(solution)/shard_map/ppermute | solution.py:556
  140.3 5.3 %collective-permute-start.23 = (f32[2,4608]{1,0:T(2,128)S(1)}, f32[2,4608]{1,0:T(2,128)S(1)}, u32[]{:S(2)}, u32[]{:S(2)}) collective-permute-start(f32[2,4608]{1,0:T(2,128)S(1)} %add.121), channel_id=1, source_target_pairs={{0,4},{1,5},{2,6},{3,7},{4,0},{5,1},{6,2},{7,3},{8,12},{9,13},{10,... | collective-permute-start | bytes 110600 | tf_op jit(solution)/shard_map/ppermute | solution.py:547
  (7 other events, 7.0 us)

commit v4 on v3

--- a/solution.py
+++ b/solution.py
@@ -536,16 +536,24 @@
                 if s + 2 < line and joint:
                     arrived[s + 2] = coming[0]
         both = jnp.concatenate(kept[0][2:], axis=1)
-        if fsdp & (fsdp - 1):
+        if lo & (lo - 1):
             both = lax.psum(both, "fsdp")
         else:
             stage = 1
-            while stage < fsdp:
-                if 2 * stage == fsdp:
-                    got[0], both = tie(got[0], both)
-                    coming[0], both = tie(coming[0], both)
+            while stage < lo:
                 both = both + lax.ppermute(both, "fsdp", [(i, i ^ stage) for i in range(fsdp)])
                 stage *= 2
+            terms = [both] + [
+                lax.ppermute(both, "fsdp", [((i + r * lo) % fsdp, i) for i in range(fsdp)])
+                for r in range(1, line)
+            ]
+            (got[0], coming[0]), terms[1] = tie((got[0], coming[0]), terms[1])
+            both = None
+            for a in chips:
+                term = terms[0]
+                for r in range(1, line):
+                    term = jnp.where(lax.rem(z + r, line) == a, terms[r], term)
+                both = term if both is None else both + term
         top, bottom = coming[0][:, :columns], coming[0][:, columns:]
         landed = []
         for part in range(2):

time: 149 us -> 145 us (0.973)
  waiting for transfers between devices: 20.2 us -> 14 us
  starting transfers between devices: 43.2 us -> 45.3 us
    ppermute x3 -> x1, waiting for transfers between devices: 9.78 us -> 1.08 us  [run(): lax.ppermute(both, 'fsdp', [(i, i ^ stage) for i in range(fsdp)])]
    ppermute x0 -> x3, starting transfers between devices: none -> 2.42 us  [run(): lax.ppermute(both, 'fsdp', [((i + r * lo) % fsdp, i) for i in range(fsdp)])]
    ppermute x4, waiting for transfers between devices: 0.09 us -> 2.11 us  [exchange(): got[k].append(lax.ppermute(blocks[j - 1], ('member', 'fsdp'), pairs))]
  transfers between devices with their start and end apart: 24 -> 25, of which waited for: 10 -> 9; matrix products, arithmetic and copies ran while one was open for 6% -> 6% of each run, Pallas kernels for 44% -> 45%
where the time goes in v4:
time: 145 us; the launch traced here: 144 us
  Pallas kernels  65.6 us (45%)
  starting transfers between devices  45.3 us (31%)
  waiting for transfers between devices  14 us (10%)
  local copies, waits for them, and re-layouts  11.9 us (8%)
  other arithmetic  6.43 us (4%)
    pallas_call x3, Pallas kernels, weight_slots(): pl.pallas_call(functools.partial(slot_kernel, n, lo, kept is not None, ba...  29 us
    pallas_call x2, Pallas kernels, partials(): pl.pallas_call(functools.partial(partials_kernel, lo, items, len(column_a...  17.6 us
    ppermute x4, starting transfers between devices, line_step(): return lax.ppermute(x, 'fsdp', pairs)  16.2 us
    pallas_call x3, Pallas kernels, hop(): pl.pallas_call(functools.partial(hop_kernel, len(got), bool(other), len(c...  12.2 us
    ppermute x4, starting transfers between devices, exchange(): got[k].append(lax.ppermute(blocks[j - 1], ('member', 'fsdp'), pairs))  10.8 us
    unnamed x31, local copies, waits for them, and re-layouts  7.89 us
    pallas_call x1, Pallas kernels, prepare(): pl.pallas_call(functools.partial(prepare_kernel, nh), out_shape=[turned,...  6.85 us
    ppermute x1, starting transfers between devices, weight_first(): arrived[1] = lax.ppermute(weight, ('groups', 'fsdp'), pairs)  6.03 us
  transfers between devices with their start and end apart: 25, of which 9 were waited for; matrix products, arithmetic and copies ran while one was open for 6% of the time, Pallas kernels for 45%

profile of v4, /device:TPU:0, one launch (start us, length us, event | category | flops | bytes accessed | tf_op | source)
XLA Modules:
  0.0 144.3 jit_solution(5353291564928796813)
XLA Ops:
  0.6 6.0 %collective-permute-start = (bf16[320,2048]{1,0:T(8,128)(2,1)}, bf16[320,2048]{1,0:T(8,128)(2,1)}, u32[]{:S(2)}, u32[]{:S(2)}) collective-permute-start(bf16[320,2048]{1,0:T(8,128)(2,1)} %refs_0_), channel_id=1, source_target_pairs={{0,2},{2,4},{3,1},{4,6},{5,3},{7,5},{17,18},{19,20},{18,17},{21,22... | collective-permute-start | bytes 3932168 | tf_op jit(solution)/shard_map/ppermute | solution.py:345
  6.7 1.5 %broadcast_in_dim.4.slot_ref.refs_10_.refs_8_ = s32[384,1]{1,0:T(8,128)} reshape(s32[384]{0:T(512)} %param.13) | data formatting | bytes 3072 | tf_op jit(solution)/shard_map/broadcast_in_dim | solution.py:311
  8.1 6.8 %shard_map.110 = (bf16[4,320,384]{2,1,0:T(8,128)(2,1)}, bf16[4,320,384]{2,1,0:T(8,128)(2,1)}, bf16[192,2048]{1,0:T(8,128)(2,1)}, bf16[192,2048]{1,0:T(8,128)(2,1)}) custom-call(bf16[384,2560]{1,0:T(8,128)(2,1)} %refs_5_.3, bf16[384,2560]{1,0:T(8,128)(2,1)} %refs_6_.5, f32[2,2560]{1,0:T(2,128)} %refs_7_.5, bf16[384,2048]{1,0:T(8,128)(2,1)} %refs_4_.3, ...), custom_call_target="tpu_custom_call" | custom-call | flops 1 | bytes 1 | tf_op jit(solution)/shard_map/pallas_call | solution.py:55
  16.7 4.3 %collective-permute-done = bf16[320,2048]{1,0:T(8,128)(2,1)} collective-permute-done((bf16[320,2048]{1,0:T(8,128)(2,1)}, bf16[320,2048]{1,0:T(8,128)(2,1)}, u32[]{:S(2)}, u32[]{:S(2)}) %collective-permute-start) | collective-permute-done | bytes 1310752 | tf_op jit(solution)/shard_map/ppermute | solution.py:345
  21.0 1.3 collective-permute-start.2
  24.5 5.5 %shard_map.112 = bf16[640,1024]{1,0:T(8,128)(2,1)} custom-call(s32[28]{0:T(128)} %stack.121.ids_ref, bf16[4,320,384]{2,1,0:T(8,128)(2,1)} %get-tuple-element.88.refs_0_.refs_4_, bf16[4,320,384]{2,1,0:T(8,128)(2,1)} %get-tuple-element.89.refs_1_.refs_5_, bf16[4,320,384]{2,1,0:T(8,128)(2,1)} %copy-done, bf16[4,320,384]{2,1,0:T(8,128)(2,1)} %copy-done.1, ...), custom_call_target="tpu_custom_call" | custom-call | flops 1 | bytes 1 | tf_op jit(solution)/shard_map/pallas_call | solution.py:129
  30.0 3.4 %collective-permute-start.7 = (bf16[640,1024]{1,0:T(8,128)(2,1)}, bf16[640,1024]{1,0:T(8,128)(2,1)}, u32[]{:S(2)}, u32[]{:S(2)}) collective-permute-start(bf16[640,1024]{1,0:T(8,128)(2,1)} %shard_map.112), channel_id=1, source_target_pairs={{8,0},{11,3},{12,4},{15,7},{0,8},{3,11},{4,12},{7,15},{24,16},{27,... | collective-permute-start | bytes 3932168 | tf_op jit(solution)/shard_map/ppermute | solution.py:462
  34.2 12.1 %shard_map.111 = (bf16[640,1024]{1,0:T(8,128)(2,1)}, bf16[640,1024]{1,0:T(8,128)(2,1)}, bf16[320,1024]{1,0:T(8,128)(2,1)}, bf16[640,1024]{1,0:T(8,128)(2,1)}, bf...) custom-call(s32[28]{0:T(128)} %stack.121.ids_ref, ...), custom_call_target="tpu_custom_call" | custom-call | flops 1 | bytes 1 | tf_op jit(solution)/shard_map/pallas_call | solution.py:129
  46.3 1.5 %broadcast_select_fusion.3.refs_2_ = bf16[320,2048]{1,0:T(8,128)(2,1)S(1)} fusion(bf16[320,2048]{1,0:T(8,128)(2,1)} %collective-permute-done, bf16[320,2048]{1,0:T(8,128)(2,1)} %collective-permute-done.2, pred[]{:T(512)S(6)} %eq.109), kind=kLoop, calls=%fused_computation.4 | loop fusion | flops 655360 | bytes 3932161 | tf_op jit(solution)/shard_map/jit(_where)/select_n | solution.py:380
  47.8 2.5 %collective-permute-start.11 = (bf16[320,2048]{1,0:T(8,128)(2,1)S(1)}, bf16[320,2048]{1,0:T(8,128)(2,1)}, u32[]{:S(2)}, u32[]{:S(2)}) collective-permute-start(bf16[320,2048]{1,0:T(8,128)(2,1)S(1)} %broadcast_select_fusion.3.refs_2_), channel_id=1, source_target_pairs={{0,1},{1,0},{2,3},{3,2},{4,5},{5,4},{6,7},{7,6},{8,9},{9,8},{10,11... | collective-permute-start | bytes 3932168 | tf_op jit(solution)/shard_map/ppermute | solution.py:327
  51.4 3.9 %shard_map.113 = bf16[320,2048]{1,0:T(8,128)(2,1)} custom-call(s32[28]{0:T(128)} %stack.121.ids_ref, bf16[640,1024]{1,0:T(8,128)(2,1)} %get-tuple-element.99.sum_ref, bf16[640,1024]{1,0:T(8,128)(2,1)} %collective-permute-done.7.refs_0_.refs_1_, bf16[320,2048]{1,0:T(8,128)(2,1)} %copy-done.7), custom_call_target="tpu_custom_call" | custom-call | flops 1 | bytes 1 | tf_op jit(solution)/shard_map/pallas_call | solution.py:164
  55.2 3.4 %collective-permute-start.9 = (bf16[640,1024]{1,0:T(8,128)(2,1)}, bf16[640,1024]{1,0:T(8,128)(2,1)}, u32[]{:S(2)}, u32[]{:S(2)}) collective-permute-start(bf16[640,1024]{1,0:T(8,128)(2,1)} %get-tuple-element.107), channel_id=1, source_target_pairs={{8,0},{10,2},{13,5},{15,7},{0,8},{2,10},{5,13},{7,15},{24,16},{26,... | collective-permute-start | bytes 3932168 | tf_op jit(solution)/shard_map/ppermute | solution.py:462
  58.6 8.2 %collective-permute-start.10 = (bf16[320,2048]{1,0:T(8,128)(2,1)}, bf16[320,2048]{1,0:T(8,128)(2,1)S(1)}, u32[]{:S(2)}, u32[]{:S(2)}) collective-permute-start(bf16[320,2048]{1,0:T(8,128)(2,1)} %shard_map.113), channel_id=1, source_target_pairs={{0,2},{4,6},{7,5},{3,1},{8,10},{12,14},{15,13},{11,9},{16,18},{20,... | collective-permute-start | bytes 3932168 | tf_op jit(solution)/shard_map/ppermute | solution.py:324
  66.9 1.3 collective-permute-start.14
  68.2 12.7 %shard_map.114 = (bf16[384,2560]{1,0:T(8,128)(2,1)}, bf16[384,2560]{1,0:T(8,128)(2,1)}, f32[2,2560]{1,0:T(2,128)}, f32[2,2048]{1,0:T(2,128)}) custom-call(s32[28]{0:T(128)} %stack.121.ids_ref, bf16[320,2048]{1,0:T(8,128)(2,1)} %refs_0_, bf16[320,2048]{1,0:T(8,128)(2,1)} %collective-permute-done.1.refs_1_, bf16[320,2048]{1,0:T(8,128)(2,1)} %copy-done.4, ...), custom_call_target="tpu_custom_call" | custom-call | flops 1 | bytes 1 | tf_op jit(solution)/shard_map/pallas_call | solution.py:273
  80.9 1.3 collective-permute-done.10.refs_1_
  83.3 4.0 %shard_map.115 = bf16[320,2048]{1,0:T(8,128)(2,1)} custom-call(s32[28]{0:T(128)} %stack.121.ids_ref, bf16[640,1024]{1,0:T(8,128)(2,1)} %get-tuple-element.105.sum_ref, bf16[640,1024]{1,0:T(8,128)(2,1)} %collective-permute-done.9.refs_0_, bf16[320,2048]{1,0:T(8,128)(2,1)} %copy-done.9), custom_call_target="tpu_custom_call" | custom-call | flops 1 | bytes 1 | tf_op jit(solution)/shard_map/pallas_call | solution.py:164
  87.2 3.4 %collective-permute-start.12 = (bf16[640,1024]{1,0:T(8,128)(2,1)}, bf16[640,1024]{1,0:T(8,128)(2,1)}, u32[]{:S(2)}, u32[]{:S(2)}) collective-permute-start(bf16[640,1024]{1,0:T(8,128)(2,1)} %get-tuple-element.123), channel_id=1, source_target_pairs={{8,0},{10,2},{13,5},{15,7},{0,8},{2,10},{5,13},{7,15},{24,16},{26,... | collective-permute-start | bytes 3932168 | tf_op jit(solution)/shard_map/ppermute | solution.py:462
  90.6 5.4 %collective-permute-start.13 = (bf16[320,2048]{1,0:T(8,128)(2,1)}, bf16[320,2048]{1,0:T(8,128)(2,1)}, u32[]{:S(2)}, u32[]{:S(2)}) collective-permute-start(bf16[320,2048]{1,0:T(8,128)(2,1)} %shard_map.115), channel_id=1, source_target_pairs={{0,2},{2,4},{5,3},{7,5},{8,10},{10,12},{13,11},{15,13},{16,18},{18... | collective-permute-start | bytes 3932168 | tf_op jit(solution)/shard_map/ppermute | solution.py:324
  96.1 1.6 %broadcast_select_fusion.2.refs_0_ = bf16[320,2048]{1,0:T(8,128)(2,1)S(1)} fusion(bf16[320,2048]{1,0:T(8,128)(2,1)S(1)} %copy-done.8, bf16[320,2048]{1,0:T(8,128)(2,1)} %collective-permute-done.14, pred[]{:T(512)S(6)} %eq.110), kind=kLoop, calls=%fused_computation.3 | loop fusion | flops 655360 | bytes 3932161 | tf_op jit(solution)/shard_map/jit(_where)/select_n | solution.py:380
  98.8 1.5 %collective-permute-start.16 = (bf16[320,2048]{1,0:T(8,128)(2,1)S(1)}, bf16[320,2048]{1,0:T(8,128)(2,1)}, u32[]{:S(2)}, u32[]{:S(2)}) collective-permute-start(bf16[320,2048]{1,0:T(8,128)(2,1)S(1)} %broadcast_select_fusion), channel_id=1, source_target_pairs={{1,16},{2,19},{5,20},{6,23},{17,0},{18,3},{21,4},{22,7},{9,24},{10... | collective-permute-start | bytes 3932168 | tf_op jit(solution)/shard_map/ppermute | solution.py:377
  101.8 8.1 %shard_map.116 = (bf16[384,2560]{1,0:T(8,128)(2,1)}, bf16[384,2560]{1,0:T(8,128)(2,1)}, f32[2,2560]{1,0:T(2,128)}, f32[2,2048]{1,0:T(2,128)}) custom-call(s32[28]{0:T(128)} %stack.121.ids_ref, bf16[320,2048]{1,0:T(8,128)(2,1)} %copy-done.6, bf16[320,2048]{1,0:T(8,128)(2,1)} %copy-done.11, ...), custom_call_target="tpu_custom_call", output_to_operand_aliasing={{0}: (10, {}), {1}: (11, {}), {2}: (12, {})} | custom-call | flops 1 | bytes 1 | tf_op jit(solution)/shard_map/pallas_call | solution.py:273
  110.4 4.3 %shard_map.117 = bf16[320,2048]{1,0:T(8,128)(2,1)} custom-call(s32[28]{0:T(128)} %stack.121.ids_ref, bf16[640,1024]{1,0:T(8,128)(2,1)} %get-tuple-element.121.sum_ref, bf16[640,1024]{1,0:T(8,128)(2,1)} %collective-permute-done.12.refs_0_, bf16[640,1024]{1,0:T(8,128)(2,1)} %collective-permute-done.7.refs_0_.refs_1_, ...), custom_call_target="tpu_custom_call" | custom-call | flops 1 | bytes 1 | tf_op jit(solution)/shard_map/pallas_call | solution.py:164
  114.7 3.2 %collective-permute-done.16 = bf16[320,2048]{1,0:T(8,128)(2,1)} collective-permute-done((bf16[320,2048]{1,0:T(8,128)(2,1)S(1)}, bf16[320,2048]{1,0:T(8,128)(2,1)}, u32[]{:S(2)}, u32[]{:S(2)}) %collective-permute-start.16) | collective-permute-done | bytes 1310752 | tf_op jit(solution)/shard_map/ppermute | solution.py:377
  117.8 1.5 %broadcast_select_fusion.1.refs_0_ = bf16[320,2048]{1,0:T(8,128)(2,1)S(1)} fusion(bf16[320,2048]{1,0:T(8,128)(2,1)S(1)} %broadcast_select_fusion, bf16[320,2048]{1,0:T(8,128)(2,1)} %collective-permute-done.16, pred[]{:T(512)S(6)} %eq.111), kind=kLoop, calls=%fused_computation.2 | loop fusion | flops 655360 | bytes 3932161 | tf_op jit(solution)/shard_map/jit(_where)/select_n | solution.py:380
  119.4 1.8 %collective-permute-start.19 = (bf16[320,2048]{1,0:T(8,128)(2,1)}, bf16[320,2048]{1,0:T(8,128)(2,1)S(1)}, u32[]{:S(2)}, u32[]{:S(2)}) collective-permute-start(bf16[320,2048]{1,0:T(8,128)(2,1)} %shard_map.117), channel_id=1, source_target_pairs={{0,2},{2,4},{4,6},{3,1},{5,3},{7,5},{8,10},{10,12},{12,14},{11,9},... | collective-permute-start | bytes 3932168 | tf_op jit(solution)/shard_map/ppermute | solution.py:324
  122.5 8.1 %shard_map.118 = (bf16[384,2560]{1,0:T(8,128)(2,1)}, bf16[384,2560]{1,0:T(8,128)(2,1)}, f32[2,2560]{1,0:T(2,128)}, f32[2,2048]{1,0:T(2,128)}) custom-call(s32[28]{0:T(128)} %stack.121.ids_ref, bf16[320,2048]{1,0:T(8,128)(2,1)} %copy-done.5, ...), custom_call_target="tpu_custom_call", output_to_operand_aliasing={{0}: (10, {}), {1}: (11, {}), {2}: (12, {})} | custom-call | flops 1 | bytes 1 | tf_op jit(solution)/shard_map/pallas_call | solution.py:273
  132.4 1.1 collective-permute-done.20
  133.6 2.0 %collective-permute-start.23 = (f32[2,4608]{1,0:T(2,128)S(1)}, f32[2,4608]{1,0:T(2,128)S(1)}, u32[]{:S(2)}, u32[]{:S(2)}) collective-permute-start(f32[2,4608]{1,0:T(2,128)S(1)} %add.135), channel_id=1, source_target_pairs={{6,0},{7,1},{0,2},{1,3},{2,4},{3,5},{4,6},{5,7},{14,8},{15,9},{8,1... | collective-permute-start | bytes 110600 | tf_op jit(solution)/shard_map/ppermute | solution.py:547
  136.0 2.1 %collective-permute-done.18 = bf16[320,1024]{1,0:T(8,128)(2,1)S(1)} collective-permute-done((bf16[320,1024]{1,0:T(8,128)(2,1)}, bf16[320,1024]{1,0:T(8,128)(2,1)S(1)}, u32[]{:S(2)}, u32[]{:S(2)}) %collective-permute-start.18) | collective-permute-done | bytes 655392 | tf_op jit(solution)/shard_map/ppermute | solution.py:462
  139.0 1.9 %collective-permute-start.22 = (bf16[320,1024]{1,0:T(8,128)(2,1)S(1)}, bf16[320,1024]{1,0:T(8,128)(2,1)S(1)}, u32[]{:S(2)}, u32[]{:S(2)}) collective-permute-start(bf16[320,1024]{1,0:T(8,128)(2,1)S(1)} %broadcast_select_fusion.4), channel_id=1, source_target_pairs={{0,1},{1,0},{2,3},{3,2},{4,5},{5,4},{6,7},{7,6},{8,9},{9,8},{10,11... | collective-permute-start | bytes 1966088 | tf_op jit(solution)/shard_map/ppermute | solution.py:564
  142.7 1.6 %convert_add_fusion = f32[320,1024]{1,0:T(8,128)} fusion(bf16[320,1024]{1,0:T(8,128)(2,1)S(1)} %collective-permute-done.22, f32[320,1024]{1,0:T(8,128)S(1)} %copy-done.12, bf16[320,1024]{1,0:T(8,128)(2,1)S(1)} %copy-done.14, pred[]{:T(512)S(6)} %lt.30, bf16[320,2048]{1,0:T(8,128)(2,1)S(1)} %collective-permute-done.19), kind=kLoop, calls=%fused_computation | loop fusion | flops 2293760 | bytes 5242881 | tf_op jit(solution)/shard_map/add | solution.py:570
  (71 shorter events, 16.0 us)
Async XLA Ops:
  0.6 20.4 %collective-permute-start = (bf16[320,2048]{1,0:T(8,128)(2,1)}, bf16[320,2048]{1,0:T(8,128)(2,1)}, u32[]{:S(2)}, u32[]{:S(2)}) collective-permute-start(bf16[320,2048]{1,0:T(8,128)(2,1)} %refs_0_), channel_id=1, source_target_pairs={{0,2},{2,4},{3,1},{4,6},{5,3},{7,5},{17,18},{19,20},{18,17},{21,22... | collective-permute-start | bytes 3932168 | tf_op jit(solution)/shard_map/ppermute | solution.py:345
  15.0 6.0 %collective-permute-start.5 = (bf16[192,2048]{1,0:T(8,128)(2,1)}, bf16[192,2048]{1,0:T(8,128)(2,1)S(1)}, u32[]{:S(2)}, u32[]{:S(2)}) collective-permute-start(bf16[192,2048]{1,0:T(8,128)(2,1)} %get-tuple-element.90.refs_8_.refs_12_.refs_4_.refs_2_), channel_id=1, source_target_pairs={{0,1},{1,0},{2,3},{3,2},{4,5},{5,4},{6,7},{7,6},{8,9},{9,8},{10,11... | collective-permute-start | bytes 2359304 | tf_op jit(solution)/shard_map/ppermute | solution.py:327
  15.0 7.3 %collective-permute-start.3 = (bf16[4,320,384]{2,1,0:T(8,128)(2,1)}, bf16[4,320,384]{2,1,0:T(8,128)(2,1)S(1)}, u32[]{:S(2)}, u32[]{:S(2)}) collective-permute-start(bf16[4,320,384]{2,1,0:T(8,128)(2,1)} %get-tuple-element.88.refs_0_.refs_4_), channel_id=1, source_target_pairs={{0,1},{1,0},{2,3},{3,2},{4,5},{5,4},{6,7},{7,6},{8,9},{9,8},{10,11... | collective-permute-start | bytes 2949128 | tf_op jit(solution)/shard_map/ppermute | solution.py:327
  15.5 6.8 %collective-permute-start.4 = (bf16[4,320,384]{2,1,0:T(8,128)(2,1)}, bf16[4,320,384]{2,1,0:T(8,128)(2,1)S(1)}, u32[]{:S(2)}, u32[]{:S(2)}) collective-permute-start(bf16[4,320,384]{2,1,0:T(8,128)(2,1)} %get-tuple-element.89.refs_1_.refs_5_), channel_id=1, source_target_pairs={{0,1},{1,0},{2,3},{3,2},{4,5},{5,4},{6,7},{7,6},{8,9},{9,8},{10,11... | collective-permute-start | bytes 2949128 | tf_op jit(solution)/shard_map/ppermute | solution.py:327
  15.6 6.7 %collective-permute-start.6 = (bf16[192,2048]{1,0:T(8,128)(2,1)}, bf16[192,2048]{1,0:T(8,128)(2,1)S(1)}, u32[]{:S(2)}, u32[]{:S(2)}) collective-permute-start(bf16[192,2048]{1,0:T(8,128)(2,1)} %get-tuple-element.91.refs_9_.refs_13_.refs_5_.refs_3_), channel_id=1, source_target_pairs={{0,1},{1,0},{2,3},{3,2},{4,5},{5,4},{6,7},{7,6},{8,9},{9,8},{10,11... | collective-permute-start | bytes 2359304 | tf_op jit(solution)/shard_map/ppermute | solution.py:327
  21.0 13.2 %collective-permute-start.1 = (bf16[320,2048]{1,0:T(8,128)(2,1)}, bf16[320,2048]{1,0:T(8,128)(2,1)}, u32[]{:S(2)}, u32[]{:S(2)}) collective-permute-start(bf16[320,2048]{1,0:T(8,128)(2,1)} %refs_0_), channel_id=1, source_target_pairs={{0,1},{1,0},{2,3},{3,2},{4,5},{5,4},{6,7},{7,6},{8,9},{9,8},{10,11... | collective-permute-start | bytes 3932168 | tf_op jit(solution)/shard_map/ppermute | solution.py:327
  21.0 1.4 copy-start.2
  21.0 25.3 %collective-permute-start.2 = (bf16[320,2048]{1,0:T(8,128)(2,1)}, bf16[320,2048]{1,0:T(8,128)(2,1)}, u32[]{:S(2)}, u32[]{:S(2)}) collective-permute-start(bf16[320,2048]{1,0:T(8,128)(2,1)} %collective-permute-done), channel_id=1, source_target_pairs={{1,16},{3,18},{4,21},{6,23},{17,0},{19,2},{20,5},{22,7},{9,24},{11... | collective-permute-start | bytes 3932168 | tf_op jit(solution)/shard_map/ppermute | solution.py:377
  30.0 20.3 %collective-permute-start.7 = (bf16[640,1024]{1,0:T(8,128)(2,1)}, bf16[640,1024]{1,0:T(8,128)(2,1)}, u32[]{:S(2)}, u32[]{:S(2)}) collective-permute-start(bf16[640,1024]{1,0:T(8,128)(2,1)} %shard_map.112), channel_id=1, source_target_pairs={{8,0},{11,3},{12,4},{15,7},{0,8},{3,11},{4,12},{7,15},{24,16},{27,... | collective-permute-start | bytes 3932168 | tf_op jit(solution)/shard_map/ppermute | solution.py:462
  33.4 16.9 %collective-permute-start.8 = (bf16[320,2048]{1,0:T(8,128)(2,1)}, bf16[320,2048]{1,0:T(8,128)(2,1)S(1)}, u32[]{:S(2)}, u32[]{:S(2)}) collective-permute-start(bf16[320,2048]{1,0:T(8,128)(2,1)} %collective-permute-done), channel_id=1, source_target_pairs={{2,4},{4,6},{3,1},{5,3},{10,12},{12,14},{11,9},{13,11},{18,20},{20... | collective-permute-start | bytes 3932168 | tf_op jit(solution)/shard_map/ppermute | solution.py:324
  47.8 7.4 %copy-start.4 = (bf16[320,2048]{1,0:T(8,128)(2,1)}, bf16[320,2048]{1,0:T(8,128)(2,1)S(1)}, u32[]{:S(2)}) copy-start(bf16[320,2048]{1,0:T(8,128)(2,1)S(1)} %broadcast_select_fusion.3.refs_2_) | copy-start | bytes 3932164
  47.8 20.4 %collective-permute-start.11 = (bf16[320,2048]{1,0:T(8,128)(2,1)S(1)}, bf16[320,2048]{1,0:T(8,128)(2,1)}, u32[]{:S(2)}, u32[]{:S(2)}) collective-permute-start(bf16[320,2048]{1,0:T(8,128)(2,1)S(1)} %broadcast_select_fusion.3.refs_2_), channel_id=1, source_target_pairs={{0,1},{1,0},{2,3},{3,2},{4,5},{5,4},{6,7},{7,6},{8,9},{9,8},{10,11... | collective-permute-start | bytes 3932168 | tf_op jit(solution)/shard_map/ppermute | solution.py:327
  55.2 25.7 %collective-permute-start.9 = (bf16[640,1024]{1,0:T(8,128)(2,1)}, bf16[640,1024]{1,0:T(8,128)(2,1)}, u32[]{:S(2)}, u32[]{:S(2)}) collective-permute-start(bf16[640,1024]{1,0:T(8,128)(2,1)} %get-tuple-element.107), channel_id=1, source_target_pairs={{8,0},{10,2},{13,5},{15,7},{0,8},{2,10},{5,13},{7,15},{24,16},{26,... | collective-permute-start | bytes 3932168 | tf_op jit(solution)/shard_map/ppermute | solution.py:462
  58.6 23.6 %collective-permute-start.10 = (bf16[320,2048]{1,0:T(8,128)(2,1)}, bf16[320,2048]{1,0:T(8,128)(2,1)S(1)}, u32[]{:S(2)}, u32[]{:S(2)}) collective-permute-start(bf16[320,2048]{1,0:T(8,128)(2,1)} %shard_map.113), channel_id=1, source_target_pairs={{0,2},{4,6},{7,5},{3,1},{8,10},{12,14},{15,13},{11,9},{16,18},{20,... | collective-permute-start | bytes 3932168 | tf_op jit(solution)/shard_map/ppermute | solution.py:324
  66.9 29.2 %collective-permute-start.14 = (bf16[320,2048]{1,0:T(8,128)(2,1)}, bf16[320,2048]{1,0:T(8,128)(2,1)}, u32[]{:S(2)}, u32[]{:S(2)}) collective-permute-start(bf16[320,2048]{1,0:T(8,128)(2,1)} %copy-done.7), channel_id=1, source_target_pairs={{1,16},{3,18},{4,21},{6,23},{17,0},{19,2},{20,5},{22,7},{9,24},{11... | collective-permute-start | bytes 3932168 | tf_op jit(solution)/shard_map/ppermute | solution.py:377
  83.3 12.8 %copy-start.8 = (bf16[320,2048]{1,0:T(8,128)(2,1)S(1)}, bf16[320,2048]{1,0:T(8,128)(2,1)}, u32[]{:S(2)}) copy-start(bf16[320,2048]{1,0:T(8,128)(2,1)} %copy-done.7) | copy-start | bytes 3932164
  87.2 22.7 %collective-permute-start.12 = (bf16[640,1024]{1,0:T(8,128)(2,1)}, bf16[640,1024]{1,0:T(8,128)(2,1)}, u32[]{:S(2)}, u32[]{:S(2)}) collective-permute-start(bf16[640,1024]{1,0:T(8,128)(2,1)} %get-tuple-element.123), channel_id=1, source_target_pairs={{8,0},{10,2},{13,5},{15,7},{0,8},{2,10},{5,13},{7,15},{24,16},{26,... | collective-permute-start | bytes 3932168 | tf_op jit(solution)/shard_map/ppermute | solution.py:462
  90.6 19.7 %collective-permute-start.13 = (bf16[320,2048]{1,0:T(8,128)(2,1)}, bf16[320,2048]{1,0:T(8,128)(2,1)}, u32[]{:S(2)}, u32[]{:S(2)}) collective-permute-start(bf16[320,2048]{1,0:T(8,128)(2,1)} %shard_map.115), channel_id=1, source_target_pairs={{0,2},{2,4},{5,3},{7,5},{8,10},{10,12},{13,11},{15,13},{16,18},{18... | collective-permute-start | bytes 3932168 | tf_op jit(solution)/shard_map/ppermute | solution.py:324
  96.1 1.7 %copy-start.10 = (bf16[320,2048]{1,0:T(8,128)(2,1)S(1)}, bf16[320,2048]{1,0:T(8,128)(2,1)}, u32[]{:S(2)}) copy-start(bf16[320,2048]{1,0:T(8,128)(2,1)} %copy-done.9) | copy-start | bytes 3932164
  97.7 3.1 %collective-permute-start.15 = (bf16[320,2048]{1,0:T(8,128)(2,1)S(1)}, bf16[320,2048]{1,0:T(8,128)(2,1)S(1)}, u32[]{:S(2)}, u32[]{:S(2)}) collective-permute-start(bf16[320,2048]{1,0:T(8,128)(2,1)S(1)} %broadcast_select_fusion.2.refs_0_), channel_id=1, source_target_pairs={{0,1},{1,0},{2,3},{3,2},{4,5},{5,4},{6,7},{7,6},{8,9},{9,8},{10,11... | collective-permute-start | bytes 3932168 | tf_op jit(solution)/shard_map/ppermute | solution.py:327
  98.8 19.0 %collective-permute-start.16 = (bf16[320,2048]{1,0:T(8,128)(2,1)S(1)}, bf16[320,2048]{1,0:T(8,128)(2,1)}, u32[]{:S(2)}, u32[]{:S(2)}) collective-permute-start(bf16[320,2048]{1,0:T(8,128)(2,1)S(1)} %broadcast_select_fusion), channel_id=1, source_target_pairs={{1,16},{2,19},{5,20},{6,23},{17,0},{18,3},{21,4},{22,7},{9,24},{10... | collective-permute-start | bytes 3932168 | tf_op jit(solution)/shard_map/ppermute | solution.py:377
  119.3 3.2 %copy-start.5 = (bf16[320,2048]{1,0:T(8,128)(2,1)}, bf16[320,2048]{1,0:T(8,128)(2,1)S(1)}, u32[]{:S(2)}) copy-start(bf16[320,2048]{1,0:T(8,128)(2,1)S(1)} %broadcast_select_fusion.1.refs_0_) | copy-start | bytes 3932164
  119.3 3.2 %collective-permute-start.17 = (bf16[320,2048]{1,0:T(8,128)(2,1)S(1)}, bf16[320,2048]{1,0:T(8,128)(2,1)}, u32[]{:S(2)}, u32[]{:S(2)}) collective-permute-start(bf16[320,2048]{1,0:T(8,128)(2,1)S(1)} %broadcast_select_fusion.1.refs_0_), channel_id=1, source_target_pairs={{0,1},{1,0},{2,3},{3,2},{4,5},{5,4},{6,7},{7,6},{8,9},{9,8},{10,11... | collective-permute-start | bytes 3932168 | tf_op jit(solution)/shard_map/ppermute | solution.py:327
  119.4 18.7 %collective-permute-start.19 = (bf16[320,2048]{1,0:T(8,128)(2,1)}, bf16[320,2048]{1,0:T(8,128)(2,1)S(1)}, u32[]{:S(2)}, u32[]{:S(2)}) collective-permute-start(bf16[320,2048]{1,0:T(8,128)(2,1)} %shard_map.117), channel_id=1, source_target_pairs={{0,2},{2,4},{4,6},{3,1},{5,3},{7,5},{8,10},{10,12},{12,14},{11,9},... | collective-permute-start | bytes 3932168 | tf_op jit(solution)/shard_map/ppermute | solution.py:324
  121.2 16.9 %collective-permute-start.18 = (bf16[320,1024]{1,0:T(8,128)(2,1)}, bf16[320,1024]{1,0:T(8,128)(2,1)S(1)}, u32[]{:S(2)}, u32[]{:S(2)}) collective-permute-start(bf16[320,1024]{1,0:T(8,128)(2,1)} %get-tuple-element.158), channel_id=1, source_target_pairs={{8,0},{9,1},{10,2},{11,3},{12,4},{13,5},{14,6},{15,7},{0,8},{1,9},... | collective-permute-start | bytes 1966088 | tf_op jit(solution)/shard_map/ppermute | solution.py:462
  130.7 12.0 %copy-start.12 = (f32[320,1024]{1,0:T(8,128)S(1)}, f32[320,1024]{1,0:T(8,128)}, u32[]{:S(2)}) copy-start(f32[320,1024]{1,0:T(8,128)} %get-tuple-element.157) | copy-start | bytes 3932164
  132.3 1.2 collective-permute-start.20
  133.5 5.4 %collective-permute-start.21 = (f32[2,4608]{1,0:T(2,128)S(1)}, f32[2,4608]{1,0:T(2,128)S(1)}, u32[]{:S(2)}, u32[]{:S(2)}) collective-permute-start(f32[2,4608]{1,0:T(2,128)S(1)} %add.135), channel_id=1, source_target_pairs={{2,0},{3,1},{4,2},{5,3},{6,4},{7,5},{0,6},{1,7},{10,8},{11,9},{12,... | collective-permute-start | bytes 110600 | tf_op jit(solution)/shard_map/ppermute | solution.py:547
  133.6 7.3 %collective-permute-start.23 = (f32[2,4608]{1,0:T(2,128)S(1)}, f32[2,4608]{1,0:T(2,128)S(1)}, u32[]{:S(2)}, u32[]{:S(2)}) collective-permute-start(f32[2,4608]{1,0:T(2,128)S(1)} %add.135), channel_id=1, source_target_pairs={{6,0},{7,1},{0,2},{1,3},{2,4},{3,5},{4,6},{5,7},{14,8},{15,9},{8,1... | collective-permute-start | bytes 110600 | tf_op jit(solution)/shard_map/ppermute | solution.py:547
  135.6 5.4 %collective-permute-start.24 = (f32[2,4608]{1,0:T(2,128)S(1)}, f32[2,4608]{1,0:T(2,128)S(1)}, u32[]{:S(2)}, u32[]{:S(2)}) collective-permute-start(f32[2,4608]{1,0:T(2,128)S(1)} %add.135), channel_id=1, source_target_pairs={{4,0},{5,1},{6,2},{7,3},{0,4},{1,5},{2,6},{3,7},{12,8},{13,9},{14,... | collective-permute-start | bytes 110600 | tf_op jit(solution)/shard_map/ppermute | solution.py:547
  138.9 3.7 %copy-start.14 = (bf16[320,1024]{1,0:T(8,128)(2,1)S(1)}, bf16[320,1024]{1,0:T(8,128)(2,1)}, u32[]{:S(2)}) copy-start(bf16[320,1024]{1,0:T(8,128)(2,1)} %copy-done.13) | copy-start | bytes 1966084
  139.0 3.7 %collective-permute-start.22 = (bf16[320,1024]{1,0:T(8,128)(2,1)S(1)}, bf16[320,1024]{1,0:T(8,128)(2,1)S(1)}, u32[]{:S(2)}, u32[]{:S(2)}) collective-permute-start(bf16[320,1024]{1,0:T(8,128)(2,1)S(1)} %broadcast_select_fusion.4), channel_id=1, source_target_pairs={{0,1},{1,0},{2,3},{3,2},{4,5},{5,4},{6,7},{7,6},{8,9},{9,8},{10,11... | collective-permute-start | bytes 1966088 | tf_op jit(solution)/shard_map/ppermute | solution.py:564
  (8 other events, 8.3 us)

commit v5 on v4

--- a/solution.py
+++ b/solution.py
@@ -100,9 +100,9 @@
     line, part, tokens = lefts[0][0].shape
     shard = part // (lo // 2)
     width = rights[0][0].shape[1] // members
-    tile = max(width // 4, 128)
+    single = len({row for row, _, _ in items}) == 1
+    tile = max(width // (2 if single else 4), 128)
     tiles = width // tile
-    single = len({row for row, _, _ in items}) == 1
     if single:
         row = items[0][0]
         left_spec = pl.BlockSpec((1, shard, tokens), lambda i, ids: (ids[row], ids[at["half"]], 0))

time: 145 us -> 144 us (level)
  no operation moved by 1% of the time
where the time goes in v5:
time: 144 us; the launch traced here: 143 us
  Pallas kernels  64.6 us (45%)
  starting transfers between devices  45.3 us (31%)
  waiting for transfers between devices  14 us (10%)
  local copies, waits for them, and re-layouts  11.9 us (8%)
  other arithmetic  6.43 us (4%)
    pallas_call x3, Pallas kernels, weight_slots(): pl.pallas_call(functools.partial(slot_kernel, n, lo, kept is not None, ba...  29 us
    pallas_call x2, Pallas kernels, partials(): pl.pallas_call(functools.partial(partials_kernel, lo, items, len(column_a...  16.7 us
    ppermute x4, starting transfers between devices, line_step(): return lax.ppermute(x, 'fsdp', pairs)  16.2 us
    pallas_call x3, Pallas kernels, hop(): pl.pallas_call(functools.partial(hop_kernel, len(got), bool(other), len(c...  12.2 us
    ppermute x4, starting transfers between devices, exchange(): got[k].append(lax.ppermute(blocks[j - 1], ('member', 'fsdp'), pairs))  10.8 us
    unnamed x31, local copies, waits for them, and re-layouts  7.89 us
    pallas_call x1, Pallas kernels, prepare(): pl.pallas_call(functools.partial(prepare_kernel, nh), out_shape=[turned,...  6.85 us
    ppermute x1, starting transfers between devices, weight_first(): arrived[1] = lax.ppermute(weight, ('groups', 'fsdp'), pairs)  6.03 us
  transfers between devices with their start and end apart: 25, of which 9 were waited for; matrix products, arithmetic and copies ran while one was open for 6% of the time, Pallas kernels for 45%

profile of v5, /device:TPU:0, one launch (start us, length us, event | category | flops | bytes accessed | tf_op | source)
XLA Modules:
  0.0 143.3 jit_solution(11114460614002070835)
XLA Ops:
  0.6 6.0 %collective-permute-start = (bf16[320,2048]{1,0:T(8,128)(2,1)}, bf16[320,2048]{1,0:T(8,128)(2,1)}, u32[]{:S(2)}, u32[]{:S(2)}) collective-permute-start(bf16[320,2048]{1,0:T(8,128)(2,1)} %refs_0_), channel_id=1, source_target_pairs={{0,2},{2,4},{3,1},{4,6},{5,3},{7,5},{17,18},{19,20},{18,17},{21,22... | collective-permute-start | bytes 3932168 | tf_op jit(solution)/shard_map/ppermute | solution.py:345
  6.7 1.5 %broadcast_in_dim.4.slot_ref.refs_10_.refs_8_ = s32[384,1]{1,0:T(8,128)} reshape(s32[384]{0:T(512)} %param.13) | data formatting | bytes 3072 | tf_op jit(solution)/shard_map/broadcast_in_dim | solution.py:311
  8.1 6.8 %shard_map.110 = (bf16[4,320,384]{2,1,0:T(8,128)(2,1)}, bf16[4,320,384]{2,1,0:T(8,128)(2,1)}, bf16[192,2048]{1,0:T(8,128)(2,1)}, bf16[192,2048]{1,0:T(8,128)(2,1)}) custom-call(bf16[384,2560]{1,0:T(8,128)(2,1)} %refs_5_.3, bf16[384,2560]{1,0:T(8,128)(2,1)} %refs_6_.5, f32[2,2560]{1,0:T(2,128)} %refs_7_.5, bf16[384,2048]{1,0:T(8,128)(2,1)} %refs_4_.3, ...), custom_call_target="tpu_custom_call" | custom-call | flops 1 | bytes 1 | tf_op jit(solution)/shard_map/pallas_call | solution.py:55
  16.7 4.3 %collective-permute-done = bf16[320,2048]{1,0:T(8,128)(2,1)} collective-permute-done((bf16[320,2048]{1,0:T(8,128)(2,1)}, bf16[320,2048]{1,0:T(8,128)(2,1)}, u32[]{:S(2)}, u32[]{:S(2)}) %collective-permute-start) | collective-permute-done | bytes 1310752 | tf_op jit(solution)/shard_map/ppermute | solution.py:345
  21.0 1.3 collective-permute-start.2
  24.5 4.6 %shard_map.112 = bf16[640,1024]{1,0:T(8,128)(2,1)} custom-call(s32[28]{0:T(128)} %stack.121.ids_ref, bf16[4,320,384]{2,1,0:T(8,128)(2,1)} %get-tuple-element.88.refs_0_.refs_4_, bf16[4,320,384]{2,1,0:T(8,128)(2,1)} %get-tuple-element.89.refs_1_.refs_5_, bf16[4,320,384]{2,1,0:T(8,128)(2,1)} %copy-done, bf16[4,320,384]{2,1,0:T(8,128)(2,1)} %copy-done.1, ...), custom_call_target="tpu_custom_call" | custom-call | flops 1 | bytes 1 | tf_op jit(solution)/shard_map/pallas_call | solution.py:129
  29.1 3.4 %collective-permute-start.7 = (bf16[640,1024]{1,0:T(8,128)(2,1)}, bf16[640,1024]{1,0:T(8,128)(2,1)}, u32[]{:S(2)}, u32[]{:S(2)}) collective-permute-start(bf16[640,1024]{1,0:T(8,128)(2,1)} %shard_map.112), channel_id=1, source_target_pairs={{8,0},{11,3},{12,4},{15,7},{0,8},{3,11},{4,12},{7,15},{24,16},{27,... | collective-permute-start | bytes 3932168 | tf_op jit(solution)/shard_map/ppermute | solution.py:462
  33.2 12.1 %shard_map.111 = (bf16[640,1024]{1,0:T(8,128)(2,1)}, bf16[640,1024]{1,0:T(8,128)(2,1)}, bf16[320,1024]{1,0:T(8,128)(2,1)}, bf16[640,1024]{1,0:T(8,128)(2,1)}, bf...) custom-call(s32[28]{0:T(128)} %stack.121.ids_ref, ...), custom_call_target="tpu_custom_call" | custom-call | flops 1 | bytes 1 | tf_op jit(solution)/shard_map/pallas_call | solution.py:129
  45.4 1.5 %broadcast_select_fusion.3.refs_2_ = bf16[320,2048]{1,0:T(8,128)(2,1)S(1)} fusion(bf16[320,2048]{1,0:T(8,128)(2,1)} %collective-permute-done, bf16[320,2048]{1,0:T(8,128)(2,1)} %collective-permute-done.2, pred[]{:T(512)S(6)} %eq.109), kind=kLoop, calls=%fused_computation.4 | loop fusion | flops 655360 | bytes 3932161 | tf_op jit(solution)/shard_map/jit(_where)/select_n | solution.py:380
  46.8 2.5 %collective-permute-start.11 = (bf16[320,2048]{1,0:T(8,128)(2,1)S(1)}, bf16[320,2048]{1,0:T(8,128)(2,1)}, u32[]{:S(2)}, u32[]{:S(2)}) collective-permute-start(bf16[320,2048]{1,0:T(8,128)(2,1)S(1)} %broadcast_select_fusion.3.refs_2_), channel_id=1, source_target_pairs={{0,1},{1,0},{2,3},{3,2},{4,5},{5,4},{6,7},{7,6},{8,9},{9,8},{10,11... | collective-permute-start | bytes 3932168 | tf_op jit(solution)/shard_map/ppermute | solution.py:327
  50.4 3.9 %shard_map.113 = bf16[320,2048]{1,0:T(8,128)(2,1)} custom-call(s32[28]{0:T(128)} %stack.121.ids_ref, bf16[640,1024]{1,0:T(8,128)(2,1)} %get-tuple-element.99.sum_ref, bf16[640,1024]{1,0:T(8,128)(2,1)} %collective-permute-done.7.refs_0_.refs_1_, bf16[320,2048]{1,0:T(8,128)(2,1)} %copy-done.7), custom_call_target="tpu_custom_call" | custom-call | flops 1 | bytes 1 | tf_op jit(solution)/shard_map/pallas_call | solution.py:164
  54.3 3.4 %collective-permute-start.9 = (bf16[640,1024]{1,0:T(8,128)(2,1)}, bf16[640,1024]{1,0:T(8,128)(2,1)}, u32[]{:S(2)}, u32[]{:S(2)}) collective-permute-start(bf16[640,1024]{1,0:T(8,128)(2,1)} %get-tuple-element.107), channel_id=1, source_target_pairs={{8,0},{10,2},{13,5},{15,7},{0,8},{2,10},{5,13},{7,15},{24,16},{26,... | collective-permute-start | bytes 3932168 | tf_op jit(solution)/shard_map/ppermute | solution.py:462
  57.7 8.2 %collective-permute-start.10 = (bf16[320,2048]{1,0:T(8,128)(2,1)}, bf16[320,2048]{1,0:T(8,128)(2,1)S(1)}, u32[]{:S(2)}, u32[]{:S(2)}) collective-permute-start(bf16[320,2048]{1,0:T(8,128)(2,1)} %shard_map.113), channel_id=1, source_target_pairs={{0,2},{4,6},{7,5},{3,1},{8,10},{12,14},{15,13},{11,9},{16,18},{20,... | collective-permute-start | bytes 3932168 | tf_op jit(solution)/shard_map/ppermute | solution.py:324
  65.9 1.3 collective-permute-start.14
  67.3 12.7 %shard_map.114 = (bf16[384,2560]{1,0:T(8,128)(2,1)}, bf16[384,2560]{1,0:T(8,128)(2,1)}, f32[2,2560]{1,0:T(2,128)}, f32[2,2048]{1,0:T(2,128)}) custom-call(s32[28]{0:T(128)} %stack.121.ids_ref, bf16[320,2048]{1,0:T(8,128)(2,1)} %refs_0_, bf16[320,2048]{1,0:T(8,128)(2,1)} %collective-permute-done.1.refs_1_, bf16[320,2048]{1,0:T(8,128)(2,1)} %copy-done.4, ...), custom_call_target="tpu_custom_call" | custom-call | flops 1 | bytes 1 | tf_op jit(solution)/shard_map/pallas_call | solution.py:273
  80.0 1.3 collective-permute-done.10.refs_1_
  82.3 4.0 %shard_map.115 = bf16[320,2048]{1,0:T(8,128)(2,1)} custom-call(s32[28]{0:T(128)} %stack.121.ids_ref, bf16[640,1024]{1,0:T(8,128)(2,1)} %get-tuple-element.105.sum_ref, bf16[640,1024]{1,0:T(8,128)(2,1)} %collective-permute-done.9.refs_0_, bf16[320,2048]{1,0:T(8,128)(2,1)} %copy-done.9), custom_call_target="tpu_custom_call" | custom-call | flops 1 | bytes 1 | tf_op jit(solution)/shard_map/pallas_call | solution.py:164
  86.3 3.4 %collective-permute-start.12 = (bf16[640,1024]{1,0:T(8,128)(2,1)}, bf16[640,1024]{1,0:T(8,128)(2,1)}, u32[]{:S(2)}, u32[]{:S(2)}) collective-permute-start(bf16[640,1024]{1,0:T(8,128)(2,1)} %get-tuple-element.123), channel_id=1, source_target_pairs={{8,0},{10,2},{13,5},{15,7},{0,8},{2,10},{5,13},{7,15},{24,16},{26,... | collective-permute-start | bytes 3932168 | tf_op jit(solution)/shard_map/ppermute | solution.py:462
  89.7 5.4 %collective-permute-start.13 = (bf16[320,2048]{1,0:T(8,128)(2,1)}, bf16[320,2048]{1,0:T(8,128)(2,1)}, u32[]{:S(2)}, u32[]{:S(2)}) collective-permute-start(bf16[320,2048]{1,0:T(8,128)(2,1)} %shard_map.115), channel_id=1, source_target_pairs={{0,2},{2,4},{5,3},{7,5},{8,10},{10,12},{13,11},{15,13},{16,18},{18... | collective-permute-start | bytes 3932168 | tf_op jit(solution)/shard_map/ppermute | solution.py:324
  95.2 1.6 %broadcast_select_fusion.2.refs_0_ = bf16[320,2048]{1,0:T(8,128)(2,1)S(1)} fusion(bf16[320,2048]{1,0:T(8,128)(2,1)S(1)} %copy-done.8, bf16[320,2048]{1,0:T(8,128)(2,1)} %collective-permute-done.14, pred[]{:T(512)S(6)} %eq.110), kind=kLoop, calls=%fused_computation.3 | loop fusion | flops 655360 | bytes 3932161 | tf_op jit(solution)/shard_map/jit(_where)/select_n | solution.py:380
  97.9 1.5 %collective-permute-start.16 = (bf16[320,2048]{1,0:T(8,128)(2,1)S(1)}, bf16[320,2048]{1,0:T(8,128)(2,1)}, u32[]{:S(2)}, u32[]{:S(2)}) collective-permute-start(bf16[320,2048]{1,0:T(8,128)(2,1)S(1)} %broadcast_select_fusion), channel_id=1, source_target_pairs={{1,16},{2,19},{5,20},{6,23},{17,0},{18,3},{21,4},{22,7},{9,24},{10... | collective-permute-start | bytes 3932168 | tf_op jit(solution)/shard_map/ppermute | solution.py:377
  100.9 8.1 %shard_map.116 = (bf16[384,2560]{1,0:T(8,128)(2,1)}, bf16[384,2560]{1,0:T(8,128)(2,1)}, f32[2,2560]{1,0:T(2,128)}, f32[2,2048]{1,0:T(2,128)}) custom-call(s32[28]{0:T(128)} %stack.121.ids_ref, bf16[320,2048]{1,0:T(8,128)(2,1)} %copy-done.6, bf16[320,2048]{1,0:T(8,128)(2,1)} %copy-done.11, ...), custom_call_target="tpu_custom_call", output_to_operand_aliasing={{0}: (10, {}), {1}: (11, {}), {2}: (12, {})} | custom-call | flops 1 | bytes 1 | tf_op jit(solution)/shard_map/pallas_call | solution.py:273
  109.4 4.3 %shard_map.117 = bf16[320,2048]{1,0:T(8,128)(2,1)} custom-call(s32[28]{0:T(128)} %stack.121.ids_ref, bf16[640,1024]{1,0:T(8,128)(2,1)} %get-tuple-element.121.sum_ref, bf16[640,1024]{1,0:T(8,128)(2,1)} %collective-permute-done.12.refs_0_, bf16[640,1024]{1,0:T(8,128)(2,1)} %collective-permute-done.7.refs_0_.refs_1_, ...), custom_call_target="tpu_custom_call" | custom-call | flops 1 | bytes 1 | tf_op jit(solution)/shard_map/pallas_call | solution.py:164
  113.7 3.2 %collective-permute-done.16 = bf16[320,2048]{1,0:T(8,128)(2,1)} collective-permute-done((bf16[320,2048]{1,0:T(8,128)(2,1)S(1)}, bf16[320,2048]{1,0:T(8,128)(2,1)}, u32[]{:S(2)}, u32[]{:S(2)}) %collective-permute-start.16) | collective-permute-done | bytes 1310752 | tf_op jit(solution)/shard_map/ppermute | solution.py:377
  116.9 1.5 %broadcast_select_fusion.1.refs_0_ = bf16[320,2048]{1,0:T(8,128)(2,1)S(1)} fusion(bf16[320,2048]{1,0:T(8,128)(2,1)S(1)} %broadcast_select_fusion, bf16[320,2048]{1,0:T(8,128)(2,1)} %collective-permute-done.16, pred[]{:T(512)S(6)} %eq.111), kind=kLoop, calls=%fused_computation.2 | loop fusion | flops 655360 | bytes 3932161 | tf_op jit(solution)/shard_map/jit(_where)/select_n | solution.py:380
  118.4 1.8 %collective-permute-start.19 = (bf16[320,2048]{1,0:T(8,128)(2,1)}, bf16[320,2048]{1,0:T(8,128)(2,1)S(1)}, u32[]{:S(2)}, u32[]{:S(2)}) collective-permute-start(bf16[320,2048]{1,0:T(8,128)(2,1)} %shard_map.117), channel_id=1, source_target_pairs={{0,2},{2,4},{4,6},{3,1},{5,3},{7,5},{8,10},{10,12},{12,14},{11,9},... | collective-permute-start | bytes 3932168 | tf_op jit(solution)/shard_map/ppermute | solution.py:324
  121.6 8.1 %shard_map.118 = (bf16[384,2560]{1,0:T(8,128)(2,1)}, bf16[384,2560]{1,0:T(8,128)(2,1)}, f32[2,2560]{1,0:T(2,128)}, f32[2,2048]{1,0:T(2,128)}) custom-call(s32[28]{0:T(128)} %stack.121.ids_ref, bf16[320,2048]{1,0:T(8,128)(2,1)} %copy-done.5, ...), custom_call_target="tpu_custom_call", output_to_operand_aliasing={{0}: (10, {}), {1}: (11, {}), {2}: (12, {})} | custom-call | flops 1 | bytes 1 | tf_op jit(solution)/shard_map/pallas_call | solution.py:273
  131.5 1.1 collective-permute-done.20
  132.7 2.0 %collective-permute-start.23 = (f32[2,4608]{1,0:T(2,128)S(1)}, f32[2,4608]{1,0:T(2,128)S(1)}, u32[]{:S(2)}, u32[]{:S(2)}) collective-permute-start(f32[2,4608]{1,0:T(2,128)S(1)} %add.135), channel_id=1, source_target_pairs={{6,0},{7,1},{0,2},{1,3},{2,4},{3,5},{4,6},{5,7},{14,8},{15,9},{8,1... | collective-permute-start | bytes 110600 | tf_op jit(solution)/shard_map/ppermute | solution.py:547
  135.0 2.1 %collective-permute-done.18 = bf16[320,1024]{1,0:T(8,128)(2,1)S(1)} collective-permute-done((bf16[320,1024]{1,0:T(8,128)(2,1)}, bf16[320,1024]{1,0:T(8,128)(2,1)S(1)}, u32[]{:S(2)}, u32[]{:S(2)}) %collective-permute-start.18) | collective-permute-done | bytes 655392 | tf_op jit(solution)/shard_map/ppermute | solution.py:462
  138.1 1.9 %collective-permute-start.22 = (bf16[320,1024]{1,0:T(8,128)(2,1)S(1)}, bf16[320,1024]{1,0:T(8,128)(2,1)S(1)}, u32[]{:S(2)}, u32[]{:S(2)}) collective-permute-start(bf16[320,1024]{1,0:T(8,128)(2,1)S(1)} %broadcast_select_fusion.4), channel_id=1, source_target_pairs={{0,1},{1,0},{2,3},{3,2},{4,5},{5,4},{6,7},{7,6},{8,9},{9,8},{10,11... | collective-permute-start | bytes 1966088 | tf_op jit(solution)/shard_map/ppermute | solution.py:564
  141.7 1.6 %convert_add_fusion = f32[320,1024]{1,0:T(8,128)} fusion(bf16[320,1024]{1,0:T(8,128)(2,1)S(1)} %collective-permute-done.22, f32[320,1024]{1,0:T(8,128)S(1)} %copy-done.12, bf16[320,1024]{1,0:T(8,128)(2,1)S(1)} %copy-done.14, pred[]{:T(512)S(6)} %lt.30, bf16[320,2048]{1,0:T(8,128)(2,1)S(1)} %collective-permute-done.19), kind=kLoop, calls=%fused_computation | loop fusion | flops 2293760 | bytes 5242881 | tf_op jit(solution)/shard_map/add | solution.py:570
  (71 shorter events, 16.0 us)
Async XLA Ops:
  0.6 20.4 %collective-permute-start = (bf16[320,2048]{1,0:T(8,128)(2,1)}, bf16[320,2048]{1,0:T(8,128)(2,1)}, u32[]{:S(2)}, u32[]{:S(2)}) collective-permute-start(bf16[320,2048]{1,0:T(8,128)(2,1)} %refs_0_), channel_id=1, source_target_pairs={{0,2},{2,4},{3,1},{4,6},{5,3},{7,5},{17,18},{19,20},{18,17},{21,22... | collective-permute-start | bytes 3932168 | tf_op jit(solution)/shard_map/ppermute | solution.py:345
  15.0 6.0 %collective-permute-start.5 = (bf16[192,2048]{1,0:T(8,128)(2,1)}, bf16[192,2048]{1,0:T(8,128)(2,1)S(1)}, u32[]{:S(2)}, u32[]{:S(2)}) collective-permute-start(bf16[192,2048]{1,0:T(8,128)(2,1)} %get-tuple-element.90.refs_8_.refs_12_.refs_4_.refs_2_), channel_id=1, source_target_pairs={{0,1},{1,0},{2,3},{3,2},{4,5},{5,4},{6,7},{7,6},{8,9},{9,8},{10,11... | collective-permute-start | bytes 2359304 | tf_op jit(solution)/shard_map/ppermute | solution.py:327
  15.0 7.3 %collective-permute-start.3 = (bf16[4,320,384]{2,1,0:T(8,128)(2,1)}, bf16[4,320,384]{2,1,0:T(8,128)(2,1)S(1)}, u32[]{:S(2)}, u32[]{:S(2)}) collective-permute-start(bf16[4,320,384]{2,1,0:T(8,128)(2,1)} %get-tuple-element.88.refs_0_.refs_4_), channel_id=1, source_target_pairs={{0,1},{1,0},{2,3},{3,2},{4,5},{5,4},{6,7},{7,6},{8,9},{9,8},{10,11... | collective-permute-start | bytes 2949128 | tf_op jit(solution)/shard_map/ppermute | solution.py:327
  15.5 6.8 %collective-permute-start.4 = (bf16[4,320,384]{2,1,0:T(8,128)(2,1)}, bf16[4,320,384]{2,1,0:T(8,128)(2,1)S(1)}, u32[]{:S(2)}, u32[]{:S(2)}) collective-permute-start(bf16[4,320,384]{2,1,0:T(8,128)(2,1)} %get-tuple-element.89.refs_1_.refs_5_), channel_id=1, source_target_pairs={{0,1},{1,0},{2,3},{3,2},{4,5},{5,4},{6,7},{7,6},{8,9},{9,8},{10,11... | collective-permute-start | bytes 2949128 | tf_op jit(solution)/shard_map/ppermute | solution.py:327
  15.6 6.7 %collective-permute-start.6 = (bf16[192,2048]{1,0:T(8,128)(2,1)}, bf16[192,2048]{1,0:T(8,128)(2,1)S(1)}, u32[]{:S(2)}, u32[]{:S(2)}) collective-permute-start(bf16[192,2048]{1,0:T(8,128)(2,1)} %get-tuple-element.91.refs_9_.refs_13_.refs_5_.refs_3_), channel_id=1, source_target_pairs={{0,1},{1,0},{2,3},{3,2},{4,5},{5,4},{6,7},{7,6},{8,9},{9,8},{10,11... | collective-permute-start | bytes 2359304 | tf_op jit(solution)/shard_map/ppermute | solution.py:327
  21.0 12.2 %collective-permute-start.1 = (bf16[320,2048]{1,0:T(8,128)(2,1)}, bf16[320,2048]{1,0:T(8,128)(2,1)}, u32[]{:S(2)}, u32[]{:S(2)}) collective-permute-start(bf16[320,2048]{1,0:T(8,128)(2,1)} %refs_0_), channel_id=1, source_target_pairs={{0,1},{1,0},{2,3},{3,2},{4,5},{5,4},{6,7},{7,6},{8,9},{9,8},{10,11... | collective-permute-start | bytes 3932168 | tf_op jit(solution)/shard_map/ppermute | solution.py:327
  21.0 1.4 copy-start.2
  21.0 24.3 %collective-permute-start.2 = (bf16[320,2048]{1,0:T(8,128)(2,1)}, bf16[320,2048]{1,0:T(8,128)(2,1)}, u32[]{:S(2)}, u32[]{:S(2)}) collective-permute-start(bf16[320,2048]{1,0:T(8,128)(2,1)} %collective-permute-done), channel_id=1, source_target_pairs={{1,16},{3,18},{4,21},{6,23},{17,0},{19,2},{20,5},{22,7},{9,24},{11... | collective-permute-start | bytes 3932168 | tf_op jit(solution)/shard_map/ppermute | solution.py:377
  29.1 20.3 %collective-permute-start.7 = (bf16[640,1024]{1,0:T(8,128)(2,1)}, bf16[640,1024]{1,0:T(8,128)(2,1)}, u32[]{:S(2)}, u32[]{:S(2)}) collective-permute-start(bf16[640,1024]{1,0:T(8,128)(2,1)} %shard_map.112), channel_id=1, source_target_pairs={{8,0},{11,3},{12,4},{15,7},{0,8},{3,11},{4,12},{7,15},{24,16},{27,... | collective-permute-start | bytes 3932168 | tf_op jit(solution)/shard_map/ppermute | solution.py:462
  32.5 16.9 %collective-permute-start.8 = (bf16[320,2048]{1,0:T(8,128)(2,1)}, bf16[320,2048]{1,0:T(8,128)(2,1)S(1)}, u32[]{:S(2)}, u32[]{:S(2)}) collective-permute-start(bf16[320,2048]{1,0:T(8,128)(2,1)} %collective-permute-done), channel_id=1, source_target_pairs={{2,4},{4,6},{3,1},{5,3},{10,12},{12,14},{11,9},{13,11},{18,20},{20... | collective-permute-start | bytes 3932168 | tf_op jit(solution)/shard_map/ppermute | solution.py:324
  46.8 7.4 %copy-start.4 = (bf16[320,2048]{1,0:T(8,128)(2,1)}, bf16[320,2048]{1,0:T(8,128)(2,1)S(1)}, u32[]{:S(2)}) copy-start(bf16[320,2048]{1,0:T(8,128)(2,1)S(1)} %broadcast_select_fusion.3.refs_2_) | copy-start | bytes 3932164
  46.8 20.4 %collective-permute-start.11 = (bf16[320,2048]{1,0:T(8,128)(2,1)S(1)}, bf16[320,2048]{1,0:T(8,128)(2,1)}, u32[]{:S(2)}, u32[]{:S(2)}) collective-permute-start(bf16[320,2048]{1,0:T(8,128)(2,1)S(1)} %broadcast_select_fusion.3.refs_2_), channel_id=1, source_target_pairs={{0,1},{1,0},{2,3},{3,2},{4,5},{5,4},{6,7},{7,6},{8,9},{9,8},{10,11... | collective-permute-start | bytes 3932168 | tf_op jit(solution)/shard_map/ppermute | solution.py:327
  54.3 25.7 %collective-permute-start.9 = (bf16[640,1024]{1,0:T(8,128)(2,1)}, bf16[640,1024]{1,0:T(8,128)(2,1)}, u32[]{:S(2)}, u32[]{:S(2)}) collective-permute-start(bf16[640,1024]{1,0:T(8,128)(2,1)} %get-tuple-element.107), channel_id=1, source_target_pairs={{8,0},{10,2},{13,5},{15,7},{0,8},{2,10},{5,13},{7,15},{24,16},{26,... | collective-permute-start | bytes 3932168 | tf_op jit(solution)/shard_map/ppermute | solution.py:462
  57.7 23.6 %collective-permute-start.10 = (bf16[320,2048]{1,0:T(8,128)(2,1)}, bf16[320,2048]{1,0:T(8,128)(2,1)S(1)}, u32[]{:S(2)}, u32[]{:S(2)}) collective-permute-start(bf16[320,2048]{1,0:T(8,128)(2,1)} %shard_map.113), channel_id=1, source_target_pairs={{0,2},{4,6},{7,5},{3,1},{8,10},{12,14},{15,13},{11,9},{16,18},{20,... | collective-permute-start | bytes 3932168 | tf_op jit(solution)/shard_map/ppermute | solution.py:324
  65.9 29.2 %collective-permute-start.14 = (bf16[320,2048]{1,0:T(8,128)(2,1)}, bf16[320,2048]{1,0:T(8,128)(2,1)}, u32[]{:S(2)}, u32[]{:S(2)}) collective-permute-start(bf16[320,2048]{1,0:T(8,128)(2,1)} %copy-done.7), channel_id=1, source_target_pairs={{1,16},{3,18},{4,21},{6,23},{17,0},{19,2},{20,5},{22,7},{9,24},{11... | collective-permute-start | bytes 3932168 | tf_op jit(solution)/shard_map/ppermute | solution.py:377
  82.3 12.8 %copy-start.8 = (bf16[320,2048]{1,0:T(8,128)(2,1)S(1)}, bf16[320,2048]{1,0:T(8,128)(2,1)}, u32[]{:S(2)}) copy-start(bf16[320,2048]{1,0:T(8,128)(2,1)} %copy-done.7) | copy-start | bytes 3932164
  86.3 22.7 %collective-permute-start.12 = (bf16[640,1024]{1,0:T(8,128)(2,1)}, bf16[640,1024]{1,0:T(8,128)(2,1)}, u32[]{:S(2)}, u32[]{:S(2)}) collective-permute-start(bf16[640,1024]{1,0:T(8,128)(2,1)} %get-tuple-element.123), channel_id=1, source_target_pairs={{8,0},{10,2},{13,5},{15,7},{0,8},{2,10},{5,13},{7,15},{24,16},{26,... | collective-permute-start | bytes 3932168 | tf_op jit(solution)/shard_map/ppermute | solution.py:462
  89.7 19.7 %collective-permute-start.13 = (bf16[320,2048]{1,0:T(8,128)(2,1)}, bf16[320,2048]{1,0:T(8,128)(2,1)}, u32[]{:S(2)}, u32[]{:S(2)}) collective-permute-start(bf16[320,2048]{1,0:T(8,128)(2,1)} %shard_map.115), channel_id=1, source_target_pairs={{0,2},{2,4},{5,3},{7,5},{8,10},{10,12},{13,11},{15,13},{16,18},{18... | collective-permute-start | bytes 3932168 | tf_op jit(solution)/shard_map/ppermute | solution.py:324
  95.2 1.7 %copy-start.10 = (bf16[320,2048]{1,0:T(8,128)(2,1)S(1)}, bf16[320,2048]{1,0:T(8,128)(2,1)}, u32[]{:S(2)}) copy-start(bf16[320,2048]{1,0:T(8,128)(2,1)} %copy-done.9) | copy-start | bytes 3932164
  96.7 3.1 %collective-permute-start.15 = (bf16[320,2048]{1,0:T(8,128)(2,1)S(1)}, bf16[320,2048]{1,0:T(8,128)(2,1)S(1)}, u32[]{:S(2)}, u32[]{:S(2)}) collective-permute-start(bf16[320,2048]{1,0:T(8,128)(2,1)S(1)} %broadcast_select_fusion.2.refs_0_), channel_id=1, source_target_pairs={{0,1},{1,0},{2,3},{3,2},{4,5},{5,4},{6,7},{7,6},{8,9},{9,8},{10,11... | collective-permute-start | bytes 3932168 | tf_op jit(solution)/shard_map/ppermute | solution.py:327
  97.9 19.0 %collective-permute-start.16 = (bf16[320,2048]{1,0:T(8,128)(2,1)S(1)}, bf16[320,2048]{1,0:T(8,128)(2,1)}, u32[]{:S(2)}, u32[]{:S(2)}) collective-permute-start(bf16[320,2048]{1,0:T(8,128)(2,1)S(1)} %broadcast_select_fusion), channel_id=1, source_target_pairs={{1,16},{2,19},{5,20},{6,23},{17,0},{18,3},{21,4},{22,7},{9,24},{10... | collective-permute-start | bytes 3932168 | tf_op jit(solution)/shard_map/ppermute | solution.py:377
  118.4 3.2 %copy-start.5 = (bf16[320,2048]{1,0:T(8,128)(2,1)}, bf16[320,2048]{1,0:T(8,128)(2,1)S(1)}, u32[]{:S(2)}) copy-start(bf16[320,2048]{1,0:T(8,128)(2,1)S(1)} %broadcast_select_fusion.1.refs_0_) | copy-start | bytes 3932164
  118.4 3.2 %collective-permute-start.17 = (bf16[320,2048]{1,0:T(8,128)(2,1)S(1)}, bf16[320,2048]{1,0:T(8,128)(2,1)}, u32[]{:S(2)}, u32[]{:S(2)}) collective-permute-start(bf16[320,2048]{1,0:T(8,128)(2,1)S(1)} %broadcast_select_fusion.1.refs_0_), channel_id=1, source_target_pairs={{0,1},{1,0},{2,3},{3,2},{4,5},{5,4},{6,7},{7,6},{8,9},{9,8},{10,11... | collective-permute-start | bytes 3932168 | tf_op jit(solution)/shard_map/ppermute | solution.py:327
  118.4 18.7 %collective-permute-start.19 = (bf16[320,2048]{1,0:T(8,128)(2,1)}, bf16[320,2048]{1,0:T(8,128)(2,1)S(1)}, u32[]{:S(2)}, u32[]{:S(2)}) collective-permute-start(bf16[320,2048]{1,0:T(8,128)(2,1)} %shard_map.117), channel_id=1, source_target_pairs={{0,2},{2,4},{4,6},{3,1},{5,3},{7,5},{8,10},{10,12},{12,14},{11,9},... | collective-permute-start | bytes 3932168 | tf_op jit(solution)/shard_map/ppermute | solution.py:324
  120.3 16.9 %collective-permute-start.18 = (bf16[320,1024]{1,0:T(8,128)(2,1)}, bf16[320,1024]{1,0:T(8,128)(2,1)S(1)}, u32[]{:S(2)}, u32[]{:S(2)}) collective-permute-start(bf16[320,1024]{1,0:T(8,128)(2,1)} %get-tuple-element.158), channel_id=1, source_target_pairs={{8,0},{9,1},{10,2},{11,3},{12,4},{13,5},{14,6},{15,7},{0,8},{1,9},... | collective-permute-start | bytes 1966088 | tf_op jit(solution)/shard_map/ppermute | solution.py:462
  129.7 12.0 %copy-start.12 = (f32[320,1024]{1,0:T(8,128)S(1)}, f32[320,1024]{1,0:T(8,128)}, u32[]{:S(2)}) copy-start(f32[320,1024]{1,0:T(8,128)} %get-tuple-element.157) | copy-start | bytes 3932164
  131.3 1.2 collective-permute-start.20
  132.6 5.4 %collective-permute-start.21 = (f32[2,4608]{1,0:T(2,128)S(1)}, f32[2,4608]{1,0:T(2,128)S(1)}, u32[]{:S(2)}, u32[]{:S(2)}) collective-permute-start(f32[2,4608]{1,0:T(2,128)S(1)} %add.135), channel_id=1, source_target_pairs={{2,0},{3,1},{4,2},{5,3},{6,4},{7,5},{0,6},{1,7},{10,8},{11,9},{12,... | collective-permute-start | bytes 110600 | tf_op jit(solution)/shard_map/ppermute | solution.py:547
  132.7 7.3 %collective-permute-start.23 = (f32[2,4608]{1,0:T(2,128)S(1)}, f32[2,4608]{1,0:T(2,128)S(1)}, u32[]{:S(2)}, u32[]{:S(2)}) collective-permute-start(f32[2,4608]{1,0:T(2,128)S(1)} %add.135), channel_id=1, source_target_pairs={{6,0},{7,1},{0,2},{1,3},{2,4},{3,5},{4,6},{5,7},{14,8},{15,9},{8,1... | collective-permute-start | bytes 110600 | tf_op jit(solution)/shard_map/ppermute | solution.py:547
  134.6 5.4 %collective-permute-start.24 = (f32[2,4608]{1,0:T(2,128)S(1)}, f32[2,4608]{1,0:T(2,128)S(1)}, u32[]{:S(2)}, u32[]{:S(2)}) collective-permute-start(f32[2,4608]{1,0:T(2,128)S(1)} %add.135), channel_id=1, source_target_pairs={{4,0},{5,1},{6,2},{7,3},{0,4},{1,5},{2,6},{3,7},{12,8},{13,9},{14,... | collective-permute-start | bytes 110600 | tf_op jit(solution)/shard_map/ppermute | solution.py:547
  138.0 3.7 %copy-start.14 = (bf16[320,1024]{1,0:T(8,128)(2,1)S(1)}, bf16[320,1024]{1,0:T(8,128)(2,1)}, u32[]{:S(2)}) copy-start(bf16[320,1024]{1,0:T(8,128)(2,1)} %copy-done.13) | copy-start | bytes 1966084
  138.1 3.7 %collective-permute-start.22 = (bf16[320,1024]{1,0:T(8,128)(2,1)S(1)}, bf16[320,1024]{1,0:T(8,128)(2,1)S(1)}, u32[]{:S(2)}, u32[]{:S(2)}) collective-permute-start(bf16[320,1024]{1,0:T(8,128)(2,1)S(1)} %broadcast_select_fusion.4), channel_id=1, source_target_pairs={{0,1},{1,0},{2,3},{3,2},{4,5},{5,4},{6,7},{7,6},{8,9},{9,8},{10,11... | collective-permute-start | bytes 1966088 | tf_op jit(solution)/shard_map/ppermute | solution.py:564
  (8 other events, 8.3 us)

commit v6 on v5

--- a/solution.py
+++ b/solution.py
@@ -158,15 +158,15 @@
 
 def hop(ids, flags, own, got, other, coming, weight):
     rows, columns = own.shape
-    stacked = pl.BlockSpec((rows // 2, columns), lambda i, ids: (i, 0))
-    beside = pl.BlockSpec((rows // 2, columns), lambda i, ids: (0, i))
+    stacked = pl.BlockSpec((rows // 4, columns), lambda i, h, ids: (2 * i + h, 0))
+    beside = pl.BlockSpec((rows // 4, columns), lambda i, h, ids: (h, i))
     ins = [own] + got + other + coming + weight
     return pl.pallas_call(
         functools.partial(hop_kernel, len(got), bool(other), len(coming), flags),
         out_shape=jax.ShapeDtypeStruct((rows // 2, 2 * columns), BF16),
         grid_spec=pltpu.PrefetchScalarGridSpec(
             num_scalar_prefetch=1,
-            grid=(2,),
+            grid=(2, 2),
             in_specs=[stacked] * (1 + len(got) + len(other))
             + [beside] * (len(coming) + len(weight)),
             out_specs=beside,

time: 144 us -> 146 us (1.014)
  Pallas kernels: 64.6 us -> 67.3 us
    pallas_call x3, Pallas kernels: 12.2 us -> 14.9 us  [hop(): pl.pallas_call(functools.partial(hop_kernel, len(got), bool(other), len(c...]
  transfers between devices with their start and end apart: 25 -> 25, of which waited for: 9 -> 9; matrix products, arithmetic and copies ran while one was open for 6% -> 6% of each run, Pallas kernels for 45% -> 46%
where the time goes in v6:
time: 146 us; the launch traced here: 145 us
  Pallas kernels  67.3 us (46%)
  starting transfers between devices  45.3 us (31%)
  waiting for transfers between devices  13.3 us (9%)
  local copies, waits for them, and re-layouts  11.9 us (8%)
  other arithmetic  6.43 us (4%)
    pallas_call x3, Pallas kernels, weight_slots(): pl.pallas_call(functools.partial(slot_kernel, n, lo, kept is not None, ba...  29 us
    pallas_call x2, Pallas kernels, partials(): pl.pallas_call(functools.partial(partials_kernel, lo, items, len(column_a...  16.7 us
    ppermute x4, starting transfers between devices, line_step(): return lax.ppermute(x, 'fsdp', pairs)  16.2 us
    pallas_call x3, Pallas kernels, hop(): pl.pallas_call(functools.partial(hop_kernel, len(got), bool(other), len(c...  14.9 us
    ppermute x4, starting transfers between devices, exchange(): got[k].append(lax.ppermute(blocks[j - 1], ('member', 'fsdp'), pairs))  10.8 us
    unnamed x31, local copies, waits for them, and re-layouts  7.89 us
    pallas_call x1, Pallas kernels, prepare(): pl.pallas_call(functools.partial(prepare_kernel, nh), out_shape=[turned,...  6.85 us
    ppermute x1, starting transfers between devices, weight_first(): arrived[1] = lax.ppermute(weight, ('groups', 'fsdp'), pairs)  6.03 us
  transfers between devices with their start and end apart: 25, of which 9 were waited for; matrix products, arithmetic and copies ran while one was open for 6% of the time, Pallas kernels for 46%

profile of v6, /device:TPU:0, one launch (start us, length us, event | category | flops | bytes accessed | tf_op | source)
XLA Modules:
  0.0 145.3 jit_solution(15860840557203893453)
XLA Ops:
  0.6 6.0 %collective-permute-start = (bf16[320,2048]{1,0:T(8,128)(2,1)}, bf16[320,2048]{1,0:T(8,128)(2,1)}, u32[]{:S(2)}, u32[]{:S(2)}) collective-permute-start(bf16[320,2048]{1,0:T(8,128)(2,1)} %refs_0_), channel_id=1, source_target_pairs={{0,2},{2,4},{3,1},{4,6},{5,3},{7,5},{17,18},{19,20},{18,17},{21,22... | collective-permute-start | bytes 3932168 | tf_op jit(solution)/shard_map/ppermute | solution.py:345
  6.7 1.5 %broadcast_in_dim.4.slot_ref.refs_10_.refs_8_ = s32[384,1]{1,0:T(8,128)} reshape(s32[384]{0:T(512)} %param.13) | data formatting | bytes 3072 | tf_op jit(solution)/shard_map/broadcast_in_dim | solution.py:311
  8.1 6.8 %shard_map.110 = (bf16[4,320,384]{2,1,0:T(8,128)(2,1)}, bf16[4,320,384]{2,1,0:T(8,128)(2,1)}, bf16[192,2048]{1,0:T(8,128)(2,1)}, bf16[192,2048]{1,0:T(8,128)(2,1)}) custom-call(bf16[384,2560]{1,0:T(8,128)(2,1)} %refs_5_.3, bf16[384,2560]{1,0:T(8,128)(2,1)} %refs_6_.5, f32[2,2560]{1,0:T(2,128)} %refs_7_.5, bf16[384,2048]{1,0:T(8,128)(2,1)} %refs_4_.3, ...), custom_call_target="tpu_custom_call" | custom-call | flops 1 | bytes 1 | tf_op jit(solution)/shard_map/pallas_call | solution.py:55
  16.7 4.3 %collective-permute-done = bf16[320,2048]{1,0:T(8,128)(2,1)} collective-permute-done((bf16[320,2048]{1,0:T(8,128)(2,1)}, bf16[320,2048]{1,0:T(8,128)(2,1)}, u32[]{:S(2)}, u32[]{:S(2)}) %collective-permute-start) | collective-permute-done | bytes 1310752 | tf_op jit(solution)/shard_map/ppermute | solution.py:345
  21.0 1.3 collective-permute-start.2
  24.5 4.6 %shard_map.112 = bf16[640,1024]{1,0:T(8,128)(2,1)} custom-call(s32[28]{0:T(128)} %stack.121.ids_ref, bf16[4,320,384]{2,1,0:T(8,128)(2,1)} %get-tuple-element.88.refs_0_.refs_4_, bf16[4,320,384]{2,1,0:T(8,128)(2,1)} %get-tuple-element.89.refs_1_.refs_5_, bf16[4,320,384]{2,1,0:T(8,128)(2,1)} %copy-done, bf16[4,320,384]{2,1,0:T(8,128)(2,1)} %copy-done.1, ...), custom_call_target="tpu_custom_call" | custom-call | flops 1 | bytes 1 | tf_op jit(solution)/shard_map/pallas_call | solution.py:129
  29.1 3.4 %collective-permute-start.7 = (bf16[640,1024]{1,0:T(8,128)(2,1)}, bf16[640,1024]{1,0:T(8,128)(2,1)}, u32[]{:S(2)}, u32[]{:S(2)}) collective-permute-start(bf16[640,1024]{1,0:T(8,128)(2,1)} %shard_map.112), channel_id=1, source_target_pairs={{8,0},{11,3},{12,4},{15,7},{0,8},{3,11},{4,12},{7,15},{24,16},{27,... | collective-permute-start | bytes 3932168 | tf_op jit(solution)/shard_map/ppermute | solution.py:462
  33.2 12.1 %shard_map.111 = (bf16[640,1024]{1,0:T(8,128)(2,1)}, bf16[640,1024]{1,0:T(8,128)(2,1)}, bf16[320,1024]{1,0:T(8,128)(2,1)}, bf16[640,1024]{1,0:T(8,128)(2,1)}, bf...) custom-call(s32[28]{0:T(128)} %stack.121.ids_ref, ...), custom_call_target="tpu_custom_call" | custom-call | flops 1 | bytes 1 | tf_op jit(solution)/shard_map/pallas_call | solution.py:129
  45.4 1.5 %broadcast_select_fusion.3.refs_2_ = bf16[320,2048]{1,0:T(8,128)(2,1)S(1)} fusion(bf16[320,2048]{1,0:T(8,128)(2,1)} %collective-permute-done, bf16[320,2048]{1,0:T(8,128)(2,1)} %collective-permute-done.2, pred[]{:T(512)S(6)} %eq.109), kind=kLoop, calls=%fused_computation.4 | loop fusion | flops 655360 | bytes 3932161 | tf_op jit(solution)/shard_map/jit(_where)/select_n | solution.py:380
  46.8 2.5 %collective-permute-start.11 = (bf16[320,2048]{1,0:T(8,128)(2,1)S(1)}, bf16[320,2048]{1,0:T(8,128)(2,1)}, u32[]{:S(2)}, u32[]{:S(2)}) collective-permute-start(bf16[320,2048]{1,0:T(8,128)(2,1)S(1)} %broadcast_select_fusion.3.refs_2_), channel_id=1, source_target_pairs={{0,1},{1,0},{2,3},{3,2},{4,5},{5,4},{6,7},{7,6},{8,9},{9,8},{10,11... | collective-permute-start | bytes 3932168 | tf_op jit(solution)/shard_map/ppermute | solution.py:327
  50.4 4.8 %shard_map.113 = bf16[320,2048]{1,0:T(8,128)(2,1)} custom-call(s32[28]{0:T(128)} %stack.121.ids_ref, bf16[640,1024]{1,0:T(8,128)(2,1)} %get-tuple-element.99.sum_ref, bf16[640,1024]{1,0:T(8,128)(2,1)} %collective-permute-done.7.refs_0_.refs_1_, bf16[320,2048]{1,0:T(8,128)(2,1)} %copy-done.7), custom_call_target="tpu_custom_call" | custom-call | flops 1 | bytes 1 | tf_op jit(solution)/shard_map/pallas_call | solution.py:164
  55.2 3.4 %collective-permute-start.9 = (bf16[640,1024]{1,0:T(8,128)(2,1)}, bf16[640,1024]{1,0:T(8,128)(2,1)}, u32[]{:S(2)}, u32[]{:S(2)}) collective-permute-start(bf16[640,1024]{1,0:T(8,128)(2,1)} %get-tuple-element.107), channel_id=1, source_target_pairs={{8,0},{10,2},{13,5},{15,7},{0,8},{2,10},{5,13},{7,15},{24,16},{26,... | collective-permute-start | bytes 3932168 | tf_op jit(solution)/shard_map/ppermute | solution.py:462
  58.6 8.2 %collective-permute-start.10 = (bf16[320,2048]{1,0:T(8,128)(2,1)}, bf16[320,2048]{1,0:T(8,128)(2,1)S(1)}, u32[]{:S(2)}, u32[]{:S(2)}) collective-permute-start(bf16[320,2048]{1,0:T(8,128)(2,1)} %shard_map.113), channel_id=1, source_target_pairs={{0,2},{4,6},{7,5},{3,1},{8,10},{12,14},{15,13},{11,9},{16,18},{20,... | collective-permute-start | bytes 3932168 | tf_op jit(solution)/shard_map/ppermute | solution.py:324
  66.9 1.3 collective-permute-start.14
  68.2 12.7 %shard_map.114 = (bf16[384,2560]{1,0:T(8,128)(2,1)}, bf16[384,2560]{1,0:T(8,128)(2,1)}, f32[2,2560]{1,0:T(2,128)}, f32[2,2048]{1,0:T(2,128)}) custom-call(s32[28]{0:T(128)} %stack.121.ids_ref, bf16[320,2048]{1,0:T(8,128)(2,1)} %refs_0_, bf16[320,2048]{1,0:T(8,128)(2,1)} %collective-permute-done.1.refs_1_, bf16[320,2048]{1,0:T(8,128)(2,1)} %copy-done.4, ...), custom_call_target="tpu_custom_call" | custom-call | flops 1 | bytes 1 | tf_op jit(solution)/shard_map/pallas_call | solution.py:273
  80.9 1.3 collective-permute-done.10.refs_1_
  83.3 5.0 %shard_map.115 = bf16[320,2048]{1,0:T(8,128)(2,1)} custom-call(s32[28]{0:T(128)} %stack.121.ids_ref, bf16[640,1024]{1,0:T(8,128)(2,1)} %get-tuple-element.105.sum_ref, bf16[640,1024]{1,0:T(8,128)(2,1)} %collective-permute-done.9.refs_0_, bf16[320,2048]{1,0:T(8,128)(2,1)} %copy-done.9), custom_call_target="tpu_custom_call" | custom-call | flops 1 | bytes 1 | tf_op jit(solution)/shard_map/pallas_call | solution.py:164
  88.3 3.4 %collective-permute-start.12 = (bf16[640,1024]{1,0:T(8,128)(2,1)}, bf16[640,1024]{1,0:T(8,128)(2,1)}, u32[]{:S(2)}, u32[]{:S(2)}) collective-permute-start(bf16[640,1024]{1,0:T(8,128)(2,1)} %get-tuple-element.123), channel_id=1, source_target_pairs={{8,0},{10,2},{13,5},{15,7},{0,8},{2,10},{5,13},{7,15},{24,16},{26,... | collective-permute-start | bytes 3932168 | tf_op jit(solution)/shard_map/ppermute | solution.py:462
  91.7 5.4 %collective-permute-start.13 = (bf16[320,2048]{1,0:T(8,128)(2,1)}, bf16[320,2048]{1,0:T(8,128)(2,1)}, u32[]{:S(2)}, u32[]{:S(2)}) collective-permute-start(bf16[320,2048]{1,0:T(8,128)(2,1)} %shard_map.115), channel_id=1, source_target_pairs={{0,2},{2,4},{5,3},{7,5},{8,10},{10,12},{13,11},{15,13},{16,18},{18... | collective-permute-start | bytes 3932168 | tf_op jit(solution)/shard_map/ppermute | solution.py:324
  97.1 1.6 %broadcast_select_fusion.2.refs_0_ = bf16[320,2048]{1,0:T(8,128)(2,1)S(1)} fusion(bf16[320,2048]{1,0:T(8,128)(2,1)S(1)} %copy-done.8, bf16[320,2048]{1,0:T(8,128)(2,1)} %collective-permute-done.14, pred[]{:T(512)S(6)} %eq.110), kind=kLoop, calls=%fused_computation.3 | loop fusion | flops 655360 | bytes 3932161 | tf_op jit(solution)/shard_map/jit(_where)/select_n | solution.py:380
  99.8 1.5 %collective-permute-start.16 = (bf16[320,2048]{1,0:T(8,128)(2,1)S(1)}, bf16[320,2048]{1,0:T(8,128)(2,1)}, u32[]{:S(2)}, u32[]{:S(2)}) collective-permute-start(bf16[320,2048]{1,0:T(8,128)(2,1)S(1)} %broadcast_select_fusion), channel_id=1, source_target_pairs={{1,16},{2,19},{5,20},{6,23},{17,0},{18,3},{21,4},{22,7},{9,24},{10... | collective-permute-start | bytes 3932168 | tf_op jit(solution)/shard_map/ppermute | solution.py:377
  102.8 8.1 %shard_map.116 = (bf16[384,2560]{1,0:T(8,128)(2,1)}, bf16[384,2560]{1,0:T(8,128)(2,1)}, f32[2,2560]{1,0:T(2,128)}, f32[2,2048]{1,0:T(2,128)}) custom-call(s32[28]{0:T(128)} %stack.121.ids_ref, bf16[320,2048]{1,0:T(8,128)(2,1)} %copy-done.6, bf16[320,2048]{1,0:T(8,128)(2,1)} %copy-done.11, ...), custom_call_target="tpu_custom_call", output_to_operand_aliasing={{0}: (10, {}), {1}: (11, {}), {2}: (12, {})} | custom-call | flops 1 | bytes 1 | tf_op jit(solution)/shard_map/pallas_call | solution.py:273
  111.4 5.1 %shard_map.117 = bf16[320,2048]{1,0:T(8,128)(2,1)} custom-call(s32[28]{0:T(128)} %stack.121.ids_ref, bf16[640,1024]{1,0:T(8,128)(2,1)} %get-tuple-element.121.sum_ref, bf16[640,1024]{1,0:T(8,128)(2,1)} %collective-permute-done.12.refs_0_, bf16[640,1024]{1,0:T(8,128)(2,1)} %collective-permute-done.7.refs_0_.refs_1_, ...), custom_call_target="tpu_custom_call" | custom-call | flops 1 | bytes 1 | tf_op jit(solution)/shard_map/pallas_call | solution.py:164
  116.5 2.4 %collective-permute-done.16 = bf16[320,2048]{1,0:T(8,128)(2,1)} collective-permute-done((bf16[320,2048]{1,0:T(8,128)(2,1)S(1)}, bf16[320,2048]{1,0:T(8,128)(2,1)}, u32[]{:S(2)}, u32[]{:S(2)}) %collective-permute-start.16) | collective-permute-done | bytes 1310752 | tf_op jit(solution)/shard_map/ppermute | solution.py:377
  118.9 1.5 %broadcast_select_fusion.1.refs_0_ = bf16[320,2048]{1,0:T(8,128)(2,1)S(1)} fusion(bf16[320,2048]{1,0:T(8,128)(2,1)S(1)} %broadcast_select_fusion, bf16[320,2048]{1,0:T(8,128)(2,1)} %collective-permute-done.16, pred[]{:T(512)S(6)} %eq.111), kind=kLoop, calls=%fused_computation.2 | loop fusion | flops 655360 | bytes 3932161 | tf_op jit(solution)/shard_map/jit(_where)/select_n | solution.py:380
  120.4 1.8 %collective-permute-start.19 = (bf16[320,2048]{1,0:T(8,128)(2,1)}, bf16[320,2048]{1,0:T(8,128)(2,1)S(1)}, u32[]{:S(2)}, u32[]{:S(2)}) collective-permute-start(bf16[320,2048]{1,0:T(8,128)(2,1)} %shard_map.117), channel_id=1, source_target_pairs={{0,2},{2,4},{4,6},{3,1},{5,3},{7,5},{8,10},{10,12},{12,14},{11,9},... | collective-permute-start | bytes 3932168 | tf_op jit(solution)/shard_map/ppermute | solution.py:324
  123.6 8.1 %shard_map.118 = (bf16[384,2560]{1,0:T(8,128)(2,1)}, bf16[384,2560]{1,0:T(8,128)(2,1)}, f32[2,2560]{1,0:T(2,128)}, f32[2,2048]{1,0:T(2,128)}) custom-call(s32[28]{0:T(128)} %stack.121.ids_ref, bf16[320,2048]{1,0:T(8,128)(2,1)} %copy-done.5, ...), custom_call_target="tpu_custom_call", output_to_operand_aliasing={{0}: (10, {}), {1}: (11, {}), {2}: (12, {})} | custom-call | flops 1 | bytes 1 | tf_op jit(solution)/shard_map/pallas_call | solution.py:273
  133.4 1.1 collective-permute-done.20
  134.6 2.0 %collective-permute-start.23 = (f32[2,4608]{1,0:T(2,128)S(1)}, f32[2,4608]{1,0:T(2,128)S(1)}, u32[]{:S(2)}, u32[]{:S(2)}) collective-permute-start(f32[2,4608]{1,0:T(2,128)S(1)} %add.135), channel_id=1, source_target_pairs={{6,0},{7,1},{0,2},{1,3},{2,4},{3,5},{4,6},{5,7},{14,8},{15,9},{8,1... | collective-permute-start | bytes 110600 | tf_op jit(solution)/shard_map/ppermute | solution.py:547
  137.0 2.1 %collective-permute-done.18 = bf16[320,1024]{1,0:T(8,128)(2,1)S(1)} collective-permute-done((bf16[320,1024]{1,0:T(8,128)(2,1)}, bf16[320,1024]{1,0:T(8,128)(2,1)S(1)}, u32[]{:S(2)}, u32[]{:S(2)}) %collective-permute-start.18) | collective-permute-done | bytes 655392 | tf_op jit(solution)/shard_map/ppermute | solution.py:462
  140.0 1.9 %collective-permute-start.22 = (bf16[320,1024]{1,0:T(8,128)(2,1)S(1)}, bf16[320,1024]{1,0:T(8,128)(2,1)S(1)}, u32[]{:S(2)}, u32[]{:S(2)}) collective-permute-start(bf16[320,1024]{1,0:T(8,128)(2,1)S(1)} %broadcast_select_fusion.4), channel_id=1, source_target_pairs={{0,1},{1,0},{2,3},{3,2},{4,5},{5,4},{6,7},{7,6},{8,9},{9,8},{10,11... | collective-permute-start | bytes 1966088 | tf_op jit(solution)/shard_map/ppermute | solution.py:564
  143.7 1.6 %convert_add_fusion = f32[320,1024]{1,0:T(8,128)} fusion(bf16[320,1024]{1,0:T(8,128)(2,1)S(1)} %collective-permute-done.22, f32[320,1024]{1,0:T(8,128)S(1)} %copy-done.12, bf16[320,1024]{1,0:T(8,128)(2,1)S(1)} %copy-done.14, pred[]{:T(512)S(6)} %lt.30, bf16[320,2048]{1,0:T(8,128)(2,1)S(1)} %collective-permute-done.19), kind=kLoop, calls=%fused_computation | loop fusion | flops 2293760 | bytes 5242881 | tf_op jit(solution)/shard_map/add | solution.py:570
  (71 shorter events, 16.0 us)
Async XLA Ops:
  0.6 20.4 %collective-permute-start = (bf16[320,2048]{1,0:T(8,128)(2,1)}, bf16[320,2048]{1,0:T(8,128)(2,1)}, u32[]{:S(2)}, u32[]{:S(2)}) collective-permute-start(bf16[320,2048]{1,0:T(8,128)(2,1)} %refs_0_), channel_id=1, source_target_pairs={{0,2},{2,4},{3,1},{4,6},{5,3},{7,5},{17,18},{19,20},{18,17},{21,22... | collective-permute-start | bytes 3932168 | tf_op jit(solution)/shard_map/ppermute | solution.py:345
  15.0 6.0 %collective-permute-start.5 = (bf16[192,2048]{1,0:T(8,128)(2,1)}, bf16[192,2048]{1,0:T(8,128)(2,1)S(1)}, u32[]{:S(2)}, u32[]{:S(2)}) collective-permute-start(bf16[192,2048]{1,0:T(8,128)(2,1)} %get-tuple-element.90.refs_8_.refs_12_.refs_4_.refs_2_), channel_id=1, source_target_pairs={{0,1},{1,0},{2,3},{3,2},{4,5},{5,4},{6,7},{7,6},{8,9},{9,8},{10,11... | collective-permute-start | bytes 2359304 | tf_op jit(solution)/shard_map/ppermute | solution.py:327
  15.0 7.3 %collective-permute-start.3 = (bf16[4,320,384]{2,1,0:T(8,128)(2,1)}, bf16[4,320,384]{2,1,0:T(8,128)(2,1)S(1)}, u32[]{:S(2)}, u32[]{:S(2)}) collective-permute-start(bf16[4,320,384]{2,1,0:T(8,128)(2,1)} %get-tuple-element.88.refs_0_.refs_4_), channel_id=1, source_target_pairs={{0,1},{1,0},{2,3},{3,2},{4,5},{5,4},{6,7},{7,6},{8,9},{9,8},{10,11... | collective-permute-start | bytes 2949128 | tf_op jit(solution)/shard_map/ppermute | solution.py:327
  15.5 6.8 %collective-permute-start.4 = (bf16[4,320,384]{2,1,0:T(8,128)(2,1)}, bf16[4,320,384]{2,1,0:T(8,128)(2,1)S(1)}, u32[]{:S(2)}, u32[]{:S(2)}) collective-permute-start(bf16[4,320,384]{2,1,0:T(8,128)(2,1)} %get-tuple-element.89.refs_1_.refs_5_), channel_id=1, source_target_pairs={{0,1},{1,0},{2,3},{3,2},{4,5},{5,4},{6,7},{7,6},{8,9},{9,8},{10,11... | collective-permute-start | bytes 2949128 | tf_op jit(solution)/shard_map/ppermute | solution.py:327
  15.6 6.7 %collective-permute-start.6 = (bf16[192,2048]{1,0:T(8,128)(2,1)}, bf16[192,2048]{1,0:T(8,128)(2,1)S(1)}, u32[]{:S(2)}, u32[]{:S(2)}) collective-permute-start(bf16[192,2048]{1,0:T(8,128)(2,1)} %get-tuple-element.91.refs_9_.refs_13_.refs_5_.refs_3_), channel_id=1, source_target_pairs={{0,1},{1,0},{2,3},{3,2},{4,5},{5,4},{6,7},{7,6},{8,9},{9,8},{10,11... | collective-permute-start | bytes 2359304 | tf_op jit(solution)/shard_map/ppermute | solution.py:327
  21.0 12.2 %collective-permute-start.1 = (bf16[320,2048]{1,0:T(8,128)(2,1)}, bf16[320,2048]{1,0:T(8,128)(2,1)}, u32[]{:S(2)}, u32[]{:S(2)}) collective-permute-start(bf16[320,2048]{1,0:T(8,128)(2,1)} %refs_0_), channel_id=1, source_target_pairs={{0,1},{1,0},{2,3},{3,2},{4,5},{5,4},{6,7},{7,6},{8,9},{9,8},{10,11... | collective-permute-start | bytes 3932168 | tf_op jit(solution)/shard_map/ppermute | solution.py:327
  21.0 1.4 copy-start.2
  21.0 24.3 %collective-permute-start.2 = (bf16[320,2048]{1,0:T(8,128)(2,1)}, bf16[320,2048]{1,0:T(8,128)(2,1)}, u32[]{:S(2)}, u32[]{:S(2)}) collective-permute-start(bf16[320,2048]{1,0:T(8,128)(2,1)} %collective-permute-done), channel_id=1, source_target_pairs={{1,16},{3,18},{4,21},{6,23},{17,0},{19,2},{20,5},{22,7},{9,24},{11... | collective-permute-start | bytes 3932168 | tf_op jit(solution)/shard_map/ppermute | solution.py:377
  29.1 20.3 %collective-permute-start.7 = (bf16[640,1024]{1,0:T(8,128)(2,1)}, bf16[640,1024]{1,0:T(8,128)(2,1)}, u32[]{:S(2)}, u32[]{:S(2)}) collective-permute-start(bf16[640,1024]{1,0:T(8,128)(2,1)} %shard_map.112), channel_id=1, source_target_pairs={{8,0},{11,3},{12,4},{15,7},{0,8},{3,11},{4,12},{7,15},{24,16},{27,... | collective-permute-start | bytes 3932168 | tf_op jit(solution)/shard_map/ppermute | solution.py:462
  32.5 16.9 %collective-permute-start.8 = (bf16[320,2048]{1,0:T(8,128)(2,1)}, bf16[320,2048]{1,0:T(8,128)(2,1)S(1)}, u32[]{:S(2)}, u32[]{:S(2)}) collective-permute-start(bf16[320,2048]{1,0:T(8,128)(2,1)} %collective-permute-done), channel_id=1, source_target_pairs={{2,4},{4,6},{3,1},{5,3},{10,12},{12,14},{11,9},{13,11},{18,20},{20... | collective-permute-start | bytes 3932168 | tf_op jit(solution)/shard_map/ppermute | solution.py:324
  46.8 8.4 %copy-start.4 = (bf16[320,2048]{1,0:T(8,128)(2,1)}, bf16[320,2048]{1,0:T(8,128)(2,1)S(1)}, u32[]{:S(2)}) copy-start(bf16[320,2048]{1,0:T(8,128)(2,1)S(1)} %broadcast_select_fusion.3.refs_2_) | copy-start | bytes 3932164
  46.8 21.4 %collective-permute-start.11 = (bf16[320,2048]{1,0:T(8,128)(2,1)S(1)}, bf16[320,2048]{1,0:T(8,128)(2,1)}, u32[]{:S(2)}, u32[]{:S(2)}) collective-permute-start(bf16[320,2048]{1,0:T(8,128)(2,1)S(1)} %broadcast_select_fusion.3.refs_2_), channel_id=1, source_target_pairs={{0,1},{1,0},{2,3},{3,2},{4,5},{5,4},{6,7},{7,6},{8,9},{9,8},{10,11... | collective-permute-start | bytes 3932168 | tf_op jit(solution)/shard_map/ppermute | solution.py:327
  55.2 25.7 %collective-permute-start.9 = (bf16[640,1024]{1,0:T(8,128)(2,1)}, bf16[640,1024]{1,0:T(8,128)(2,1)}, u32[]{:S(2)}, u32[]{:S(2)}) collective-permute-start(bf16[640,1024]{1,0:T(8,128)(2,1)} %get-tuple-element.107), channel_id=1, source_target_pairs={{8,0},{10,2},{13,5},{15,7},{0,8},{2,10},{5,13},{7,15},{24,16},{26,... | collective-permute-start | bytes 3932168 | tf_op jit(solution)/shard_map/ppermute | solution.py:462
  58.6 23.6 %collective-permute-start.10 = (bf16[320,2048]{1,0:T(8,128)(2,1)}, bf16[320,2048]{1,0:T(8,128)(2,1)S(1)}, u32[]{:S(2)}, u32[]{:S(2)}) collective-permute-start(bf16[320,2048]{1,0:T(8,128)(2,1)} %shard_map.113), channel_id=1, source_target_pairs={{0,2},{4,6},{7,5},{3,1},{8,10},{12,14},{15,13},{11,9},{16,18},{20,... | collective-permute-start | bytes 3932168 | tf_op jit(solution)/shard_map/ppermute | solution.py:324
  66.9 30.2 %collective-permute-start.14 = (bf16[320,2048]{1,0:T(8,128)(2,1)}, bf16[320,2048]{1,0:T(8,128)(2,1)}, u32[]{:S(2)}, u32[]{:S(2)}) collective-permute-start(bf16[320,2048]{1,0:T(8,128)(2,1)} %copy-done.7), channel_id=1, source_target_pairs={{1,16},{3,18},{4,21},{6,23},{17,0},{19,2},{20,5},{22,7},{9,24},{11... | collective-permute-start | bytes 3932168 | tf_op jit(solution)/shard_map/ppermute | solution.py:377
  83.3 13.8 %copy-start.8 = (bf16[320,2048]{1,0:T(8,128)(2,1)S(1)}, bf16[320,2048]{1,0:T(8,128)(2,1)}, u32[]{:S(2)}) copy-start(bf16[320,2048]{1,0:T(8,128)(2,1)} %copy-done.7) | copy-start | bytes 3932164
  88.3 22.7 %collective-permute-start.12 = (bf16[640,1024]{1,0:T(8,128)(2,1)}, bf16[640,1024]{1,0:T(8,128)(2,1)}, u32[]{:S(2)}, u32[]{:S(2)}) collective-permute-start(bf16[640,1024]{1,0:T(8,128)(2,1)} %get-tuple-element.123), channel_id=1, source_target_pairs={{8,0},{10,2},{13,5},{15,7},{0,8},{2,10},{5,13},{7,15},{24,16},{26,... | collective-permute-start | bytes 3932168 | tf_op jit(solution)/shard_map/ppermute | solution.py:462
  91.7 19.7 %collective-permute-start.13 = (bf16[320,2048]{1,0:T(8,128)(2,1)}, bf16[320,2048]{1,0:T(8,128)(2,1)}, u32[]{:S(2)}, u32[]{:S(2)}) collective-permute-start(bf16[320,2048]{1,0:T(8,128)(2,1)} %shard_map.115), channel_id=1, source_target_pairs={{0,2},{2,4},{5,3},{7,5},{8,10},{10,12},{13,11},{15,13},{16,18},{18... | collective-permute-start | bytes 3932168 | tf_op jit(solution)/shard_map/ppermute | solution.py:324
  97.1 1.7 %copy-start.10 = (bf16[320,2048]{1,0:T(8,128)(2,1)S(1)}, bf16[320,2048]{1,0:T(8,128)(2,1)}, u32[]{:S(2)}) copy-start(bf16[320,2048]{1,0:T(8,128)(2,1)} %copy-done.9) | copy-start | bytes 3932164
  98.7 3.1 %collective-permute-start.15 = (bf16[320,2048]{1,0:T(8,128)(2,1)S(1)}, bf16[320,2048]{1,0:T(8,128)(2,1)S(1)}, u32[]{:S(2)}, u32[]{:S(2)}) collective-permute-start(bf16[320,2048]{1,0:T(8,128)(2,1)S(1)} %broadcast_select_fusion.2.refs_0_), channel_id=1, source_target_pairs={{0,1},{1,0},{2,3},{3,2},{4,5},{5,4},{6,7},{7,6},{8,9},{9,8},{10,11... | collective-permute-start | bytes 3932168 | tf_op jit(solution)/shard_map/ppermute | solution.py:327
  99.8 19.0 %collective-permute-start.16 = (bf16[320,2048]{1,0:T(8,128)(2,1)S(1)}, bf16[320,2048]{1,0:T(8,128)(2,1)}, u32[]{:S(2)}, u32[]{:S(2)}) collective-permute-start(bf16[320,2048]{1,0:T(8,128)(2,1)S(1)} %broadcast_select_fusion), channel_id=1, source_target_pairs={{1,16},{2,19},{5,20},{6,23},{17,0},{18,3},{21,4},{22,7},{9,24},{10... | collective-permute-start | bytes 3932168 | tf_op jit(solution)/shard_map/ppermute | solution.py:377
  120.3 3.2 %copy-start.5 = (bf16[320,2048]{1,0:T(8,128)(2,1)}, bf16[320,2048]{1,0:T(8,128)(2,1)S(1)}, u32[]{:S(2)}) copy-start(bf16[320,2048]{1,0:T(8,128)(2,1)S(1)} %broadcast_select_fusion.1.refs_0_) | copy-start | bytes 3932164
  120.3 3.2 %collective-permute-start.17 = (bf16[320,2048]{1,0:T(8,128)(2,1)S(1)}, bf16[320,2048]{1,0:T(8,128)(2,1)}, u32[]{:S(2)}, u32[]{:S(2)}) collective-permute-start(bf16[320,2048]{1,0:T(8,128)(2,1)S(1)} %broadcast_select_fusion.1.refs_0_), channel_id=1, source_target_pairs={{0,1},{1,0},{2,3},{3,2},{4,5},{5,4},{6,7},{7,6},{8,9},{9,8},{10,11... | collective-permute-start | bytes 3932168 | tf_op jit(solution)/shard_map/ppermute | solution.py:327
  120.4 18.7 %collective-permute-start.19 = (bf16[320,2048]{1,0:T(8,128)(2,1)}, bf16[320,2048]{1,0:T(8,128)(2,1)S(1)}, u32[]{:S(2)}, u32[]{:S(2)}) collective-permute-start(bf16[320,2048]{1,0:T(8,128)(2,1)} %shard_map.117), channel_id=1, source_target_pairs={{0,2},{2,4},{4,6},{3,1},{5,3},{7,5},{8,10},{10,12},{12,14},{11,9},... | collective-permute-start | bytes 3932168 | tf_op jit(solution)/shard_map/ppermute | solution.py:324
  122.2 16.9 %collective-permute-start.18 = (bf16[320,1024]{1,0:T(8,128)(2,1)}, bf16[320,1024]{1,0:T(8,128)(2,1)S(1)}, u32[]{:S(2)}, u32[]{:S(2)}) collective-permute-start(bf16[320,1024]{1,0:T(8,128)(2,1)} %get-tuple-element.158), channel_id=1, source_target_pairs={{8,0},{9,1},{10,2},{11,3},{12,4},{13,5},{14,6},{15,7},{0,8},{1,9},... | collective-permute-start | bytes 1966088 | tf_op jit(solution)/shard_map/ppermute | solution.py:462
  131.7 12.0 %copy-start.12 = (f32[320,1024]{1,0:T(8,128)S(1)}, f32[320,1024]{1,0:T(8,128)}, u32[]{:S(2)}) copy-start(f32[320,1024]{1,0:T(8,128)} %get-tuple-element.157) | copy-start | bytes 3932164
  133.3 1.2 collective-permute-start.20
  134.5 5.4 %collective-permute-start.21 = (f32[2,4608]{1,0:T(2,128)S(1)}, f32[2,4608]{1,0:T(2,128)S(1)}, u32[]{:S(2)}, u32[]{:S(2)}) collective-permute-start(f32[2,4608]{1,0:T(2,128)S(1)} %add.135), channel_id=1, source_target_pairs={{2,0},{3,1},{4,2},{5,3},{6,4},{7,5},{0,6},{1,7},{10,8},{11,9},{12,... | collective-permute-start | bytes 110600 | tf_op jit(solution)/shard_map/ppermute | solution.py:547
  134.6 7.3 %collective-permute-start.23 = (f32[2,4608]{1,0:T(2,128)S(1)}, f32[2,4608]{1,0:T(2,128)S(1)}, u32[]{:S(2)}, u32[]{:S(2)}) collective-permute-start(f32[2,4608]{1,0:T(2,128)S(1)} %add.135), channel_id=1, source_target_pairs={{6,0},{7,1},{0,2},{1,3},{2,4},{3,5},{4,6},{5,7},{14,8},{15,9},{8,1... | collective-permute-start | bytes 110600 | tf_op jit(solution)/shard_map/ppermute | solution.py:547
  136.6 5.4 %collective-permute-start.24 = (f32[2,4608]{1,0:T(2,128)S(1)}, f32[2,4608]{1,0:T(2,128)S(1)}, u32[]{:S(2)}, u32[]{:S(2)}) collective-permute-start(f32[2,4608]{1,0:T(2,128)S(1)} %add.135), channel_id=1, source_target_pairs={{4,0},{5,1},{6,2},{7,3},{0,4},{1,5},{2,6},{3,7},{12,8},{13,9},{14,... | collective-permute-start | bytes 110600 | tf_op jit(solution)/shard_map/ppermute | solution.py:547
  139.9 3.7 %copy-start.14 = (bf16[320,1024]{1,0:T(8,128)(2,1)S(1)}, bf16[320,1024]{1,0:T(8,128)(2,1)}, u32[]{:S(2)}) copy-start(bf16[320,1024]{1,0:T(8,128)(2,1)} %copy-done.13) | copy-start | bytes 1966084
  140.0 3.7 %collective-permute-start.22 = (bf16[320,1024]{1,0:T(8,128)(2,1)S(1)}, bf16[320,1024]{1,0:T(8,128)(2,1)S(1)}, u32[]{:S(2)}, u32[]{:S(2)}) collective-permute-start(bf16[320,1024]{1,0:T(8,128)(2,1)S(1)} %broadcast_select_fusion.4), channel_id=1, source_target_pairs={{0,1},{1,0},{2,3},{3,2},{4,5},{5,4},{6,7},{7,6},{8,9},{9,8},{10,11... | collective-permute-start | bytes 1966088 | tf_op jit(solution)/shard_map/ppermute | solution.py:564
  (8 other events, 8.3 us)

commit v7 on v5

--- a/solution.py
+++ b/solution.py
@@ -101,7 +101,7 @@
     shard = part // (lo // 2)
     width = rights[0][0].shape[1] // members
     single = len({row for row, _, _ in items}) == 1
-    tile = max(width // (2 if single else 4), 128)
+    tile = max(width // 2, 128)
     tiles = width // tile
     if single:
         row = items[0][0]

time: 144 us -> 144 us (level)
  no operation moved by 1% of the time
where the time goes in v7:
time: 144 us; the launch traced here: 143 us
  Pallas kernels  65 us (45%)
  starting transfers between devices  45 us (31%)
  waiting for transfers between devices  14 us (10%)
  local copies, waits for them, and re-layouts  11.9 us (8%)
  other arithmetic  6.43 us (4%)
    pallas_call x3, Pallas kernels, weight_slots(): pl.pallas_call(functools.partial(slot_kernel, n, lo, kept is not None, ba...  29 us
    pallas_call x2, Pallas kernels, partials(): pl.pallas_call(functools.partial(partials_kernel, lo, items, len(column_a...  17 us
    ppermute x4, starting transfers between devices, line_step(): return lax.ppermute(x, 'fsdp', pairs)  15.9 us
    pallas_call x3, Pallas kernels, hop(): pl.pallas_call(functools.partial(hop_kernel, len(got), bool(other), len(c...  12.2 us
    ppermute x4, starting transfers between devices, exchange(): got[k].append(lax.ppermute(blocks[j - 1], ('member', 'fsdp'), pairs))  10.8 us
    unnamed x31, local copies, waits for them, and re-layouts  7.89 us
    pallas_call x1, Pallas kernels, prepare(): pl.pallas_call(functools.partial(prepare_kernel, nh), out_shape=[turned,...  6.85 us
    ppermute x1, starting transfers between devices, weight_first(): arrived[1] = lax.ppermute(weight, ('groups', 'fsdp'), pairs)  6.03 us
  transfers between devices with their start and end apart: 25, of which 9 were waited for; matrix products, arithmetic and copies ran while one was open for 6% of the time, Pallas kernels for 45%

profile of v7, /device:TPU:0, one launch (start us, length us, event | category | flops | bytes accessed | tf_op | source)
XLA Modules:
  0.0 143.3 jit_solution(14230148119356375575)
XLA Ops:
  0.6 6.0 %collective-permute-start = (bf16[320,2048]{1,0:T(8,128)(2,1)}, bf16[320,2048]{1,0:T(8,128)(2,1)}, u32[]{:S(2)}, u32[]{:S(2)}) collective-permute-start(bf16[320,2048]{1,0:T(8,128)(2,1)} %refs_0_), channel_id=1, source_target_pairs={{0,2},{2,4},{3,1},{4,6},{5,3},{7,5},{17,18},{19,20},{18,17},{21,22... | collective-permute-start | bytes 3932168 | tf_op jit(solution)/shard_map/ppermute | solution.py:345
  6.7 1.5 %broadcast_in_dim.4.slot_ref.refs_10_.refs_8_ = s32[384,1]{1,0:T(8,128)} reshape(s32[384]{0:T(512)} %param.13) | data formatting | bytes 3072 | tf_op jit(solution)/shard_map/broadcast_in_dim | solution.py:311
  8.1 6.8 %shard_map.110 = (bf16[4,320,384]{2,1,0:T(8,128)(2,1)}, bf16[4,320,384]{2,1,0:T(8,128)(2,1)}, bf16[192,2048]{1,0:T(8,128)(2,1)}, bf16[192,2048]{1,0:T(8,128)(2,1)}) custom-call(bf16[384,2560]{1,0:T(8,128)(2,1)} %refs_5_.3, bf16[384,2560]{1,0:T(8,128)(2,1)} %refs_6_.5, f32[2,2560]{1,0:T(2,128)} %refs_7_.5, bf16[384,2048]{1,0:T(8,128)(2,1)} %refs_4_.3, ...), custom_call_target="tpu_custom_call" | custom-call | flops 1 | bytes 1 | tf_op jit(solution)/shard_map/pallas_call | solution.py:55
  16.7 4.3 %collective-permute-done = bf16[320,2048]{1,0:T(8,128)(2,1)} collective-permute-done((bf16[320,2048]{1,0:T(8,128)(2,1)}, bf16[320,2048]{1,0:T(8,128)(2,1)}, u32[]{:S(2)}, u32[]{:S(2)}) %collective-permute-start) | collective-permute-done | bytes 1310752 | tf_op jit(solution)/shard_map/ppermute | solution.py:345
  21.0 1.3 collective-permute-start.2
  24.5 4.6 %shard_map.112 = bf16[640,1024]{1,0:T(8,128)(2,1)} custom-call(s32[28]{0:T(128)} %stack.121.ids_ref, bf16[4,320,384]{2,1,0:T(8,128)(2,1)} %get-tuple-element.88.refs_0_.refs_4_, bf16[4,320,384]{2,1,0:T(8,128)(2,1)} %get-tuple-element.89.refs_1_.refs_5_, bf16[4,320,384]{2,1,0:T(8,128)(2,1)} %copy-done, bf16[4,320,384]{2,1,0:T(8,128)(2,1)} %copy-done.1, ...), custom_call_target="tpu_custom_call" | custom-call | flops 1 | bytes 1 | tf_op jit(solution)/shard_map/pallas_call | solution.py:129
  29.1 3.4 %collective-permute-start.7 = (bf16[640,1024]{1,0:T(8,128)(2,1)}, bf16[640,1024]{1,0:T(8,128)(2,1)}, u32[]{:S(2)}, u32[]{:S(2)}) collective-permute-start(bf16[640,1024]{1,0:T(8,128)(2,1)} %shard_map.112), channel_id=1, source_target_pairs={{8,0},{11,3},{12,4},{15,7},{0,8},{3,11},{4,12},{7,15},{24,16},{27,... | collective-permute-start | bytes 3932168 | tf_op jit(solution)/shard_map/ppermute | solution.py:462
  33.2 12.4 %shard_map.111 = (bf16[640,1024]{1,0:T(8,128)(2,1)}, bf16[640,1024]{1,0:T(8,128)(2,1)}, bf16[320,1024]{1,0:T(8,128)(2,1)}, bf16[640,1024]{1,0:T(8,128)(2,1)}, bf...) custom-call(s32[28]{0:T(128)} %stack.121.ids_ref, ...), custom_call_target="tpu_custom_call" | custom-call | flops 1 | bytes 1 | tf_op jit(solution)/shard_map/pallas_call | solution.py:129
  45.7 1.5 %broadcast_select_fusion.3.refs_2_ = bf16[320,2048]{1,0:T(8,128)(2,1)S(1)} fusion(bf16[320,2048]{1,0:T(8,128)(2,1)} %collective-permute-done, bf16[320,2048]{1,0:T(8,128)(2,1)} %collective-permute-done.2, pred[]{:T(512)S(6)} %eq.109), kind=kLoop, calls=%fused_computation.4 | loop fusion | flops 655360 | bytes 3932161 | tf_op jit(solution)/shard_map/jit(_where)/select_n | solution.py:380
  47.2 2.5 %collective-permute-start.11 = (bf16[320,2048]{1,0:T(8,128)(2,1)S(1)}, bf16[320,2048]{1,0:T(8,128)(2,1)}, u32[]{:S(2)}, u32[]{:S(2)}) collective-permute-start(bf16[320,2048]{1,0:T(8,128)(2,1)S(1)} %broadcast_select_fusion.3.refs_2_), channel_id=1, source_target_pairs={{0,1},{1,0},{2,3},{3,2},{4,5},{5,4},{6,7},{7,6},{8,9},{9,8},{10,11... | collective-permute-start | bytes 3932168 | tf_op jit(solution)/shard_map/ppermute | solution.py:327
  50.7 3.9 %shard_map.113 = bf16[320,2048]{1,0:T(8,128)(2,1)} custom-call(s32[28]{0:T(128)} %stack.121.ids_ref, bf16[640,1024]{1,0:T(8,128)(2,1)} %get-tuple-element.99.sum_ref, bf16[640,1024]{1,0:T(8,128)(2,1)} %collective-permute-done.7.refs_0_.refs_1_, bf16[320,2048]{1,0:T(8,128)(2,1)} %copy-done.7), custom_call_target="tpu_custom_call" | custom-call | flops 1 | bytes 1 | tf_op jit(solution)/shard_map/pallas_call | solution.py:164
  54.6 3.5 %collective-permute-start.9 = (bf16[640,1024]{1,0:T(8,128)(2,1)}, bf16[640,1024]{1,0:T(8,128)(2,1)}, u32[]{:S(2)}, u32[]{:S(2)}) collective-permute-start(bf16[640,1024]{1,0:T(8,128)(2,1)} %get-tuple-element.107), channel_id=1, source_target_pairs={{8,0},{10,2},{13,5},{15,7},{0,8},{2,10},{5,13},{7,15},{24,16},{26,... | collective-permute-start | bytes 3932168 | tf_op jit(solution)/shard_map/ppermute | solution.py:462
  58.0 7.9 %collective-permute-start.10 = (bf16[320,2048]{1,0:T(8,128)(2,1)}, bf16[320,2048]{1,0:T(8,128)(2,1)S(1)}, u32[]{:S(2)}, u32[]{:S(2)}) collective-permute-start(bf16[320,2048]{1,0:T(8,128)(2,1)} %shard_map.113), channel_id=1, source_target_pairs={{0,2},{4,6},{7,5},{3,1},{8,10},{12,14},{15,13},{11,9},{16,18},{20,... | collective-permute-start | bytes 3932168 | tf_op jit(solution)/shard_map/ppermute | solution.py:324
  65.9 1.3 collective-permute-start.14
  67.3 12.7 %shard_map.114 = (bf16[384,2560]{1,0:T(8,128)(2,1)}, bf16[384,2560]{1,0:T(8,128)(2,1)}, f32[2,2560]{1,0:T(2,128)}, f32[2,2048]{1,0:T(2,128)}) custom-call(s32[28]{0:T(128)} %stack.121.ids_ref, bf16[320,2048]{1,0:T(8,128)(2,1)} %refs_0_, bf16[320,2048]{1,0:T(8,128)(2,1)} %collective-permute-done.1.refs_1_, bf16[320,2048]{1,0:T(8,128)(2,1)} %copy-done.4, ...), custom_call_target="tpu_custom_call" | custom-call | flops 1 | bytes 1 | tf_op jit(solution)/shard_map/pallas_call | solution.py:273
  80.0 1.3 collective-permute-done.10.refs_1_
  82.3 4.0 %shard_map.115 = bf16[320,2048]{1,0:T(8,128)(2,1)} custom-call(s32[28]{0:T(128)} %stack.121.ids_ref, bf16[640,1024]{1,0:T(8,128)(2,1)} %get-tuple-element.105.sum_ref, bf16[640,1024]{1,0:T(8,128)(2,1)} %collective-permute-done.9.refs_0_, bf16[320,2048]{1,0:T(8,128)(2,1)} %copy-done.9), custom_call_target="tpu_custom_call" | custom-call | flops 1 | bytes 1 | tf_op jit(solution)/shard_map/pallas_call | solution.py:164
  86.3 3.4 %collective-permute-start.12 = (bf16[640,1024]{1,0:T(8,128)(2,1)}, bf16[640,1024]{1,0:T(8,128)(2,1)}, u32[]{:S(2)}, u32[]{:S(2)}) collective-permute-start(bf16[640,1024]{1,0:T(8,128)(2,1)} %get-tuple-element.123), channel_id=1, source_target_pairs={{8,0},{10,2},{13,5},{15,7},{0,8},{2,10},{5,13},{7,15},{24,16},{26,... | collective-permute-start | bytes 3932168 | tf_op jit(solution)/shard_map/ppermute | solution.py:462
  89.7 5.4 %collective-permute-start.13 = (bf16[320,2048]{1,0:T(8,128)(2,1)}, bf16[320,2048]{1,0:T(8,128)(2,1)}, u32[]{:S(2)}, u32[]{:S(2)}) collective-permute-start(bf16[320,2048]{1,0:T(8,128)(2,1)} %shard_map.115), channel_id=1, source_target_pairs={{0,2},{2,4},{5,3},{7,5},{8,10},{10,12},{13,11},{15,13},{16,18},{18... | collective-permute-start | bytes 3932168 | tf_op jit(solution)/shard_map/ppermute | solution.py:324
  95.2 1.6 %broadcast_select_fusion.2.refs_0_ = bf16[320,2048]{1,0:T(8,128)(2,1)S(1)} fusion(bf16[320,2048]{1,0:T(8,128)(2,1)S(1)} %copy-done.8, bf16[320,2048]{1,0:T(8,128)(2,1)} %collective-permute-done.14, pred[]{:T(512)S(6)} %eq.110), kind=kLoop, calls=%fused_computation.3 | loop fusion | flops 655360 | bytes 3932161 | tf_op jit(solution)/shard_map/jit(_where)/select_n | solution.py:380
  97.9 1.5 %collective-permute-start.16 = (bf16[320,2048]{1,0:T(8,128)(2,1)S(1)}, bf16[320,2048]{1,0:T(8,128)(2,1)}, u32[]{:S(2)}, u32[]{:S(2)}) collective-permute-start(bf16[320,2048]{1,0:T(8,128)(2,1)S(1)} %broadcast_select_fusion), channel_id=1, source_target_pairs={{1,16},{2,19},{5,20},{6,23},{17,0},{18,3},{21,4},{22,7},{9,24},{10... | collective-permute-start | bytes 3932168 | tf_op jit(solution)/shard_map/ppermute | solution.py:377
  100.9 8.1 %shard_map.116 = (bf16[384,2560]{1,0:T(8,128)(2,1)}, bf16[384,2560]{1,0:T(8,128)(2,1)}, f32[2,2560]{1,0:T(2,128)}, f32[2,2048]{1,0:T(2,128)}) custom-call(s32[28]{0:T(128)} %stack.121.ids_ref, bf16[320,2048]{1,0:T(8,128)(2,1)} %copy-done.6, bf16[320,2048]{1,0:T(8,128)(2,1)} %copy-done.11, ...), custom_call_target="tpu_custom_call", output_to_operand_aliasing={{0}: (10, {}), {1}: (11, {}), {2}: (12, {})} | custom-call | flops 1 | bytes 1 | tf_op jit(solution)/shard_map/pallas_call | solution.py:273
  109.4 4.3 %shard_map.117 = bf16[320,2048]{1,0:T(8,128)(2,1)} custom-call(s32[28]{0:T(128)} %stack.121.ids_ref, bf16[640,1024]{1,0:T(8,128)(2,1)} %get-tuple-element.121.sum_ref, bf16[640,1024]{1,0:T(8,128)(2,1)} %collective-permute-done.12.refs_0_, bf16[640,1024]{1,0:T(8,128)(2,1)} %collective-permute-done.7.refs_0_.refs_1_, ...), custom_call_target="tpu_custom_call" | custom-call | flops 1 | bytes 1 | tf_op jit(solution)/shard_map/pallas_call | solution.py:164
  113.7 3.2 %collective-permute-done.16 = bf16[320,2048]{1,0:T(8,128)(2,1)} collective-permute-done((bf16[320,2048]{1,0:T(8,128)(2,1)S(1)}, bf16[320,2048]{1,0:T(8,128)(2,1)}, u32[]{:S(2)}, u32[]{:S(2)}) %collective-permute-start.16) | collective-permute-done | bytes 1310752 | tf_op jit(solution)/shard_map/ppermute | solution.py:377
  116.9 1.5 %broadcast_select_fusion.1.refs_0_ = bf16[320,2048]{1,0:T(8,128)(2,1)S(1)} fusion(bf16[320,2048]{1,0:T(8,128)(2,1)S(1)} %broadcast_select_fusion, bf16[320,2048]{1,0:T(8,128)(2,1)} %collective-permute-done.16, pred[]{:T(512)S(6)} %eq.111), kind=kLoop, calls=%fused_computation.2 | loop fusion | flops 655360 | bytes 3932161 | tf_op jit(solution)/shard_map/jit(_where)/select_n | solution.py:380
  118.4 1.8 %collective-permute-start.19 = (bf16[320,2048]{1,0:T(8,128)(2,1)}, bf16[320,2048]{1,0:T(8,128)(2,1)S(1)}, u32[]{:S(2)}, u32[]{:S(2)}) collective-permute-start(bf16[320,2048]{1,0:T(8,128)(2,1)} %shard_map.117), channel_id=1, source_target_pairs={{0,2},{2,4},{4,6},{3,1},{5,3},{7,5},{8,10},{10,12},{12,14},{11,9},... | collective-permute-start | bytes 3932168 | tf_op jit(solution)/shard_map/ppermute | solution.py:324
  121.6 8.1 %shard_map.118 = (bf16[384,2560]{1,0:T(8,128)(2,1)}, bf16[384,2560]{1,0:T(8,128)(2,1)}, f32[2,2560]{1,0:T(2,128)}, f32[2,2048]{1,0:T(2,128)}) custom-call(s32[28]{0:T(128)} %stack.121.ids_ref, bf16[320,2048]{1,0:T(8,128)(2,1)} %copy-done.5, ...), custom_call_target="tpu_custom_call", output_to_operand_aliasing={{0}: (10, {}), {1}: (11, {}), {2}: (12, {})} | custom-call | flops 1 | bytes 1 | tf_op jit(solution)/shard_map/pallas_call | solution.py:273
  131.5 1.1 collective-permute-done.20
  132.7 2.0 %collective-permute-start.23 = (f32[2,4608]{1,0:T(2,128)S(1)}, f32[2,4608]{1,0:T(2,128)S(1)}, u32[]{:S(2)}, u32[]{:S(2)}) collective-permute-start(f32[2,4608]{1,0:T(2,128)S(1)} %add.135), channel_id=1, source_target_pairs={{6,0},{7,1},{0,2},{1,3},{2,4},{3,5},{4,6},{5,7},{14,8},{15,9},{8,1... | collective-permute-start | bytes 110600 | tf_op jit(solution)/shard_map/ppermute | solution.py:547
  135.0 2.1 %collective-permute-done.18 = bf16[320,1024]{1,0:T(8,128)(2,1)S(1)} collective-permute-done((bf16[320,1024]{1,0:T(8,128)(2,1)}, bf16[320,1024]{1,0:T(8,128)(2,1)S(1)}, u32[]{:S(2)}, u32[]{:S(2)}) %collective-permute-start.18) | collective-permute-done | bytes 655392 | tf_op jit(solution)/shard_map/ppermute | solution.py:462
  138.1 1.9 %collective-permute-start.22 = (bf16[320,1024]{1,0:T(8,128)(2,1)S(1)}, bf16[320,1024]{1,0:T(8,128)(2,1)S(1)}, u32[]{:S(2)}, u32[]{:S(2)}) collective-permute-start(bf16[320,1024]{1,0:T(8,128)(2,1)S(1)} %broadcast_select_fusion.4), channel_id=1, source_target_pairs={{0,1},{1,0},{2,3},{3,2},{4,5},{5,4},{6,7},{7,6},{8,9},{9,8},{10,11... | collective-permute-start | bytes 1966088 | tf_op jit(solution)/shard_map/ppermute | solution.py:564
  141.7 1.6 %convert_add_fusion = f32[320,1024]{1,0:T(8,128)} fusion(bf16[320,1024]{1,0:T(8,128)(2,1)S(1)} %collective-permute-done.22, f32[320,1024]{1,0:T(8,128)S(1)} %copy-done.12, bf16[320,1024]{1,0:T(8,128)(2,1)S(1)} %copy-done.14, pred[]{:T(512)S(6)} %lt.30, bf16[320,2048]{1,0:T(8,128)(2,1)S(1)} %collective-permute-done.19), kind=kLoop, calls=%fused_computation | loop fusion | flops 2293760 | bytes 5242881 | tf_op jit(solution)/shard_map/add | solution.py:570
  (71 shorter events, 16.0 us)
Async XLA Ops:
  0.6 20.4 %collective-permute-start = (bf16[320,2048]{1,0:T(8,128)(2,1)}, bf16[320,2048]{1,0:T(8,128)(2,1)}, u32[]{:S(2)}, u32[]{:S(2)}) collective-permute-start(bf16[320,2048]{1,0:T(8,128)(2,1)} %refs_0_), channel_id=1, source_target_pairs={{0,2},{2,4},{3,1},{4,6},{5,3},{7,5},{17,18},{19,20},{18,17},{21,22... | collective-permute-start | bytes 3932168 | tf_op jit(solution)/shard_map/ppermute | solution.py:345
  15.0 6.0 %collective-permute-start.5 = (bf16[192,2048]{1,0:T(8,128)(2,1)}, bf16[192,2048]{1,0:T(8,128)(2,1)S(1)}, u32[]{:S(2)}, u32[]{:S(2)}) collective-permute-start(bf16[192,2048]{1,0:T(8,128)(2,1)} %get-tuple-element.90.refs_8_.refs_12_.refs_4_.refs_2_), channel_id=1, source_target_pairs={{0,1},{1,0},{2,3},{3,2},{4,5},{5,4},{6,7},{7,6},{8,9},{9,8},{10,11... | collective-permute-start | bytes 2359304 | tf_op jit(solution)/shard_map/ppermute | solution.py:327
  15.0 7.3 %collective-permute-start.3 = (bf16[4,320,384]{2,1,0:T(8,128)(2,1)}, bf16[4,320,384]{2,1,0:T(8,128)(2,1)S(1)}, u32[]{:S(2)}, u32[]{:S(2)}) collective-permute-start(bf16[4,320,384]{2,1,0:T(8,128)(2,1)} %get-tuple-element.88.refs_0_.refs_4_), channel_id=1, source_target_pairs={{0,1},{1,0},{2,3},{3,2},{4,5},{5,4},{6,7},{7,6},{8,9},{9,8},{10,11... | collective-permute-start | bytes 2949128 | tf_op jit(solution)/shard_map/ppermute | solution.py:327
  15.5 6.8 %collective-permute-start.4 = (bf16[4,320,384]{2,1,0:T(8,128)(2,1)}, bf16[4,320,384]{2,1,0:T(8,128)(2,1)S(1)}, u32[]{:S(2)}, u32[]{:S(2)}) collective-permute-start(bf16[4,320,384]{2,1,0:T(8,128)(2,1)} %get-tuple-element.89.refs_1_.refs_5_), channel_id=1, source_target_pairs={{0,1},{1,0},{2,3},{3,2},{4,5},{5,4},{6,7},{7,6},{8,9},{9,8},{10,11... | collective-permute-start | bytes 2949128 | tf_op jit(solution)/shard_map/ppermute | solution.py:327
  15.6 6.7 %collective-permute-start.6 = (bf16[192,2048]{1,0:T(8,128)(2,1)}, bf16[192,2048]{1,0:T(8,128)(2,1)S(1)}, u32[]{:S(2)}, u32[]{:S(2)}) collective-permute-start(bf16[192,2048]{1,0:T(8,128)(2,1)} %get-tuple-element.91.refs_9_.refs_13_.refs_5_.refs_3_), channel_id=1, source_target_pairs={{0,1},{1,0},{2,3},{3,2},{4,5},{5,4},{6,7},{7,6},{8,9},{9,8},{10,11... | collective-permute-start | bytes 2359304 | tf_op jit(solution)/shard_map/ppermute | solution.py:327
  21.0 12.2 %collective-permute-start.1 = (bf16[320,2048]{1,0:T(8,128)(2,1)}, bf16[320,2048]{1,0:T(8,128)(2,1)}, u32[]{:S(2)}, u32[]{:S(2)}) collective-permute-start(bf16[320,2048]{1,0:T(8,128)(2,1)} %refs_0_), channel_id=1, source_target_pairs={{0,1},{1,0},{2,3},{3,2},{4,5},{5,4},{6,7},{7,6},{8,9},{9,8},{10,11... | collective-permute-start | bytes 3932168 | tf_op jit(solution)/shard_map/ppermute | solution.py:327
  21.0 1.4 copy-start.2
  21.0 24.7 %collective-permute-start.2 = (bf16[320,2048]{1,0:T(8,128)(2,1)}, bf16[320,2048]{1,0:T(8,128)(2,1)}, u32[]{:S(2)}, u32[]{:S(2)}) collective-permute-start(bf16[320,2048]{1,0:T(8,128)(2,1)} %collective-permute-done), channel_id=1, source_target_pairs={{1,16},{3,18},{4,21},{6,23},{17,0},{19,2},{20,5},{22,7},{9,24},{11... | collective-permute-start | bytes 3932168 | tf_op jit(solution)/shard_map/ppermute | solution.py:377
  29.1 20.6 %collective-permute-start.7 = (bf16[640,1024]{1,0:T(8,128)(2,1)}, bf16[640,1024]{1,0:T(8,128)(2,1)}, u32[]{:S(2)}, u32[]{:S(2)}) collective-permute-start(bf16[640,1024]{1,0:T(8,128)(2,1)} %shard_map.112), channel_id=1, source_target_pairs={{8,0},{11,3},{12,4},{15,7},{0,8},{3,11},{4,12},{7,15},{24,16},{27,... | collective-permute-start | bytes 3932168 | tf_op jit(solution)/shard_map/ppermute | solution.py:462
  32.5 17.2 %collective-permute-start.8 = (bf16[320,2048]{1,0:T(8,128)(2,1)}, bf16[320,2048]{1,0:T(8,128)(2,1)S(1)}, u32[]{:S(2)}, u32[]{:S(2)}) collective-permute-start(bf16[320,2048]{1,0:T(8,128)(2,1)} %collective-permute-done), channel_id=1, source_target_pairs={{2,4},{4,6},{3,1},{5,3},{10,12},{12,14},{11,9},{13,11},{18,20},{20... | collective-permute-start | bytes 3932168 | tf_op jit(solution)/shard_map/ppermute | solution.py:324
  47.1 7.4 %copy-start.4 = (bf16[320,2048]{1,0:T(8,128)(2,1)}, bf16[320,2048]{1,0:T(8,128)(2,1)S(1)}, u32[]{:S(2)}) copy-start(bf16[320,2048]{1,0:T(8,128)(2,1)S(1)} %broadcast_select_fusion.3.refs_2_) | copy-start | bytes 3932164
  47.2 20.1 %collective-permute-start.11 = (bf16[320,2048]{1,0:T(8,128)(2,1)S(1)}, bf16[320,2048]{1,0:T(8,128)(2,1)}, u32[]{:S(2)}, u32[]{:S(2)}) collective-permute-start(bf16[320,2048]{1,0:T(8,128)(2,1)S(1)} %broadcast_select_fusion.3.refs_2_), channel_id=1, source_target_pairs={{0,1},{1,0},{2,3},{3,2},{4,5},{5,4},{6,7},{7,6},{8,9},{9,8},{10,11... | collective-permute-start | bytes 3932168 | tf_op jit(solution)/shard_map/ppermute | solution.py:327
  54.6 25.4 %collective-permute-start.9 = (bf16[640,1024]{1,0:T(8,128)(2,1)}, bf16[640,1024]{1,0:T(8,128)(2,1)}, u32[]{:S(2)}, u32[]{:S(2)}) collective-permute-start(bf16[640,1024]{1,0:T(8,128)(2,1)} %get-tuple-element.107), channel_id=1, source_target_pairs={{8,0},{10,2},{13,5},{15,7},{0,8},{2,10},{5,13},{7,15},{24,16},{26,... | collective-permute-start | bytes 3932168 | tf_op jit(solution)/shard_map/ppermute | solution.py:462
  58.0 23.2 %collective-permute-start.10 = (bf16[320,2048]{1,0:T(8,128)(2,1)}, bf16[320,2048]{1,0:T(8,128)(2,1)S(1)}, u32[]{:S(2)}, u32[]{:S(2)}) collective-permute-start(bf16[320,2048]{1,0:T(8,128)(2,1)} %shard_map.113), channel_id=1, source_target_pairs={{0,2},{4,6},{7,5},{3,1},{8,10},{12,14},{15,13},{11,9},{16,18},{20,... | collective-permute-start | bytes 3932168 | tf_op jit(solution)/shard_map/ppermute | solution.py:324
  65.9 29.2 %collective-permute-start.14 = (bf16[320,2048]{1,0:T(8,128)(2,1)}, bf16[320,2048]{1,0:T(8,128)(2,1)}, u32[]{:S(2)}, u32[]{:S(2)}) collective-permute-start(bf16[320,2048]{1,0:T(8,128)(2,1)} %copy-done.7), channel_id=1, source_target_pairs={{1,16},{3,18},{4,21},{6,23},{17,0},{19,2},{20,5},{22,7},{9,24},{11... | collective-permute-start | bytes 3932168 | tf_op jit(solution)/shard_map/ppermute | solution.py:377
  82.3 12.8 %copy-start.8 = (bf16[320,2048]{1,0:T(8,128)(2,1)S(1)}, bf16[320,2048]{1,0:T(8,128)(2,1)}, u32[]{:S(2)}) copy-start(bf16[320,2048]{1,0:T(8,128)(2,1)} %copy-done.7) | copy-start | bytes 3932164
  86.3 22.7 %collective-permute-start.12 = (bf16[640,1024]{1,0:T(8,128)(2,1)}, bf16[640,1024]{1,0:T(8,128)(2,1)}, u32[]{:S(2)}, u32[]{:S(2)}) collective-permute-start(bf16[640,1024]{1,0:T(8,128)(2,1)} %get-tuple-element.123), channel_id=1, source_target_pairs={{8,0},{10,2},{13,5},{15,7},{0,8},{2,10},{5,13},{7,15},{24,16},{26,... | collective-permute-start | bytes 3932168 | tf_op jit(solution)/shard_map/ppermute | solution.py:462
  89.7 19.7 %collective-permute-start.13 = (bf16[320,2048]{1,0:T(8,128)(2,1)}, bf16[320,2048]{1,0:T(8,128)(2,1)}, u32[]{:S(2)}, u32[]{:S(2)}) collective-permute-start(bf16[320,2048]{1,0:T(8,128)(2,1)} %shard_map.115), channel_id=1, source_target_pairs={{0,2},{2,4},{5,3},{7,5},{8,10},{10,12},{13,11},{15,13},{16,18},{18... | collective-permute-start | bytes 3932168 | tf_op jit(solution)/shard_map/ppermute | solution.py:324
  95.2 1.7 %copy-start.10 = (bf16[320,2048]{1,0:T(8,128)(2,1)S(1)}, bf16[320,2048]{1,0:T(8,128)(2,1)}, u32[]{:S(2)}) copy-start(bf16[320,2048]{1,0:T(8,128)(2,1)} %copy-done.9) | copy-start | bytes 3932164
  96.7 3.1 %collective-permute-start.15 = (bf16[320,2048]{1,0:T(8,128)(2,1)S(1)}, bf16[320,2048]{1,0:T(8,128)(2,1)S(1)}, u32[]{:S(2)}, u32[]{:S(2)}) collective-permute-start(bf16[320,2048]{1,0:T(8,128)(2,1)S(1)} %broadcast_select_fusion.2.refs_0_), channel_id=1, source_target_pairs={{0,1},{1,0},{2,3},{3,2},{4,5},{5,4},{6,7},{7,6},{8,9},{9,8},{10,11... | collective-permute-start | bytes 3932168 | tf_op jit(solution)/shard_map/ppermute | solution.py:327
  97.9 19.0 %collective-permute-start.16 = (bf16[320,2048]{1,0:T(8,128)(2,1)S(1)}, bf16[320,2048]{1,0:T(8,128)(2,1)}, u32[]{:S(2)}, u32[]{:S(2)}) collective-permute-start(bf16[320,2048]{1,0:T(8,128)(2,1)S(1)} %broadcast_select_fusion), channel_id=1, source_target_pairs={{1,16},{2,19},{5,20},{6,23},{17,0},{18,3},{21,4},{22,7},{9,24},{10... | collective-permute-start | bytes 3932168 | tf_op jit(solution)/shard_map/ppermute | solution.py:377
  118.4 3.2 %copy-start.5 = (bf16[320,2048]{1,0:T(8,128)(2,1)}, bf16[320,2048]{1,0:T(8,128)(2,1)S(1)}, u32[]{:S(2)}) copy-start(bf16[320,2048]{1,0:T(8,128)(2,1)S(1)} %broadcast_select_fusion.1.refs_0_) | copy-start | bytes 3932164
  118.4 3.2 %collective-permute-start.17 = (bf16[320,2048]{1,0:T(8,128)(2,1)S(1)}, bf16[320,2048]{1,0:T(8,128)(2,1)}, u32[]{:S(2)}, u32[]{:S(2)}) collective-permute-start(bf16[320,2048]{1,0:T(8,128)(2,1)S(1)} %broadcast_select_fusion.1.refs_0_), channel_id=1, source_target_pairs={{0,1},{1,0},{2,3},{3,2},{4,5},{5,4},{6,7},{7,6},{8,9},{9,8},{10,11... | collective-permute-start | bytes 3932168 | tf_op jit(solution)/shard_map/ppermute | solution.py:327
  118.4 18.7 %collective-permute-start.19 = (bf16[320,2048]{1,0:T(8,128)(2,1)}, bf16[320,2048]{1,0:T(8,128)(2,1)S(1)}, u32[]{:S(2)}, u32[]{:S(2)}) collective-permute-start(bf16[320,2048]{1,0:T(8,128)(2,1)} %shard_map.117), channel_id=1, source_target_pairs={{0,2},{2,4},{4,6},{3,1},{5,3},{7,5},{8,10},{10,12},{12,14},{11,9},... | collective-permute-start | bytes 3932168 | tf_op jit(solution)/shard_map/ppermute | solution.py:324
  120.3 16.9 %collective-permute-start.18 = (bf16[320,1024]{1,0:T(8,128)(2,1)}, bf16[320,1024]{1,0:T(8,128)(2,1)S(1)}, u32[]{:S(2)}, u32[]{:S(2)}) collective-permute-start(bf16[320,1024]{1,0:T(8,128)(2,1)} %get-tuple-element.158), channel_id=1, source_target_pairs={{8,0},{9,1},{10,2},{11,3},{12,4},{13,5},{14,6},{15,7},{0,8},{1,9},... | collective-permute-start | bytes 1966088 | tf_op jit(solution)/shard_map/ppermute | solution.py:462
  129.7 12.0 %copy-start.12 = (f32[320,1024]{1,0:T(8,128)S(1)}, f32[320,1024]{1,0:T(8,128)}, u32[]{:S(2)}) copy-start(f32[320,1024]{1,0:T(8,128)} %get-tuple-element.157) | copy-start | bytes 3932164
  131.3 1.2 collective-permute-start.20
  132.6 5.4 %collective-permute-start.21 = (f32[2,4608]{1,0:T(2,128)S(1)}, f32[2,4608]{1,0:T(2,128)S(1)}, u32[]{:S(2)}, u32[]{:S(2)}) collective-permute-start(f32[2,4608]{1,0:T(2,128)S(1)} %add.135), channel_id=1, source_target_pairs={{2,0},{3,1},{4,2},{5,3},{6,4},{7,5},{0,6},{1,7},{10,8},{11,9},{12,... | collective-permute-start | bytes 110600 | tf_op jit(solution)/shard_map/ppermute | solution.py:547
  132.7 7.3 %collective-permute-start.23 = (f32[2,4608]{1,0:T(2,128)S(1)}, f32[2,4608]{1,0:T(2,128)S(1)}, u32[]{:S(2)}, u32[]{:S(2)}) collective-permute-start(f32[2,4608]{1,0:T(2,128)S(1)} %add.135), channel_id=1, source_target_pairs={{6,0},{7,1},{0,2},{1,3},{2,4},{3,5},{4,6},{5,7},{14,8},{15,9},{8,1... | collective-permute-start | bytes 110600 | tf_op jit(solution)/shard_map/ppermute | solution.py:547
  134.6 5.4 %collective-permute-start.24 = (f32[2,4608]{1,0:T(2,128)S(1)}, f32[2,4608]{1,0:T(2,128)S(1)}, u32[]{:S(2)}, u32[]{:S(2)}) collective-permute-start(f32[2,4608]{1,0:T(2,128)S(1)} %add.135), channel_id=1, source_target_pairs={{4,0},{5,1},{6,2},{7,3},{0,4},{1,5},{2,6},{3,7},{12,8},{13,9},{14,... | collective-permute-start | bytes 110600 | tf_op jit(solution)/shard_map/ppermute | solution.py:547
  138.0 3.7 %copy-start.14 = (bf16[320,1024]{1,0:T(8,128)(2,1)S(1)}, bf16[320,1024]{1,0:T(8,128)(2,1)}, u32[]{:S(2)}) copy-start(bf16[320,1024]{1,0:T(8,128)(2,1)} %copy-done.13) | copy-start | bytes 1966084
  138.1 3.7 %collective-permute-start.22 = (bf16[320,1024]{1,0:T(8,128)(2,1)S(1)}, bf16[320,1024]{1,0:T(8,128)(2,1)S(1)}, u32[]{:S(2)}, u32[]{:S(2)}) collective-permute-start(bf16[320,1024]{1,0:T(8,128)(2,1)S(1)} %broadcast_select_fusion.4), channel_id=1, source_target_pairs={{0,1},{1,0},{2,3},{3,2},{4,5},{5,4},{6,7},{7,6},{8,9},{9,8},{10,11... | collective-permute-start | bytes 1966088 | tf_op jit(solution)/shard_map/ppermute | solution.py:564
  (8 other events, 8.3 us)
